TPU v7x, 128 devices: a whole 4x4x4 slice. The times are simulated.
128 devices in a mesh: row: 16 (over y, z_hi, core), col: 8 (over z_lo, x).
Axes of the slice: x: 4, y: 4, z: 4 (z_hi: 2, z_lo: 2; z = z_hi * 2 + z_lo), core: 2. Of those that a mesh axis runs over, the one named last changes fastest.
Arguments:
- tokens: bfloat16 [32768, 1024], P(('row', 'col')), may hold values from -6 to 6
- grad_out: bfloat16 [32768, 1024], P(('row', 'col')), may hold values from -6 to 6
- target: int32 [32768], P(('row', 'col')), may hold values from 0 to 32767, as said below
- lengths: int32 [16, 8], P('row'), may hold values from 1 to 1024, 2048 in all within a row
- attn_gain: float32 [1024], replicated, may hold values from 0.1 to 1.9
- ffn_gain: float32 [1024], replicated, may hold values from 0.1 to 1.9
- q_gain: float32 [128], replicated, may hold values from 0.1 to 1.9
- k_gain: float32 [128], replicated, may hold values from 0.1 to 1.9
- w_query: bfloat16 [1024, 2048], P('row', 'col'), may hold values from -0.1875 to 0.1875
- key_matrix: bfloat16 [1024, 1024], P('row', 'col'), may hold values from -0.1875 to 0.1875
- value_matrix: bfloat16 [1024, 1024], P('row', 'col'), may hold values from -0.1875 to 0.1875
- w_out: bfloat16 [2048, 1024], P('col', 'row'), may hold values from -0.5 to 0.5
- w_gate: bfloat16 [1024, 3072], P('row', 'col'), may hold values from -0.1875 to 0.1875
- w_up: bfloat16 [1024, 3072], P('row', 'col'), may hold values from -0.1875 to 0.1875
- w_down: bfloat16 [3072, 1024], P('col', 'row'), may hold values from -0.109375 to 0.109375
Outputs:
- output: bfloat16 [32768, 1024], P(('row', 'col'))
- input_grad: bfloat16 [32768, 1024], P(('row', 'col'))
- grad_attn_gain: float32 [1024], replicated
- grad_ffn_gain: float32 [1024], replicated
- grad_q_gain: float32 [128], replicated
- grad_k_gain: float32 [128], replicated
- grad_w_query: float32 [1024, 2048], P('row', 'col')
- grad_w_key: float32 [1024, 1024], P('row', 'col')
- grad_w_value: float32 [1024, 1024], P('row', 'col')
- grad_w_out: float32 [2048, 1024], P('col', 'row')
- grad_w_gate: float32 [1024, 3072], P('row', 'col')
- grad_w_up: float32 [1024, 3072], P('row', 'col')
- grad_w_down: float32 [3072, 1024], P('col', 'row')
Inputs may be any that keep to these rules, and one draw needn't show every extreme that they name: target is a permutation of 0 to 32767. Arrival position a lies on device a // 256 of row+col and slot s on device s // 256; these two devices have the same col index, and every device sends exactly 16 of its tokens to each row group. `lengths`: each row sums to 2048, and its largest entry is 1024.
All inputs are finite; a program needn't handle non-finite values.
Results may differ from a plain program's by a relative error of at most 0.024.
Values may be sent and summed in bfloat16 or wider, within the bound.
A program may use at most 192 MiB of HBM per device.

v0:
```python
import jax
import jax.numpy as jnp
from jax import lax
from jax.sharding import PartitionSpec as P

QUERY_HEADS = 16
VALUE_HEADS = 8
HEAD_SIZE = 128


EPSILON = 1e-06
ROPE_BASE = 1000000.0


def rms_scale(values, weights):
    inverse = lax.rsqrt(jnp.mean(values * values, axis=-1, keepdims=True) + EPSILON)
    return values * inverse * weights


def rotate(values, position):
    head_width = values.shape[-1]
    halfway = head_width // 2
    inverse_freq = ROPE_BASE ** (-jnp.arange(halfway, dtype=jnp.float32) * 2.0 / head_width)
    shaped = (values.shape[0],) + (1,) * (values.ndim - 1)
    angles = position.astype(jnp.float32).reshape(shaped) * inverse_freq
    cosine = jnp.cos(angles)
    sine_part = jnp.sin(angles)
    leading = values[..., :halfway]
    trailing = values[..., halfway:]
    return jnp.concatenate(
        [leading * cosine - trailing * sine_part, trailing * cosine + leading * sine_part], axis=-1
    )


def head_prep(raw_heads, weights, position):
    return rotate(rms_scale(raw_heads, weights), position)


def sequence_layout(seq_lengths, total):
    ends_at = jnp.cumsum(seq_lengths)
    starts_at = ends_at - seq_lengths
    slot_ids = jnp.arange(total, dtype=jnp.int32)
    segment = jnp.sum((slot_ids[:, None] >= ends_at[None, :]).astype(jnp.int32), axis=1)
    member = segment[:, None] == jnp.arange(seq_lengths.shape[0], dtype=jnp.int32)[None, :]
    first_slot = jnp.sum(jnp.where(member, starts_at[None, :], 0), axis=1)
    return (segment, slot_ids - first_slot)


def block_probs(query_part, keys_rot, segment, block_start, block_stop):
    scale = query_part.shape[-1] ** (-0.5)
    raw_scores = jnp.einsum(
        "qcrd,kcd->crqk", query_part, keys_rot[:block_stop], preferred_element_type=jnp.float32
    )
    query_slots = jnp.arange(block_start, block_stop, dtype=jnp.int32)
    key_slots = jnp.arange(block_stop, dtype=jnp.int32)
    allowed = (segment[block_start:block_stop, None] == segment[None, :block_stop]) & (
        key_slots[None, :] <= query_slots[:, None]
    )
    return jax.nn.softmax(jnp.where(allowed[None, None], raw_scores * scale, -1e30), axis=-1)


def attend(queries, keys_rot, value_heads_rows, segment, block_rows):
    pieces = []
    for block_start in range(0, queries.shape[0], block_rows):
        block_stop = block_start + block_rows
        probs = block_probs(
            queries[block_start:block_stop], keys_rot, segment, block_start, block_stop
        )
        pieces.append(
            jnp.einsum(
                "crqk,kcd->qcrd",
                probs.astype(jnp.bfloat16),
                value_heads_rows[:block_stop],
                preferred_element_type=jnp.float32,
            )
        )
    return jnp.concatenate(pieces, axis=0)


def attend_back(queries, keys_rot, value_heads_rows, grad_attended, segment, block_rows):
    query_grads = []
    key_grads = jnp.zeros(keys_rot.shape, jnp.float32)
    value_grads = jnp.zeros(value_heads_rows.shape, jnp.float32)
    scale = queries.shape[-1] ** (-0.5)
    for block_start in range(0, queries.shape[0], block_rows):
        block_stop = block_start + block_rows
        query_part = queries[block_start:block_stop]
        grad_part = grad_attended[block_start:block_stop]
        probs = block_probs(query_part, keys_rot, segment, block_start, block_stop)
        grad_probs = jnp.einsum(
            "qcrd,kcd->crqk",
            grad_part,
            value_heads_rows[:block_stop],
            preferred_element_type=jnp.float32,
        )
        weighted = jnp.sum(probs * grad_probs, axis=-1, keepdims=True)
        grad_scores = (probs * (grad_probs - weighted) * scale).astype(jnp.bfloat16)
        query_grads.append(
            jnp.einsum(
                "crqk,kcd->qcrd",
                grad_scores,
                keys_rot[:block_stop],
                preferred_element_type=jnp.float32,
            )
        )
        key_grads = key_grads.at[:block_stop].add(
            jnp.einsum(
                "crqk,qcrd->kcd", grad_scores, query_part, preferred_element_type=jnp.float32
            )
        )
        value_grads = value_grads.at[:block_stop].add(
            jnp.einsum(
                "crqk,qcrd->kcd",
                probs.astype(jnp.bfloat16),
                grad_part,
                preferred_element_type=jnp.float32,
            )
        )
    return (jnp.concatenate(query_grads, axis=0), key_grads, value_grads)


def local(
    tokens,
    grad_out,
    target,
    lengths,
    attn_gain,
    ffn_gain,
    q_gain,
    k_gain,
    w_query,
    key_matrix,
    value_matrix,
    w_out,
    w_gate,
    w_up,
    w_down,
):
    row_count = tokens.shape[0]
    row_groups = lax.axis_size("row")
    group_size = row_count * lax.axis_size("col")
    per_group = row_count // row_groups
    block_rows = min(group_size, max(512, group_size // 8))
    target_group = target // group_size
    bucket = (target_group[:, None] == jnp.arange(row_groups, dtype=jnp.int32)[None, :]).astype(
        jnp.int32
    )
    bucket_rank = jnp.sum((jnp.cumsum(bucket, axis=0) - bucket) * bucket, axis=1)
    send_slot = target_group * per_group + bucket_rank
    sent_tokens = jnp.zeros_like(tokens).at[send_slot].set(tokens)
    sent_grads = jnp.zeros_like(grad_out).at[send_slot].set(grad_out)
    sent_slots = jnp.zeros_like(target).at[send_slot].set(target)
    got_tokens, got_grads, got_slots = (
        lax.all_to_all(sent_tokens, "row", split_axis=0, concat_axis=0, tiled=True),
        lax.all_to_all(sent_grads, "row", split_axis=0, concat_axis=0, tiled=True),
        lax.all_to_all(sent_slots, "row", split_axis=0, concat_axis=0, tiled=True),
    )
    local_slot = (got_slots % row_count).astype(jnp.int32)
    inputs = jnp.zeros_like(tokens).at[local_slot].set(got_tokens).astype(jnp.float32)
    grad_final = jnp.zeros_like(grad_out).at[local_slot].set(got_grads)
    segment, position = sequence_layout(lengths[0], group_size)
    full_query, complete_keys, complete_values, full_out, full_gate, full_up, full_down = (
        lax.all_gather(w_query, "row", axis=0, tiled=True),
        lax.all_gather(key_matrix, "row", axis=0, tiled=True),
        lax.all_gather(value_matrix, "row", axis=0, tiled=True),
        lax.all_gather(w_out, "row", axis=1, tiled=True),
        lax.all_gather(w_gate, "row", axis=0, tiled=True),
        lax.all_gather(w_up, "row", axis=0, tiled=True),
        lax.all_gather(w_down, "row", axis=1, tiled=True),
    )
    kv_count = complete_keys.shape[1] // HEAD_SIZE
    query_per_value_head = QUERY_HEADS // VALUE_HEADS

    def attention_all(normed_all):
        query_raw = jnp.dot(normed_all, full_query, preferred_element_type=jnp.float32).reshape(
            group_size, kv_count, query_per_value_head, HEAD_SIZE
        )
        unrotated_key = jnp.dot(
            normed_all, complete_keys, preferred_element_type=jnp.float32
        ).reshape(group_size, kv_count, HEAD_SIZE)
        value_heads_rows = (
            jnp.dot(normed_all, complete_values, preferred_element_type=jnp.float32)
            .astype(jnp.bfloat16)
            .reshape(group_size, kv_count, HEAD_SIZE)
        )
        queries = head_prep(query_raw, q_gain, position).astype(jnp.bfloat16)
        keys_rot = head_prep(unrotated_key, k_gain, position).astype(jnp.bfloat16)
        attended = (
            attend(queries, keys_rot, value_heads_rows, segment, block_rows)
            .reshape(group_size, -1)
            .astype(jnp.bfloat16)
        )
        return (query_raw, unrotated_key, queries, keys_rot, value_heads_rows, attended)

    def ffn_all(normed_all):
        gate_pre = jnp.dot(normed_all, full_gate, preferred_element_type=jnp.float32)
        up_pre = jnp.dot(normed_all, full_up, preferred_element_type=jnp.float32)
        hidden = (jax.nn.silu(gate_pre) * up_pre).astype(jnp.bfloat16)
        return (gate_pre, up_pre, hidden)

    first_normalized = rms_scale(inputs, attn_gain).astype(jnp.bfloat16)
    normed_first = lax.all_gather(first_normalized, "col", axis=0, tiled=True)
    query_raw, unrotated_key, queries, keys_rot, value_heads_rows, attended = attention_all(
        normed_first
    )
    middle = inputs + lax.psum_scatter(
        jnp.dot(attended, full_out, preferred_element_type=jnp.float32).astype(jnp.bfloat16),
        "col",
        scatter_dimension=0,
        tiled=True,
    ).astype(jnp.float32)
    normed_two = rms_scale(middle, ffn_gain).astype(jnp.bfloat16)
    normed_second = lax.all_gather(normed_two, "col", axis=0, tiled=True)
    gate_pre, up_pre, hidden = ffn_all(normed_second)
    result = (
        middle
        + lax.psum_scatter(
            jnp.dot(hidden, full_down, preferred_element_type=jnp.float32).astype(jnp.bfloat16),
            "col",
            scatter_dimension=0,
            tiled=True,
        ).astype(jnp.float32)
    ).astype(jnp.bfloat16)
    normed_first, normed_second = (
        lax.all_gather(first_normalized, "col", axis=0, tiled=True),
        lax.all_gather(normed_two, "col", axis=0, tiled=True),
    )
    query_raw, unrotated_key, queries, keys_rot, value_heads_rows, attended = attention_all(
        normed_first
    )
    gate_pre, up_pre, hidden = ffn_all(normed_second)
    grad_rows = lax.all_gather(grad_final, "col", axis=0, tiled=True)
    grad_down = jnp.einsum("tf,td->fd", hidden, grad_rows, preferred_element_type=jnp.float32)
    grad_hidden = jnp.einsum("td,fd->tf", grad_rows, full_down, preferred_element_type=jnp.float32)
    _, pull_gate = jax.vjp(lambda gate_in, up_in: jax.nn.silu(gate_in) * up_in, gate_pre, up_pre)
    grad_gate_pre, grad_up_pre = pull_gate(grad_hidden)
    grad_gate_pre = grad_gate_pre.astype(jnp.bfloat16)
    grad_up_pre = grad_up_pre.astype(jnp.bfloat16)
    grad_gate = jnp.einsum(
        "td,tf->df", normed_second, grad_gate_pre, preferred_element_type=jnp.float32
    )
    grad_up = jnp.einsum(
        "td,tf->df", normed_second, grad_up_pre, preferred_element_type=jnp.float32
    )
    grad_normed_two = lax.psum_scatter(
        (
            jnp.einsum("tf,df->td", grad_gate_pre, full_gate, preferred_element_type=jnp.float32)
            + jnp.einsum("tf,df->td", grad_up_pre, full_up, preferred_element_type=jnp.float32)
        ).astype(jnp.bfloat16),
        "col",
        scatter_dimension=0,
        tiled=True,
    ).astype(jnp.float32)
    _, pull_two = jax.vjp(rms_scale, middle, ffn_gain)
    grad_middle_norm, grad_ffn_gain = pull_two(grad_normed_two)
    grad_middle = grad_final.astype(jnp.float32) + grad_middle_norm
    grad_middle_rows = lax.all_gather(grad_middle.astype(jnp.bfloat16), "col", axis=0, tiled=True)
    grad_out_weight = jnp.einsum(
        "ta,td->ad", attended, grad_middle_rows, preferred_element_type=jnp.float32
    )
    grad_attended = (
        jnp.einsum("td,ad->ta", grad_middle_rows, full_out, preferred_element_type=jnp.float32)
        .astype(jnp.bfloat16)
        .reshape(queries.shape)
    )
    grad_queries, grad_keys, grad_values = attend_back(
        queries, keys_rot, value_heads_rows, grad_attended, segment, block_rows
    )
    _, pull_query = jax.vjp(
        lambda raw_in, gain_in: head_prep(raw_in, gain_in, position), query_raw, q_gain
    )
    grad_query_raw, grad_q_gain = pull_query(grad_queries)
    _, pull_key = jax.vjp(
        lambda raw_in, gain_in: head_prep(raw_in, gain_in, position), unrotated_key, k_gain
    )
    grad_key_raw, grad_k_gain = pull_key(grad_keys)
    query_back = grad_query_raw.reshape(group_size, -1).astype(jnp.bfloat16)
    key_back = grad_key_raw.reshape(group_size, -1).astype(jnp.bfloat16)
    value_back = grad_values.reshape(group_size, -1).astype(jnp.bfloat16)
    grad_query = jnp.einsum(
        "td,ta->da", normed_first, query_back, preferred_element_type=jnp.float32
    )
    grad_key = jnp.einsum("td,ta->da", normed_first, key_back, preferred_element_type=jnp.float32)
    grad_value = jnp.einsum(
        "td,ta->da", normed_first, value_back, preferred_element_type=jnp.float32
    )
    total_term = jnp.einsum("ta,da->td", query_back, full_query, preferred_element_type=jnp.float32)
    total_term = total_term + jnp.einsum(
        "ta,da->td", key_back, complete_keys, preferred_element_type=jnp.float32
    )
    grad_normed_one = lax.psum_scatter(
        (
            total_term
            + jnp.einsum(
                "ta,da->td", value_back, complete_values, preferred_element_type=jnp.float32
            )
        ).astype(jnp.bfloat16),
        "col",
        scatter_dimension=0,
        tiled=True,
    ).astype(jnp.float32)
    _, pull_one = jax.vjp(rms_scale, inputs, attn_gain)
    grad_input_norm, grad_attn_gain = pull_one(grad_normed_one)
    grad_inputs = (grad_middle + grad_input_norm).astype(jnp.bfloat16)
    grad_attn_gain, grad_ffn_gain, grad_q_gain, grad_k_gain = lax.psum(
        (grad_attn_gain, grad_ffn_gain, grad_q_gain, grad_k_gain), ("row", "col")
    )
    grad_query, grad_key, grad_value, grad_out_weight, grad_gate, grad_up, grad_down = (
        lax.psum_scatter(
            grad_query.astype(jnp.bfloat16), "row", scatter_dimension=0, tiled=True
        ).astype(jnp.float32),
        lax.psum_scatter(
            grad_key.astype(jnp.bfloat16), "row", scatter_dimension=0, tiled=True
        ).astype(jnp.float32),
        lax.psum_scatter(
            grad_value.astype(jnp.bfloat16), "row", scatter_dimension=0, tiled=True
        ).astype(jnp.float32),
        lax.psum_scatter(
            grad_out_weight.astype(jnp.bfloat16), "row", scatter_dimension=1, tiled=True
        ).astype(jnp.float32),
        lax.psum_scatter(
            grad_gate.astype(jnp.bfloat16), "row", scatter_dimension=0, tiled=True
        ).astype(jnp.float32),
        lax.psum_scatter(
            grad_up.astype(jnp.bfloat16), "row", scatter_dimension=0, tiled=True
        ).astype(jnp.float32),
        lax.psum_scatter(
            grad_down.astype(jnp.bfloat16), "row", scatter_dimension=1, tiled=True
        ).astype(jnp.float32),
    )
    back_result = result[local_slot]
    back_grads = grad_inputs[local_slot]
    got_result, got_input_grads = (
        lax.all_to_all(back_result, "row", split_axis=0, concat_axis=0, tiled=True),
        lax.all_to_all(back_grads, "row", split_axis=0, concat_axis=0, tiled=True),
    )
    output = got_result[send_slot]
    input_grad = got_input_grads[send_slot]
    return (
        output,
        input_grad,
        grad_attn_gain,
        grad_ffn_gain,
        grad_q_gain,
        grad_k_gain,
        grad_query,
        grad_key,
        grad_value,
        grad_out_weight,
        grad_gate,
        grad_up,
        grad_down,
    )


def solution(mesh):
    return jax.shard_map(
        local,
        mesh=mesh,
        in_specs=(
            P(("row", "col"), None),
            P(("row", "col"), None),
            P(("row", "col")),
            P("row", None),
            P(),
            P(),
            P(),
            P(),
            P("row", "col"),
            P("row", "col"),
            P("row", "col"),
            P("col", "row"),
            P("row", "col"),
            P("row", "col"),
            P("col", "row"),
        ),
        out_specs=(
            P(("row", "col"), None),
            P(("row", "col"), None),
            P(),
            P(),
            P(),
            P(),
            P("row", "col"),
            P("row", "col"),
            P("row", "col"),
            P("col", "row"),
            P("row", "col"),
            P("row", "col"),
            P("col", "row"),
        ),
        check_vma=False,
    )
```

profile of v0, /device:TPU:0, one launch (start us, length us, event | category | flops | bytes accessed | tf_op | source)
XLA Modules:
  0.0 1329.7 jit_solution(13453992353371147175)
XLA Ops:
  12.5 8.0 all-to-all-start
  32.9 11.0 all-to-all-done.1
  48.1 56.3 %all_gather.37 = bf16[1024,128]{1,0:T(8,128)(2,1)S(1)} all-gather(bf16[64,128]{1,0:T(8,128)(2,1)S(1)} %copy-done.69), channel_id=1, replica_groups=mesh['row'=16,'col'=8] {'row'}, dimensions={0}, use_global_device_ids=true | all-gather | bytes 278528 | tf_op jit(solution)/shard_map/all_gather | solution.py:164
  104.4 24.0 %all_gather.36 = bf16[1024,128]{1,0:T(8,128)(2,1)} all-gather(bf16[64,128]{1,0:T(8,128)(2,1)S(1)} %copy-done.70), channel_id=1, replica_groups=mesh['row'=16,'col'=8] {'row'}, dimensions={0}, use_global_device_ids=true | all-gather | bytes 278528 | tf_op jit(solution)/shard_map/all_gather | solution.py:165
  130.7 20.9 %all_gather.38 = bf16[1024,256]{1,0:T(8,128)(2,1)S(1)} all-gather(bf16[64,256]{1,0:T(8,128)(2,1)S(1)} %copy-done.62), channel_id=1, replica_groups=mesh['row'=16,'col'=8] {'row'}, dimensions={0}, use_global_device_ids=true | all-gather | bytes 557056 | tf_op jit(solution)/shard_map/all_gather | solution.py:163
  151.5 25.1 %all_gather.39 = bf16[256,1024]{0,1:T(8,128)(2,1)} all-gather(bf16[256,64]{0,1:T(8,128)(2,1)S(1)} %copy-done.63), channel_id=1, replica_groups=mesh['row'=16,'col'=8] {'row'}, dimensions={1}, use_global_device_ids=true | all-gather | bytes 557056 | tf_op jit(solution)/shard_map/all_gather | solution.py:166
  232.5 51.4 %reduce-scatter.12.cloned.1.call-done = bf16[256,1024]{1,0:T(8,128)(2,1)} async-done(((bf16[2048,1024]{1,0:T(8,128)(2,1)}), bf16[256,1024]{1,0:T(8,128)(2,1)}) %reduce-scatter.12.cloned.1.call-update) | async-done | bytes 524304 | tf_op jit(solution)/shard_map/reduce_scatter | solution.py:206
  289.7 55.8 %all_to_all.60 = bf16[16,16,1024]{2,1,0:T(8,128)(2,1)} all-to-all(bf16[16,16,1024]{2,1,0:T(8,128)(2,1)S(1)} %bitcast.516), channel_id=1, replica_groups=mesh['row'=16,'col'=8] {'row'}, dimensions={0} | all-to-all | bytes 1048576 | tf_op jit(solution)/shard_map/all_to_all | solution.py:155
  348.5 63.4 %all_gather.41 = bf16[1024,384]{1,0:T(8,128)(2,1)} all-gather(bf16[64,384]{1,0:T(8,128)(2,1)} %param.47), channel_id=1, replica_groups=mesh['row'=16,'col'=8] {'row'}, dimensions={0}, use_global_device_ids=true | all-gather | bytes 835584 | tf_op jit(solution)/shard_map/all_gather | solution.py:167
  412.0 25.6 %all_gather.42 = bf16[1024,384]{1,0:T(8,128)(2,1)} all-gather(bf16[64,384]{1,0:T(8,128)(2,1)} %param.48), channel_id=1, replica_groups=mesh['row'=16,'col'=8] {'row'}, dimensions={0}, use_global_device_ids=true | all-gather | bytes 835584 | tf_op jit(solution)/shard_map/all_gather | solution.py:168
  437.6 23.4 %all_gather.43 = bf16[384,1024]{0,1:T(8,128)(2,1)} all-gather(bf16[384,64]{0,1:T(8,128)(2,1)} %param.49), channel_id=1, replica_groups=mesh['row'=16,'col'=8] {'row'}, dimensions={1}, use_global_device_ids=true | all-gather | bytes 835584 | tf_op jit(solution)/shard_map/all_gather | solution.py:169
  471.7 9.1 multiply_convert_fusion
  488.1 50.0 %reduce-scatter.16.cloned.1.call-done = bf16[256,1024]{1,0:T(8,128)(2,1)} async-done(((bf16[2048,1024]{1,0:T(8,128)(2,1)}), bf16[256,1024]{1,0:T(8,128)(2,1)}) %reduce-scatter.16.cloned.1.call-update) | async-done | bytes 524304 | tf_op jit(solution)/shard_map/reduce_scatter | solution.py:245
  543.9 51.5 %all-gather.11.cloned.1.call-done = bf16[2048,1024]{1,0:T(8,128)(2,1)} async-done(((bf16[256,1024]{1,0:T(8,128)(2,1)}), bf16[2048,1024]{1,0:T(8,128)(2,1)}) %all-gather.11.cloned.1.call-update) | async-done | bytes 4194320 | tf_op jit(solution)/shard_map/all_gather | solution.py:257
  708.2 12.1 reduce-scatter.18.cloned.1.call-done
  721.8 52.8 %reduce-scatter.14.cloned.1.call-done = bf16[256,1024]{1,0:T(8,128)(2,1)} async-done(((bf16[2048,1024]{1,0:T(8,128)(2,1)}), bf16[256,1024]{1,0:T(8,128)(2,1)}) %reduce-scatter.14.cloned.1.call-update) | async-done | bytes 524304 | tf_op jit(solution)/shard_map/reduce_scatter | solution.py:217
  801.2 42.0 %reduce-scatter.32.cloned.1.call-done = bf16[384,64]{0,1:T(8,128)(2,1)} async-done(((bf16[384,1024]{0,1:T(8,128)(2,1)}), bf16[384,64]{0,1:T(8,128)(2,1)}) %reduce-scatter.32.cloned.1.call-update) | async-done | bytes 49168 | tf_op jit(solution)/shard_map/reduce_scatter | solution.py:327
  844.6 67.1 %reduce-scatter.30.cloned.1.call-done = bf16[64,384]{1,0:T(8,128)(2,1)} async-done(((bf16[1024,384]{1,0:T(8,128)(2,1)}), bf16[64,384]{1,0:T(8,128)(2,1)}) %reduce-scatter.30.cloned.1.call-update) | async-done | bytes 49168 | tf_op jit(solution)/shard_map/reduce_scatter | solution.py:324
  913.2 67.3 %reduce-scatter.28.cloned.1.call-done = bf16[64,384]{1,0:T(8,128)(2,1)} async-done(((bf16[1024,384]{1,0:T(8,128)(2,1)}), bf16[64,384]{1,0:T(8,128)(2,1)}) %reduce-scatter.28.cloned.1.call-update) | async-done | bytes 49168 | tf_op jit(solution)/shard_map/reduce_scatter | solution.py:321
  981.9 66.1 %reduce-scatter.24.cloned.1.call-done = bf16[64,128]{1,0:T(8,128)(2,1)} async-done(((bf16[1024,128]{1,0:T(8,128)(2,1)}), bf16[64,128]{1,0:T(8,128)(2,1)}) %reduce-scatter.24.cloned.1.call-update) | async-done | bytes 16400 | tf_op jit(solution)/shard_map/reduce_scatter | solution.py:315
  1049.4 66.9 %reduce-scatter.22.cloned.1.call-done = bf16[64,128]{1,0:T(8,128)(2,1)} async-done(((bf16[1024,128]{1,0:T(8,128)(2,1)}), bf16[64,128]{1,0:T(8,128)(2,1)}) %reduce-scatter.22.cloned.1.call-update) | async-done | bytes 16400 | tf_op jit(solution)/shard_map/reduce_scatter | solution.py:312
  1117.6 66.7 %reduce-scatter.26.cloned.1.call-done = bf16[256,64]{0,1:T(8,128)(2,1)} async-done(((bf16[256,1024]{0,1:T(8,128)(2,1)}), bf16[256,64]{0,1:T(8,128)(2,1)}) %reduce-scatter.26.cloned.1.call-update) | async-done | bytes 32784 | tf_op jit(solution)/shard_map/reduce_scatter | solution.py:318
  1185.7 67.1 %reduce-scatter.20.cloned.1.call-done = bf16[64,256]{1,0:T(8,128)(2,1)} async-done(((bf16[1024,256]{1,0:T(8,128)(2,1)}), bf16[64,256]{1,0:T(8,128)(2,1)}) %reduce-scatter.20.cloned.1.call-update) | async-done | bytes 32784 | tf_op jit(solution)/shard_map/reduce_scatter | solution.py:309
  1254.3 64.5 %all-reduce.6 = (f32[1024]{0:T(1024)}, f32[1024]{0:T(1024)}, f32[128]{0:T(128)}, f32[128]{0:T(128)}) all-reduce(f32[1024]{0:T(1024)S(1)} %get-tuple-element.131, f32[1024]{0:T(1024)S(1)} %copy-done.68, f32[128]{0:T(128)S(1)} %get-tuple-element.125, f32[128]{0:T(128)S(1)} %get-tuple-element.127), channel_id=1, replica_groups=mesh['row'=16,'col'=8] {'row','col'}, use_global_device_ids=true, to_apply=%region_36.37 | all-reduce | flops 2304 | bytes 18432 | tf_op jit(solution)/shard_map/psum | solution.py:305
  (392 shorter events, 265.5 us)
Async XLA Ops:
  7.2 97.2 %copy-start.70 = (bf16[64,128]{1,0:T(8,128)(2,1)S(1)}, bf16[64,128]{1,0:T(8,128)(2,1)}, u32[]{:S(2)}) copy-start(bf16[64,128]{1,0:T(8,128)(2,1)} %param.45) | copy-start | bytes 49156
  7.2 123.5 %copy-start.62 = (bf16[64,256]{1,0:T(8,128)(2,1)S(1)}, bf16[64,256]{1,0:T(8,128)(2,1)}, u32[]{:S(2)}) copy-start(bf16[64,256]{1,0:T(8,128)(2,1)} %param.43) | copy-start | bytes 98308
  7.2 144.3 %copy-start.63 = (bf16[256,64]{0,1:T(8,128)(2,1)S(1)}, bf16[256,64]{0,1:T(8,128)(2,1)}, u32[]{:S(2)}) copy-start(bf16[256,64]{0,1:T(8,128)(2,1)} %param.46) | copy-start | bytes 98308
  12.5 15.5 %all-to-all-start = ((s32[16,16,1]{1,2,0:T(1,128)}), s32[16,16,1]{1,2,0:T(1,128)S(1)}, u32[]{:S(2)}, u32[]{:S(2)}) async-start(s32[16,16,1]{1,2,0:T(1,128)} %bitcast.2), calls=%async_computation | async-start | bytes 16384 | tf_op jit(solution)/shard_map/all_to_all | solution.py:156
  28.0 15.9 %all-to-all-start.1 = ((bf16[16,16,1024]{2,1,0:T(8,128)(2,1)}), bf16[16,16,1024]{2,1,0:T(8,128)(2,1)S(1)}, u32[]{:S(2)}, u32[]{:S(2)}) async-start(bf16[16,16,1024]{2,1,0:T(8,128)(2,1)} %bitcast.4), calls=%async_computation.1 | async-start | bytes 1048576 | tf_op jit(solution)/shard_map/all_to_all | solution.py:154
  31.5 153.9 %all-gather.5.cloned.1.call-start = ((), (), s32[]{:S(2)}) async-start(), calls=%async_computation.16 | async-start | bytes 4718592 | tf_op jit(solution)/shard_map/all_gather | solution.py:202
  47.6 236.4 %reduce-scatter.12.cloned.1.call-start = ((), (), s32[]{:S(2)}) async-start(), calls=%async_computation.17 | async-start | bytes 4718592 | tf_op jit(solution)/shard_map/reduce_scatter | solution.py:206
  48.0 151.4 %copy-start.86 = (f32[64]{0:T(128)}, f32[64]{0:T(128)S(1)}, u32[]{:S(2)}) copy-start(f32[64]{0:T(128)S(1)} %multiply_power_fusion) | copy-start | bytes 772
  232.5 228.6 %all-gather.7.cloned.1.call-start = ((), (), s32[]{:S(2)}) async-start(), calls=%async_computation.18 | async-start | bytes 4718592 | tf_op jit(solution)/shard_map/all_gather | solution.py:213
  287.4 184.3 %all-gather.9.cloned.1.call-start = ((), (), s32[]{:S(2)}) async-start(), calls=%async_computation.20 | async-start | bytes 4718592 | tf_op jit(solution)/shard_map/all_gather | solution.py:232
  348.5 189.7 %reduce-scatter.16.cloned.1.call-start = ((), (), s32[]{:S(2)}) async-start(), calls=%async_computation.21 | async-start | bytes 4718592 | tf_op jit(solution)/shard_map/reduce_scatter | solution.py:245
  487.9 107.5 %all-gather.11.cloned.1.call-start = ((), (), s32[]{:S(2)}) async-start(), calls=%async_computation.22 | async-start | bytes 4718592 | tf_op jit(solution)/shard_map/all_gather | solution.py:257
  543.9 176.4 %reduce-scatter.18.cloned.1.call-start = ((), (), s32[]{:S(2)}) async-start(), calls=%async_computation.23 | async-start | bytes 4718592 | tf_op jit(solution)/shard_map/reduce_scatter | solution.py:291
  668.3 106.3 %reduce-scatter.14.cloned.1.call-start = ((), (), s32[]{:S(2)}) async-start(), calls=%async_computation.19 | async-start | bytes 4718592 | tf_op jit(solution)/shard_map/reduce_scatter | solution.py:217
  675.2 168.0 %reduce-scatter.32.cloned.1.call-start = ((), (), s32[]{:S(2)}) async-start(), calls=%async_computation.30 | async-start | bytes 835584 | tf_op jit(solution)/shard_map/reduce_scatter | solution.py:327
  682.3 229.5 %reduce-scatter.30.cloned.1.call-start = ((), (), s32[]{:S(2)}) async-start(), calls=%async_computation.29 | async-start | bytes 835584 | tf_op jit(solution)/shard_map/reduce_scatter | solution.py:324
  688.5 292.0 %reduce-scatter.28.cloned.1.call-start = ((), (), s32[]{:S(2)}) async-start(), calls=%async_computation.28 | async-start | bytes 835584 | tf_op jit(solution)/shard_map/reduce_scatter | solution.py:321
  694.2 353.9 %reduce-scatter.24.cloned.1.call-start = ((), (), s32[]{:S(2)}) async-start(), calls=%async_computation.26 | async-start | bytes 278528 | tf_op jit(solution)/shard_map/reduce_scatter | solution.py:315
  698.6 417.7 %reduce-scatter.22.cloned.1.call-start = ((), (), s32[]{:S(2)}) async-start(), calls=%async_computation.25 | async-start | bytes 278528 | tf_op jit(solution)/shard_map/reduce_scatter | solution.py:312
  703.2 481.1 %reduce-scatter.26.cloned.1.call-start = ((), (), s32[]{:S(2)}) async-start(), calls=%async_computation.27 | async-start | bytes 557056 | tf_op jit(solution)/shard_map/reduce_scatter | solution.py:318
  778.5 19.1 %all-to-all-start.4 = ((bf16[16,16,1024]{2,1,0:T(8,128)(2,1)}), bf16[16,16,1024]{2,1,0:T(8,128)(2,1)S(1)}, u32[]{:S(2)}, u32[]{:S(2)}) async-start(bf16[16,16,1024]{2,1,0:T(8,128)(2,1)} %bitcast.119), calls=%async_computation.8 | async-start | bytes 1048576 | tf_op jit(solution)/shard_map/all_to_all | solution.py:335
  785.2 467.6 %reduce-scatter.20.cloned.1.call-start = ((), (), s32[]{:S(2)}) async-start(), calls=%async_computation.24 | async-start | bytes 557056 | tf_op jit(solution)/shard_map/reduce_scatter | solution.py:309
  790.0 464.3 %copy-start.68 = (f32[1024]{0:T(1024)S(1)}, f32[1024]{0:T(1024)}, u32[]{:S(2)}) copy-start(f32[1024]{0:T(1024)} %get-tuple-element.129) | copy-start | bytes 12292
  797.6 523.2 %all-to-all-start.2 = ((bf16[16,16,1024]{2,1,0:T(8,128)(2,1)}), bf16[16,16,1024]{2,1,0:T(8,128)(2,1)S(1)}, u32[]{:S(2)}, u32[]{:S(2)}) async-start(bf16[16,16,1024]{2,1,0:T(8,128)(2,1)} %bitcast.50), calls=%async_computation.4 | async-start | bytes 1048576 | tf_op jit(solution)/shard_map/all_to_all | solution.py:334
  (102 other events, 1096.2 us)
Sparse Core Ops, SparseCore 0:
  47.7 50.3 all-gather.4
  232.6 51.2 reduce-scatter.11
  287.5 55.6 all-gather.6
  348.6 51.2 all-gather.8
  488.0 50.1 reduce-scatter.15
  544.0 51.3 all-gather.10
  668.4 51.8 reduce-scatter.17
  722.7 51.8 reduce-scatter.13
  778.3 64.7 reduce-scatter.31
  846.8 64.9 reduce-scatter.29
  915.5 64.9 reduce-scatter.27
  984.1 63.9 reduce-scatter.23
  1052.2 63.9 reduce-scatter.21
  1119.9 64.4 reduce-scatter.25
  1188.4 64.3 reduce-scatter.19
where the time goes:
time: 1340 us; the launch traced here: 1330 us
  waiting for transfers between devices  682 us (51%)
  blocking collectives  359 us (27%)
  matrix products  144 us (11%)
  other arithmetic  69.7 us (5%)
  local copies, waits for them, and re-layouts  35.4 us (3%)
  starting transfers between devices  22.9 us (2%)
  between operations  16 us (1%)
    reduce_scatter x1, waiting for transfers between devices, local(): lax.psum_scatter(grad_gate.astype(jnp.bfloat16), 'row', scatter_dimension...  67.3 us
    reduce_scatter x1, waiting for transfers between devices, local(): lax.psum_scatter(grad_up.astype(jnp.bfloat16), 'row', scatter_dimension=0...  67.1 us
    reduce_scatter x1, waiting for transfers between devices, local(): lax.psum_scatter(grad_query.astype(jnp.bfloat16), 'row', scatter_dimensio...  67.1 us
    reduce_scatter x1, waiting for transfers between devices, local(): lax.psum_scatter(grad_key.astype(jnp.bfloat16), 'row', scatter_dimension=...  66.9 us
    reduce_scatter x1, waiting for transfers between devices, local(): lax.psum_scatter(grad_out_weight.astype(jnp.bfloat16), 'row', scatter_dim...  66.7 us
    reduce_scatter x1, waiting for transfers between devices, local(): lax.psum_scatter(grad_value.astype(jnp.bfloat16), 'row', scatter_dimensio...  66.1 us
    psum x1, blocking collectives, local(): lax.psum((grad_attn_gain, grad_ffn_gain, grad_q_gain, grad_k_gain), ('row...  64.5 us
    all_gather x1, blocking collectives, local(): lax.all_gather(w_gate, 'row', axis=0, tiled=True)  63.4 us
  transfers between devices with their start and end apart: 19, of which 15 were waited for; matrix products, arithmetic and copies ran while one was open for 7% of the time, Pallas kernels for 0%

commit v1 on v0

v1 whole, which is shorter than its diff:
```python
import functools
import math

import jax
import jax.numpy as jnp
from jax import lax
from jax.experimental import pallas as pl
from jax.experimental.pallas import tpu as pltpu
from jax.sharding import PartitionSpec as P

MESH = pl.DeviceIdType.MESH
BF = jnp.bfloat16
F32 = jnp.float32
I32 = jnp.int32
EPSILON = 1e-06
ROPE_BASE = 1000000.0
HEAD = 128
NR = 16
NC = 8
ROWS = 256
WIDTH = 1024
GROUP = 2048
ORDERS = (("x", "y", "z"), ("y", "z", "x"), ("z", "x", "y"))
HBM = pl.BlockSpec(memory_space=pltpu.HBM)
VMEM = pl.BlockSpec(memory_space=pltpu.VMEM)
DMA = pltpu.SemaphoreType.DMA


def sds(shape, dtype=BF):
    return jax.ShapeDtypeStruct(shape, dtype)


def params(cid=None, mib=56, **kw):
    if cid is not None:
        kw.update(collective_id=cid, has_side_effects=True)
    return pltpu.CompilerParams(vmem_limit_bytes=mib << 20, **kw)


def where_am_i():
    r = lax.axis_index("row")
    c = lax.axis_index("col")
    return {"x": c % 4, "y": r // 4, "z": 2 * ((r // 2) % 2) + c // 4, "k": r % 2}


def device(at):
    return (at["y"] * 4 + (at["z"] // 2) * 2 + at["k"], (at["z"] % 2) * 4 + at["x"])


def moved(at, axis, step):
    out = dict(at)
    out[axis] = (at[axis] + step) % 4
    return out


def mate(at):
    out = dict(at)
    out["k"] = 1 - at["k"]
    return out


def meet(peers):
    barrier = pltpu.get_barrier_semaphore()
    for p in peers:
        pl.semaphore_signal(barrier, inc=1, device_id=p, device_id_type=MESH)
    pl.semaphore_wait(barrier, len(peers))


def ring_peers(at):
    return [device(moved(at, a, s)) for a in "xyz" for s in (1, -1)]


def row_peers(at):
    r = lax.axis_index("row")
    c = lax.axis_index("col")
    return [((r + d) % NR, c) for d in range(1, NR)]


def col_peers(at):
    r = lax.axis_index("row")
    c = lax.axis_index("col")
    return [(r, (c + d) % NC) for d in range(1, NC)]


def remote(src, dst, ssem, rsem, to):
    return pltpu.make_async_remote_copy(
        src_ref=src, dst_ref=dst, send_sem=ssem, recv_sem=rsem, device_id=to, device_id_type=MESH
    )


def block_index(sel, with_core=None):
    full = slice(None)
    z = sel.get("z")
    idx = (
        sel.get("x", full),
        full if z is None else z % 2,
        sel.get("y", full),
        full if z is None else z // 2,
    )
    return idx if with_core is None else idx + (with_core,)


def gather_phases(at, locs, outs, sems, late):
    ssem, rsem, msem, nsem = sems
    k = at["k"]
    waits = []

    def region(s, t, pos):
        order = ORDERS[s]
        sel = {a: at[a] for a in order[t + 1 :]}
        sel[order[t]] = pos
        return block_index(sel, k)

    n = len(locs)
    half = locs[0].shape[0] // 2
    for t in range(3):
        firsts = []
        for s in range(n):
            a = ORDERS[s][t]
            p = at[a]
            here = outs[s].at[region(s, t, p)]
            src = locs[s] if t == 0 else here
            pair = []
            for d, step in enumerate((1, -1)):
                cp = remote(
                    src, here, ssem.at[s, t, d], rsem.at[s, t, d], device(moved(at, a, step))
                )
                cp.start()
                pair.append(cp)
            if t == 2:
                cp = remote(here, here, msem.at[s, 0], nsem.at[s, 0], device(mate(at)))
                cp.start()
                late.append(cp)
            firsts.append(pair)
        seconds = []
        for s in range(n):
            a = ORDERS[s][t]
            p = at[a]
            pair = []
            for d, step in enumerate((1, -1)):
                firsts[s][d].wait_recv()
                came = region(s, t, (p - step) % 4)
                rows = pl.ds(d * half, half)
                cp = remote(
                    outs[s].at[came + (rows,)],
                    outs[s].at[came + (rows,)],
                    ssem.at[s, t, 2 + d],
                    rsem.at[s, t, 2 + d],
                    device(moved(at, a, step)),
                )
                cp.start()
                pair.append(cp)
                if t == 2:
                    ref = outs[s].at[came]
                    cp = remote(ref, ref, msem.at[s, 1 + d], nsem.at[s, 1 + d], device(mate(at)))
                    cp.start()
                    late.append(cp)
            seconds.append(pair)
        for s in range(n):
            for cp in seconds[s]:
                cp.wait_recv()
            if t == 2:
                p = at[ORDERS[s][t]]
                ref = outs[s].at[region(s, t, (p + 2) % 4)]
                cp = remote(ref, ref, msem.at[s, 3], nsem.at[s, 3], device(mate(at)))
                cp.start()
                late.append(cp)
        waits += [c for pair in firsts + seconds for c in pair]
    return waits


def gather_sems(n=3):
    return [DMA((n, 3, 4)), DMA((n, 3, 4)), DMA((n, 4)), DMA((n, 4)), DMA((n,))]


def gather_shape(w):
    return sds((4, 2, 4, 2, 2, 64, w))


def run_gather(at, locs, outs, sems):
    ssem, rsem, msem, nsem, lsem = sems
    own = []
    for s in range(len(locs)):
        cp = pltpu.make_async_copy(
            locs[s], outs[s].at[block_index({a: at[a] for a in "xyz"}, at["k"])], lsem.at[s]
        )
        cp.start()
        own.append(cp)
    for cp in own:
        cp.wait()
    late = []
    waits = gather_phases(at, locs, outs, (ssem, rsem, msem, nsem), late)
    for cp in late:
        cp.wait()
    for cp in waits:
        cp.wait_send()


def gather_kernel(l0, l1, l2, g0, g1, g2, *sems):
    at = where_am_i()
    meet(ring_peers(at) + [device(mate(at))])
    run_gather(at, (l0, l1, l2), (g0, g1, g2), sems)


def gather(blocks, cid, name):
    w = blocks[0].shape[1]
    return pl.pallas_call(
        gather_kernel,
        name=name,
        out_shape=[gather_shape(w)] * 3,
        in_specs=[HBM] * 3,
        out_specs=[HBM] * 3,
        scratch_shapes=gather_sems(),
        compiler_params=params(cid),
    )(*blocks)


def lead_shape(axes):
    out = ()
    for a in ("x", "zl", "y", "zh"):
        if a[0] in axes:
            out += (4,) if a in "xy" else (2,)
    return out


def sub_index(sel, axes):
    out = ()
    for a in ("x", "zl", "y", "zh"):
        if a[0] not in axes:
            continue
        pos = sel.get(a[0])
        if pos is None:
            out += (slice(None),)
        elif a == "zl":
            out += (pos % 2,)
        elif a == "zh":
            out += (pos // 2,)
        else:
            out += (pos,)
    return out


def unravel(i, shape):
    out = ()
    for n in reversed(shape):
        out = (i % n,) + out
        i = i // n
    return out


def add_blocks(lead, dst, terms):
    n = math.prod(lead)

    def one(i):
        j = unravel(i, lead)
        total = None
        for ref, pre in terms:
            v = ref[pre(j)].astype(F32)
            total = v if total is None else total + v
        dst[0][dst[1](j)] = total.astype(dst[0].dtype)

    if n == 1:
        one(0)
    else:

        @pl.loop(0, n)
        def _(i):
            one(i)


def scatter_buffers(w, n=3):
    out = []
    for s in range(n):
        for t in range(3):
            lead = lead_shape(ORDERS[s][: 2 - t])
            out.append(pltpu.VMEM((2,) + lead + (32, w), BF))
            out.append(pltpu.VMEM((2,) + lead + (64, w), BF))
            out.append(pltpu.VMEM((2,) + lead + (32, w), BF))
            if t == 0:
                out.append(pltpu.VMEM(lead + (64, w), BF))
            elif t == 1:
                out.append(pltpu.VMEM(lead + (64, w), BF))
    return out


PER_STREAM = 11


def scatter_sems(n=3):
    return [DMA((n, 3, 6)), DMA((n, 3, 6)), DMA((n, 3))]


def run_scatter(at, parts, results, bufs, sems):
    ssem, rsem, lsem = sems
    n = len(parts)
    cur = [(parts[s], "xyz") for s in range(n)]
    waits = []
    lo, hi = pl.ds(0, 32), pl.ds(32, 32)
    for t in range(3):
        st = []
        for s in range(n):
            b = bufs[s * PER_STREAM : (s + 1) * PER_STREAM]
            rel_in, piece_in, rel_out = b[4 * t : 4 * t + 3]
            total = b[4 * t + 3] if t < 2 else None
            a = ORDERS[s][2 - t]
            rem = ORDERS[s][: 2 - t]
            ref, axes = cur[s]
            p = at[a]

            def src(pos, rows, ref=ref, axes=axes, a=a):
                return ref.at[sub_index({a: pos % 4}, axes) + (rows,)]

            right, left = device(moved(at, a, 1)), device(moved(at, a, -1))
            allr = (slice(None),) * len(lead_shape(rem))
            cps = [
                remote(src(p + 2, lo), rel_in.at[0], ssem.at[s, t, 0], rsem.at[s, t, 0], right),
                remote(src(p + 2, hi), rel_in.at[1], ssem.at[s, t, 1], rsem.at[s, t, 1], left),
                remote(
                    src(p + 1, hi),
                    piece_in.at[(0,) + allr + (hi,)],
                    ssem.at[s, t, 2],
                    rsem.at[s, t, 2],
                    right,
                ),
                remote(
                    src(p - 1, lo),
                    piece_in.at[(1,) + allr + (lo,)],
                    ssem.at[s, t, 3],
                    rsem.at[s, t, 3],
                    left,
                ),
            ]
            for cp in cps:
                cp.start()
            loads = []
            if t == 0:
                loads = [
                    pltpu.make_async_copy(src(p + 1, lo), rel_out.at[0], lsem.at[s, 0]),
                    pltpu.make_async_copy(src(p - 1, hi), rel_out.at[1], lsem.at[s, 1]),
                    pltpu.make_async_copy(src(p, slice(None)), total, lsem.at[s, 2]),
                ]
                for cp in loads:
                    cp.start()
            st.append((rel_in, piece_in, rel_out, total, a, rem, right, left, cps, loads, allr))
        for s in range(n):
            rel_in, piece_in, rel_out, total, a, rem, right, left, cps, loads, allr = st[s]
            ref, axes = cur[s]
            lead = lead_shape(rem)
            p = at[a]
            for d, (rows, pos, to) in enumerate(((lo, p + 1, right), (hi, p - 1, left))):
                cps[d].wait_recv()
                if t == 0:
                    loads[d].wait()
                    mine = (rel_out, lambda j, d=d: (d,) + j)
                else:

                    def pick(j, pos=pos, rows=rows, axes=axes, a=a, rem=rem):
                        it = iter(j)
                        out = ()
                        for q in ("x", "zl", "y", "zh"):
                            if q[0] not in axes:
                                continue
                            if q[0] == a:
                                z = pos % 4
                                out += (z % 2 if q == "zl" else z // 2 if q == "zh" else z,)
                            else:
                                out += (next(it),)
                        return out + (rows,)

                    mine = (ref, pick)
                add_blocks(
                    lead,
                    (rel_out, lambda j, d=d: (d,) + j),
                    [mine, (rel_in, lambda j, d=d: (d,) + j)],
                )
                cp = remote(
                    rel_out.at[d],
                    piece_in.at[(d,) + allr + (rows,)],
                    ssem.at[s, t, 4 + d],
                    rsem.at[s, t, 4 + d],
                    to,
                )
                cp.start()
                cps.append(cp)
        for s in range(n):
            rel_in, piece_in, rel_out, total, a, rem, right, left, cps, loads, allr = st[s]
            ref, axes = cur[s]
            lead = lead_shape(rem)
            p = at[a]
            for i in (2, 3, 4, 5):
                cps[i].wait_recv()
            if t == 0:
                loads[2].wait()
                mine = (total, lambda j: j)
            else:

                def pick(j, pos=p, axes=axes, a=a):
                    it = iter(j)
                    out = ()
                    for q in ("x", "zl", "y", "zh"):
                        if q[0] not in axes:
                            continue
                        if q[0] == a:
                            out += (pos % 2 if q == "zl" else pos // 2 if q == "zh" else pos,)
                        else:
                            out += (next(it),)
                    return out

                mine = (ref, pick)
            dst = (total, lambda j: j) if t < 2 else (results[s], lambda j: (slice(None),) * 2)
            add_blocks(
                lead,
                dst,
                [
                    mine,
                    (piece_in, lambda j: (0,) + j),
                    (piece_in, lambda j: (1,) + j),
                ],
            )
            cur[s] = (total, rem)
            waits += cps
    for cp in waits:
        cp.wait_send()


def scatter_kernel(w, p0, p1, p2, r0, r1, r2, *scratch):
    at = where_am_i()
    meet(ring_peers(at))
    bufs, sems = scratch[: 3 * PER_STREAM], scratch[3 * PER_STREAM :]
    run_scatter(at, (p0, p1, p2), (r0, r1, r2), bufs, sems)


def scatter(parts, cid, name):
    w = parts[0].shape[-1]
    return pl.pallas_call(
        functools.partial(scatter_kernel, w),
        name=name,
        out_shape=[sds((64, w), F32)] * 3,
        in_specs=[HBM] * 3,
        out_specs=[VMEM] * 3,
        scratch_shapes=scatter_buffers(w) + scatter_sems(),
        compiler_params=params(cid),
    )(*parts)


def swap_over(axis, src, dst, ssem, rsem, lsem):
    n = NR if axis == "row" else NC
    r = lax.axis_index("row")
    c = lax.axis_index("col")
    me = r if axis == "row" else c
    cps = []
    for d in range(1, n):
        to = (me + d) % n
        cp = remote(
            src.at[to],
            dst.at[me],
            ssem.at[d - 1],
            rsem.at[d - 1],
            (to, c) if axis == "row" else (r, to),
        )
        cp.start()
        cps.append(cp)
    own = pltpu.make_async_copy(src.at[me], dst.at[me], lsem)
    own.start()
    return cps + [own]


def swap_sems(axis):
    n = NR if axis == "row" else NC
    return [DMA((n - 1,)), DMA((n - 1,)), DMA]


def col_swap_kernel(src, dst, ssem, rsem, lsem):
    at = where_am_i()
    meet(col_peers(at))
    for cp in swap_over("col", src, dst, ssem, rsem, lsem):
        cp.wait()


def col_swap(src, cid, name):
    return pl.pallas_call(
        col_swap_kernel,
        name=name,
        out_shape=sds(src.shape),
        in_specs=[HBM],
        out_specs=HBM,
        scratch_shapes=swap_sems("col"),
        compiler_params=params(cid),
    )(src)


def dot(a, b, dims=((1,), (0,))):
    return lax.dot_general(a, b, (dims, ((), ())), preferred_element_type=F32)


NT = ((1,), (1,))
TN = ((0,), (0,))


def iota(shape, dim):
    return lax.broadcasted_iota(I32, shape, dim)


def onehot(cond):
    return cond.astype(F32).astype(BF)


def unrope(g, cos, sin):
    return g * cos - pltpu.roll(g, HEAD // 2, 1) * sin


def mean_square_scale(v):
    return lax.rsqrt(jnp.mean(v * v, axis=-1, keepdims=True) + EPSILON)


def slots_sent(target_row, target_col):
    g_row, g_col = target_row // GROUP, target_col // GROUP
    same = g_row == g_col
    i0, i1 = iota((ROWS, ROWS), 0), iota((ROWS, ROWS), 1)
    before_row = jnp.sum((same & (i0 < i1)).astype(F32), axis=0, keepdims=True).astype(I32)
    before_col = jnp.sum((same & (i1 < i0)).astype(F32), axis=1, keepdims=True).astype(I32)
    return g_row * (ROWS // NR) + before_row, g_col * (ROWS // NR) + before_col


def dispatch_kernel(
    t_row, t_col, tokens, grads, l0, l1, l2, tok, grd, slt, g0, g1, g2, tok_s, grd_s, slt_s, *sems
):
    at = where_am_i()
    meet(ring_peers(at) + row_peers(at))
    place, _ = slots_sent(t_row[...], t_col[...])
    sel = place == iota((ROWS, ROWS), 0)
    pick = onehot(sel)
    tok_s[...] = dot(pick, tokens[...]).astype(BF).reshape(tok_s.shape)
    slot = jnp.sum(jnp.where(sel, t_row[...], 0).astype(F32), axis=1, keepdims=True)
    slt_s[...] = jnp.broadcast_to(slot, (ROWS, HEAD)).astype(I32).reshape(slt_s.shape)
    cps = swap_over("row", tok_s, tok, *sems[0:3])
    cps += swap_over("row", slt_s, slt, *sems[6:9])
    grd_s[...] = dot(pick, grads[...]).astype(BF).reshape(grd_s.shape)
    cps += swap_over("row", grd_s, grd, *sems[3:6])
    run_gather(at, (l0, l1, l2), (g0, g1, g2), sems[9:])
    for cp in cps:
        cp.wait()


def dispatch(target, tokens, grads, blocks):
    w = blocks[0].shape[1]
    return pl.pallas_call(
        dispatch_kernel,
        name="dispatch",
        out_shape=[sds((NR, 16, WIDTH))] * 2
        + [sds((NR, 16, HEAD), I32)]
        + [gather_shape(w)] * 3,
        in_specs=[VMEM] * 4 + [HBM] * 3,
        out_specs=[HBM] * 6,
        scratch_shapes=[pltpu.VMEM((NR, 16, WIDTH), BF)] * 2
        + [pltpu.VMEM((NR, 16, HEAD), I32)]
        + swap_sems("row") * 3
        + gather_sems(),
        compiler_params=params(1),
    )(target.reshape(1, ROWS), target.reshape(ROWS, 1), tokens, grads, *blocks)


def halves_of(v):
    even, odd = [], []
    low = iota((v.shape[0], HEAD), 1) < HEAD // 2
    for m in range(4):
        a, b = v[:, 256 * m : 256 * m + 128], v[:, 256 * m + 128 : 256 * m + 256]
        even.append(jnp.where(low, a, pltpu.roll(b, 64, 1)))
        odd.append(jnp.where(low, pltpu.roll(a, 64, 1), b))
    return jnp.concatenate(even, axis=1), jnp.concatenate(odd, axis=1)


def project_kernel(
    slt, tok, grd, again, qgain, kgain, cos, sin, wq, wkv, out, raw, x_o, dy_o, n1h, dyh, n1_s
):
    c = pl.program_id(0)

    @pl.when(c == 0)
    def _():
        local = slt[...].reshape(ROWS, HEAD)[:, :1] % ROWS
        put = onehot(local == iota((ROWS, ROWS), 1))
        x = dot(put, tok[...].reshape(ROWS, WIDTH), TN)
        dy = dot(put, grd[...].reshape(ROWS, WIDTH), TN)
        x_o[...] = x.astype(BF)
        dy_o[...] = dy.astype(BF)
        n1 = x * mean_square_scale(x) * again[...]
        n1_s[...] = n1.astype(BF)
        a, b = halves_of(n1)
        n1h[0] = a.astype(BF)
        n1h[1] = b.astype(BF)
        a, b = halves_of(dy)
        dyh[0] = a.astype(BF)
        dyh[1] = b.astype(BF)

    n1 = n1_s[...]
    q = dot(n1, wq[0, 0].reshape(WIDTH, 256))
    kv = dot(n1, wkv[0, 0].reshape(WIDTH, 256))
    raw[0, :, 0:256] = q
    raw[0, :, 256:384] = kv[:, :HEAD]
    pieces = ((q[:, :HEAD], qgain), (q[:, HEAD:], qgain), (kv[:, :HEAD], kgain))
    for i, (v, gain) in enumerate(pieces):
        n = v * mean_square_scale(v) * gain[...]
        n = n * cos[...] + pltpu.roll(n, HEAD // 2, 1) * sin[...]
        out[0, :, i * HEAD : (i + 1) * HEAD] = n.astype(BF)
    out[0, :, 3 * HEAD :] = kv[:, HEAD:].astype(BF)


def slab(w):
    return pl.BlockSpec((1, 1, 4, 2, 2, 64, w), lambda c: (c % 4, c // 4, 0, 0, 0, 0, 0))


def whole(shape):
    return pl.BlockSpec(shape, lambda *_: (0,) * len(shape))


def project(slt, tok, grd, again, qgain, kgain, cos, sin, wq, wkv):
    return pl.pallas_call(
        project_kernel,
        name="project",
        grid=(NC,),
        out_shape=[
            sds((NC, ROWS, 512)),
            sds((NC, ROWS, 384), F32),
            sds((ROWS, WIDTH)),
            sds((ROWS, WIDTH)),
            sds((2, ROWS, 512)),
            sds((2, ROWS, 512)),
        ],
        in_specs=[
            whole((NR, 16, HEAD)),
            whole((NR, 16, WIDTH)),
            whole((NR, 16, WIDTH)),
            whole((1, WIDTH)),
            whole((1, HEAD)),
            whole((1, HEAD)),
            whole((ROWS, HEAD)),
            whole((ROWS, HEAD)),
            slab(256),
            slab(256),
        ],
        out_specs=[
            pl.BlockSpec((1, ROWS, 512), lambda c: (c, 0, 0)),
            pl.BlockSpec((1, ROWS, 384), lambda c: (c, 0, 0)),
            whole((ROWS, WIDTH)),
            whole((ROWS, WIDTH)),
            whole((2, ROWS, 512)),
            whole((2, ROWS, 512)),
        ],
        scratch_shapes=[pltpu.VMEM((ROWS, WIDTH), BF)],
        compiler_params=params(),
    )(slt, tok, grd, again, qgain, kgain, cos, sin, wq, wkv)


LOG2E = math.log2(math.e)
QK = 512


def stacked(v):
    return jnp.concatenate([v[:, :HEAD], v[:, HEAD : 2 * HEAD]], axis=0)


def allowed(i, j, first):
    key = j * ROWS + iota((ROWS, QK), 0)
    query = i * ROWS + iota((ROWS, QK), 1) % ROWS
    return (key <= query) & (key >= first)


def attend_kernel(lo, qkv, first, out, o_t, lse):
    i = pl.program_id(0)
    scale = HEAD**-0.5 * LOG2E
    q = stacked(qkv[i, :, 0 : 2 * HEAD])
    start = first[0]

    def scores(j):
        s = dot(qkv[j, :, 2 * HEAD : 3 * HEAD], q, NT) * scale
        return jnp.where(allowed(i, j, start), s, -1e30)

    s = scores(i)
    m = jnp.max(s, axis=0, keepdims=True)
    p = jnp.exp2(s - m)
    total = jnp.sum(p, axis=0, keepdims=True)
    acc = dot(qkv[i, :, 3 * HEAD :], p.astype(BF), TN)

    def step(d, carry):
        m, total, acc = carry
        j = i - 1 - d
        s = scores(j)
        m2 = jnp.maximum(m, jnp.max(s, axis=0, keepdims=True))
        fade = jnp.exp2(m - m2)
        p = jnp.exp2(s - m2)
        total = total * fade + jnp.sum(p, axis=0, keepdims=True)
        acc = acc * fade + dot(qkv[j, :, 3 * HEAD :], p.astype(BF), TN)
        return m2, total, acc

    m, total, acc = lax.fori_loop(0, i - lo[i], step, (m, total, acc))
    o = acc / total
    o_t[0] = o
    lse[0] = m + jnp.log2(total)
    back = o.T
    out[0] = jnp.concatenate([back[:ROWS], back[ROWS:]], axis=1).astype(BF)


def attend(lo, qkv, first):
    return pl.pallas_call(
        attend_kernel,
        name="attend",
        grid_spec=pltpu.PrefetchScalarGridSpec(
            num_scalar_prefetch=1,
            grid=(NC,),
            in_specs=[
                pl.BlockSpec((NC, ROWS, 512), lambda i, lo: (0, 0, 0)),
                pl.BlockSpec((1, 1, QK), lambda i, lo: (i, 0, 0)),
            ],
            out_specs=[
                pl.BlockSpec((1, ROWS, 256), lambda i, lo: (i, 0, 0)),
                pl.BlockSpec((1, HEAD, QK), lambda i, lo: (i, 0, 0)),
                pl.BlockSpec((1, 1, QK), lambda i, lo: (i, 0, 0)),
            ],
        ),
        out_shape=[
            sds((NC, ROWS, 256)),
            sds((NC, HEAD, QK), F32),
            sds((NC, 1, QK), F32),
        ],
        compiler_params=params(),
    )(lo, qkv, first)


def attend_back_kernel(hi, qkv, first, d_o, o_t, lse, out, qs, dos, delta, dq):
    j = pl.program_id(0)
    scale = HEAD**-0.5

    @pl.when(j == 0)
    def _():
        for i in range(NC):
            qs[i] = stacked(qkv[i, :, 0 : 2 * HEAD])
            g = stacked(d_o[i])
            dos[i] = g
            delta[i] = jnp.sum(g.astype(F32).T * o_t[i], axis=0, keepdims=True)
            dq[i] = jnp.zeros((HEAD, QK), F32)

    k = qkv[j, :, 2 * HEAD : 3 * HEAD]
    v = qkv[j, :, 3 * HEAD :]
    k_t = k.astype(F32).T.astype(BF)

    def step(i, carry):
        dk, dv = carry
        s = dot(k, qs[i], NT) * (scale * LOG2E) - lse[i]
        p = jnp.where(allowed(i, j, first[i]), jnp.exp2(s), 0.0)
        ds = (p * (dot(v, dos[i], NT) - delta[i]) * scale).astype(BF)
        dv = dv + dot(p.astype(BF), dos[i])
        dk = dk + dot(ds, qs[i])
        dq[i] += dot(k_t, ds)
        return dk, dv

    zero = jnp.zeros((ROWS, HEAD), F32)
    dk, dv = lax.fori_loop(j, hi[j] + 1, step, (zero, zero))
    done = dq[j].T
    out[0, :, 0:HEAD] = done[:ROWS].astype(BF)
    out[0, :, HEAD : 2 * HEAD] = done[ROWS:].astype(BF)
    out[0, :, 2 * HEAD : 3 * HEAD] = dk.astype(BF)
    out[0, :, 3 * HEAD :] = dv.astype(BF)


def attend_back(hi, qkv, first, d_o, o_t, lse):
    def full(shape):
        return pl.BlockSpec(shape, lambda j, hi: (0,) * len(shape))

    return pl.pallas_call(
        attend_back_kernel,
        name="attend_back",
        grid_spec=pltpu.PrefetchScalarGridSpec(
            num_scalar_prefetch=1,
            grid=(NC,),
            in_specs=[
                full((NC, ROWS, 512)),
                full((NC, 1, QK)),
                full((NC, ROWS, 256)),
                full((NC, HEAD, QK)),
                full((NC, 1, QK)),
            ],
            out_specs=pl.BlockSpec((1, ROWS, 512), lambda j, hi: (j, 0, 0)),
            scratch_shapes=[
                pltpu.VMEM((NC, QK, HEAD), BF),
                pltpu.VMEM((NC, QK, HEAD), BF),
                pltpu.VMEM((NC, 1, QK), F32),
                pltpu.VMEM((NC, HEAD, QK), F32),
            ],
        ),
        out_shape=sds((NC, ROWS, 512)),
        compiler_params=params(),
    )(hi, qkv, first, d_o, o_t, lse)


def middle_kernel(
    slt, x, dy, oa, fgain, wo, wg, wu, wd,
    out_s, dh_o, dhlh, n2h, act, d_o, gain_o,
    h_s, n2_s, acc, dn2, dhl_s,
):
    i = pl.program_id(0)

    @pl.when(i < NC)
    def _():
        part = dot(oa[0], wo[0, 0].reshape(WIDTH, 256), NT)

        @pl.when(i == 0)
        def _():
            acc[...] = x[...].astype(F32) + part

        @pl.when(i > 0)
        def _():
            acc[...] += part

    @pl.when(i == NC)
    def _():
        h = acc[...]
        h_s[...] = h
        n2 = h * mean_square_scale(h) * fgain[...]
        n2_s[...] = n2.astype(BF)
        a, b = halves_of(n2)
        n2h[0] = a.astype(BF)
        n2h[1] = b.astype(BF)
        dn2[...] = jnp.zeros_like(dn2)

    @pl.when((i >= NC) & (i < 2 * NC))
    def _():
        g_w = wg[0, 0].reshape(WIDTH, 384)
        u_w = wu[0, 0].reshape(WIDTH, 384)
        d_w = wd[0, 0].reshape(WIDTH, 384)
        g = dot(n2_s[...], g_w)
        u = dot(n2_s[...], u_w)
        dhid = dot(dy[...], d_w)
        sig = jax.nn.sigmoid(g)
        silu = g * sig
        hid = (silu * u).astype(BF)
        dg = (dhid * u * sig * (1.0 + g * (1.0 - sig))).astype(BF)
        du = (dhid * silu).astype(BF)
        act[0, :, 0:384] = dg
        act[0, :, 384:768] = du
        act[0, :, 768:] = hid
        acc[...] += dot(hid, d_w, NT)
        dn2[...] += dot(dg, g_w, NT) + dot(du, u_w, NT)

    @pl.when(i == 2 * NC - 1)
    def _():
        local = slt[...].reshape(ROWS, HEAD)[:, :1] % ROWS
        take = onehot(local == iota((ROWS, ROWS), 1))
        out_s[...] = dot(take, acc[...].astype(BF)).astype(BF).reshape(out_s.shape)
        h = h_s[...]
        r2 = mean_square_scale(h)
        hn = h * r2
        e = dn2[...]
        gain_o[...] = jnp.sum(e * hn, axis=0, keepdims=True)
        e = e * fgain[...]
        dh = dy[...].astype(F32) + r2 * (e - hn * jnp.mean(e * hn, axis=-1, keepdims=True))
        dh_o[...] = dh
        dhl_s[...] = dh.astype(BF)
        a, b = halves_of(dh)
        dhlh[0] = a.astype(BF)
        dhlh[1] = b.astype(BF)

    @pl.when(i >= 2 * NC)
    def _():
        d_o[0] = dot(dhl_s[...], wo[0, 0].reshape(WIDTH, 256)).astype(BF)


def middle(slt, x, dy, oa, fgain, wo, wg, wu, wd):
    def ffn(w):
        def at(i):
            c = jnp.clip(i - NC, 0, NC - 1)
            return (c % 4, c // 4, 0, 0, 0, 0, 0)

        return pl.BlockSpec((1, 1, 4, 2, 2, 64, w), at)

    def out_at(i):
        c = jnp.where(i < NC, i, jnp.where(i < 2 * NC, NC - 1, i - 2 * NC))
        return (c % 4, c // 4, 0, 0, 0, 0, 0)

    return pl.pallas_call(
        middle_kernel,
        name="middle",
        grid=(3 * NC,),
        out_shape=[
            sds((NR, 16, WIDTH)),
            sds((ROWS, WIDTH), F32),
            sds((2, ROWS, 512)),
            sds((2, ROWS, 512)),
            sds((NC, ROWS, 1152)),
            sds((NC, ROWS, 256)),
            sds((1, WIDTH), F32),
        ],
        in_specs=[
            whole((NR, 16, HEAD)),
            whole((ROWS, WIDTH)),
            whole((ROWS, WIDTH)),
            pl.BlockSpec((1, ROWS, 256), lambda i: (jnp.minimum(i, NC - 1), 0, 0)),
            whole((1, WIDTH)),
            pl.BlockSpec((1, 1, 4, 2, 2, 64, 256), out_at),
            ffn(384),
            ffn(384),
            ffn(384),
        ],
        out_specs=[
            whole((NR, 16, WIDTH)),
            whole((ROWS, WIDTH)),
            whole((2, ROWS, 512)),
            whole((2, ROWS, 512)),
            pl.BlockSpec((1, ROWS, 1152), lambda i: (jnp.clip(i - NC, 0, NC - 1), 0, 0)),
            pl.BlockSpec((1, ROWS, 256), lambda i: (jnp.maximum(i - 2 * NC, 0), 0, 0)),
            whole((1, WIDTH)),
        ],
        scratch_shapes=[
            pltpu.VMEM((ROWS, WIDTH), F32),
            pltpu.VMEM((ROWS, WIDTH), BF),
            pltpu.VMEM((ROWS, WIDTH), F32),
            pltpu.VMEM((ROWS, WIDTH), F32),
            pltpu.VMEM((ROWS, WIDTH), BF),
        ],
        compiler_params=params(),
    )(slt, x, dy, oa, fgain, wo, wg, wu, wd)


def back_swap_kernel(d_o, out_s, act, oa, n2h, dyh, dhlh, *rest):
    outs, sems = rest[:7], rest[7:]
    g_o, got, act_m, oa_m, n2_m, dy_m, dhl_m = outs
    at = where_am_i()
    meet(col_peers(at) + row_peers(at))
    cps = swap_over("col", d_o, g_o, *sems[0:3])
    to = device(mate(at))
    other = 1 - at["k"]
    pairs = (
        (act, act_m),
        (oa, oa_m),
        (n2h.at[other], n2_m),
        (dyh.at[other], dy_m),
        (dhlh.at[other], dhl_m),
    )
    for i, (src, dst) in enumerate(pairs):
        cp = remote(src, dst, sems[6].at[i], sems[7].at[i], to)
        cp.start()
        cps.append(cp)
    cps += swap_over("row", out_s, got, *sems[3:6])
    for cp in cps:
        cp.wait()


def back_swap(d_o, out_s, act, oa, n2h, dyh, dhlh):
    return pl.pallas_call(
        back_swap_kernel,
        name="back_swap",
        out_shape=[sds(d_o.shape), sds(out_s.shape), sds(act.shape), sds(oa.shape)]
        + [sds((ROWS, 512))] * 3,
        in_specs=[HBM] * 7,
        out_specs=[HBM] * 7,
        scratch_shapes=swap_sems("col") + swap_sems("row") + [DMA((5,)), DMA((5,))],
        compiler_params=params(5),
    )(d_o, out_s, act, oa, n2h, dyh, dhlh)


def stack_tokens(k, mine, others, scratch):
    scratch[:, 0:ROWS] = mine[k].astype(F32).T.astype(BF)
    scratch[:, ROWS:] = others[...].astype(F32).T.astype(BF)


def ffn_grads_kernel(n2h, n2_m, dyh, dy_m, act, act_m, g0, g1, g2, n_s, y_s):
    c = pl.program_id(0)

    @pl.when(c == 0)
    def _():
        k = lax.axis_index("row") % 2
        stack_tokens(k, n2h, n2_m, n_s)
        stack_tokens(k, dyh, dy_m, y_s)

    for i, (lhs, out) in enumerate(((n_s, g0), (n_s, g1), (y_s, g2))):
        cols = slice(384 * i, 384 * i + 384)
        rhs = jnp.concatenate([act[0, :, cols], act_m[0, :, cols]], axis=0)
        out[0, 0] = dot(lhs[...], rhs).astype(BF).reshape(4, 2, 64, 384)


def grad_slab(w):
    return pl.BlockSpec((1, 1, 4, 2, 64, w), lambda c: (c % 4, c // 4, 0, 0, 0, 0))


def ffn_grads(n2h, n2_m, dyh, dy_m, act, act_m):
    one = pl.BlockSpec((1, ROWS, 1152), lambda c: (c, 0, 0))
    return pl.pallas_call(
        ffn_grads_kernel,
        name="ffn_grads",
        grid=(NC,),
        out_shape=[sds((4, 2, 4, 2, 64, 384))] * 3,
        in_specs=[whole((2, ROWS, 512)), whole((ROWS, 512))] * 2 + [one, one],
        out_specs=[grad_slab(384)] * 3,
        scratch_shapes=[pltpu.VMEM((512, 2 * ROWS), BF)] * 2,
        compiler_params=params(),
    )(n2h, n2_m, dyh, dy_m, act, act_m)


def attn_grads_kernel(n1h, n1_m, dhlh, dhl_m, dqkv, dqkv_m, oa, oa_m, g0, g1, g2, n_s, h_s):
    c = pl.program_id(0)

    @pl.when(c == 0)
    def _():
        k = lax.axis_index("row") % 2
        stack_tokens(k, n1h, n1_m, n_s)
        stack_tokens(k, dhlh, dhl_m, h_s)

    for i, (lhs, mine, others, out) in enumerate(
        ((n_s, dqkv, dqkv_m, g0), (n_s, dqkv, dqkv_m, g1), (h_s, oa, oa_m, g2))
    ):
        cols = slice(256 * i, 256 * i + 256) if i < 2 else slice(0, 256)
        rhs = jnp.concatenate([mine[0, :, cols], others[0, :, cols]], axis=0)
        out[0, 0] = dot(lhs[...], rhs).astype(BF).reshape(4, 2, 64, 256)


def attn_grads(n1h, n1_m, dhlh, dhl_m, dqkv, dqkv_m, oa, oa_m):
    def one(w):
        return pl.BlockSpec((1, ROWS, w), lambda c: (c, 0, 0))

    return pl.pallas_call(
        attn_grads_kernel,
        name="attn_grads",
        grid=(NC,),
        out_shape=[sds((4, 2, 4, 2, 64, 256))] * 3,
        in_specs=[whole((2, ROWS, 512)), whole((ROWS, 512))] * 2
        + [one(512), one(512), one(256), one(256)],
        out_specs=[grad_slab(256)] * 3,
        scratch_shapes=[pltpu.VMEM((512, 2 * ROWS), BF)] * 2,
        compiler_params=params(),
    )(n1h, n1_m, dhlh, dhl_m, dqkv, dqkv_m, oa, oa_m)


def project_back_kernel(
    slt, x, dh, again, qgain, kgain, cos, sin, raw, dqkv, wq, wkv,
    d_o, dx_s, gain_o, qk_o, acc, gq, gk,
):
    c = pl.program_id(0)

    @pl.when(c == 0)
    def _():
        acc[...] = jnp.zeros_like(acc)
        gq[...] = jnp.zeros_like(gq)
        gk[...] = jnp.zeros_like(gk)

    for i, (gain, g_acc) in enumerate(((qgain, gq), (qgain, gq), (kgain, gk))):
        cols = slice(i * HEAD, (i + 1) * HEAD)
        v = raw[0, :, cols]
        r = mean_square_scale(v)
        xn = v * r
        dn = unrope(dqkv[0, :, cols].astype(F32), cos[...], sin[...])
        g_acc[...] += jnp.sum(dn * xn, axis=0, keepdims=True)
        e = dn * gain[...]
        d_o[0, :, cols] = (r * (e - xn * jnp.mean(e * xn, axis=-1, keepdims=True))).astype(BF)
    d_o[0, :, 3 * HEAD :] = dqkv[0, :, 3 * HEAD :]
    acc[...] += dot(d_o[0, :, 0:256], wq[0, 0].reshape(WIDTH, 256), NT) + dot(
        d_o[0, :, 256:512], wkv[0, 0].reshape(WIDTH, 256), NT
    )

    @pl.when(c == NC - 1)
    def _():
        xv = x[...].astype(F32)
        r1 = mean_square_scale(xv)
        xn = xv * r1
        e = acc[...]
        gain_o[...] = jnp.sum(e * xn, axis=0, keepdims=True)
        e = e * again[...]
        dx = dh[...] + r1 * (e - xn * jnp.mean(e * xn, axis=-1, keepdims=True))
        local = slt[...].reshape(ROWS, HEAD)[:, :1] % ROWS
        take = onehot(local == iota((ROWS, ROWS), 1))
        dx_s[...] = dot(take, dx.astype(BF)).astype(BF).reshape(dx_s.shape)
        qk_o[...] = jnp.concatenate([gq[...], gk[...]], axis=1)


def project_back(slt, x, dh, again, qgain, kgain, cos, sin, raw, dqkv, wq, wkv):
    return pl.pallas_call(
        project_back_kernel,
        name="project_back",
        grid=(NC,),
        out_shape=[
            sds((NC, ROWS, 512)),
            sds((NR, 16, WIDTH)),
            sds((1, WIDTH), F32),
            sds((1, 2 * HEAD), F32),
        ],
        in_specs=[
            whole((NR, 16, HEAD)),
            whole((ROWS, WIDTH)),
            whole((ROWS, WIDTH)),
            whole((1, WIDTH)),
            whole((1, HEAD)),
            whole((1, HEAD)),
            whole((ROWS, HEAD)),
            whole((ROWS, HEAD)),
            pl.BlockSpec((1, ROWS, 384), lambda c: (c, 0, 0)),
            pl.BlockSpec((1, ROWS, 512), lambda c: (c, 0, 0)),
            slab(256),
            slab(256),
        ],
        out_specs=[
            pl.BlockSpec((1, ROWS, 512), lambda c: (c, 0, 0)),
            whole((NR, 16, WIDTH)),
            whole((1, WIDTH)),
            whole((1, 2 * HEAD)),
        ],
        scratch_shapes=[
            pltpu.VMEM((ROWS, WIDTH), F32),
            pltpu.VMEM((1, HEAD), F32),
            pltpu.VMEM((1, HEAD), F32),
        ],
        compiler_params=params(),
    )(slt, x, dh, again, qgain, kgain, cos, sin, raw, dqkv, wq, wkv)


def core_swap_kernel(dqkv, n1h, dqkv_m, n1_m, ssem, rsem):
    at = where_am_i()
    to = device(mate(at))
    meet([to])
    cps = [
        remote(dqkv, dqkv_m, ssem.at[0], rsem.at[0], to),
        remote(n1h.at[1 - at["k"]], n1_m, ssem.at[1], rsem.at[1], to),
    ]
    for cp in cps:
        cp.start()
    for cp in cps:
        cp.wait()


def core_swap(dqkv, n1h):
    return pl.pallas_call(
        core_swap_kernel,
        name="core_swap",
        out_shape=[sds(dqkv.shape), sds((ROWS, 512))],
        in_specs=[HBM] * 2,
        out_specs=[HBM] * 2,
        scratch_shapes=[DMA((2,)), DMA((2,))],
        compiler_params=params(7),
    )(dqkv, n1h)


def last_kernel(p0, p1, p2, dx_s, gains, r0, r1, r2, got, gsum, *scratch):
    nb = 3 * PER_STREAM
    bufs, rest = scratch[:nb], scratch[nb:]
    room, ssem, rsem = rest[:3]
    at = where_am_i()
    far = [device(moved(at, a, 2)) for a in "xyz"]
    meet(ring_peers(at) + far + row_peers(at))
    cps = swap_over("row", dx_s, got, *rest[3:6])
    gsum[...] = gains[...]
    waits = []
    for t, a in enumerate("xyz"):
        p = at[a]
        room[t, p] = gsum[...]
        step = []
        for d in (1, 2, 3):
            cp = remote(
                room.at[t, p], room.at[t, p], ssem.at[t, d - 1], rsem.at[t, d - 1],
                device(moved(at, a, d)),
            )
            cp.start()
            step.append(cp)
        for cp in step:
            cp.wait()
        gsum[...] = room[t, 0] + room[t, 1] + room[t, 2] + room[t, 3]
    k = at["k"]
    room[3, k] = gsum[...]
    cp = remote(room.at[3, k], room.at[3, k], ssem.at[3, 0], rsem.at[3, 0], device(mate(at)))
    cp.start()
    cp.wait()
    gsum[...] = room[3, 0] + room[3, 1]
    run_scatter(at, (p0, p1, p2), (r0, r1, r2), bufs, rest[6:])
    for cp in cps:
        cp.wait()


def last(parts, dx_s, gains):
    w = parts[0].shape[-1]
    return pl.pallas_call(
        last_kernel,
        name="last",
        out_shape=[sds((64, w), F32)] * 3 + [sds(dx_s.shape), sds(gains.shape, F32)],
        in_specs=[HBM] * 4 + [VMEM],
        out_specs=[VMEM] * 3 + [HBM, VMEM],
        scratch_shapes=scatter_buffers(w)
        + [pltpu.VMEM((4, 4) + gains.shape, F32), DMA((4, 3)), DMA((4, 3))]
        + swap_sems("row")
        + scatter_sems(),
        compiler_params=params(8),
    )(*parts, dx_s, gains)


def arrive_kernel(t_row, t_col, out, dx, out_o, dx_o):
    _, place = slots_sent(t_row[...], t_col[...])
    pick = onehot(place == iota((ROWS, ROWS), 1))
    out_o[...] = dot(pick, out[...].reshape(ROWS, WIDTH)).astype(BF)
    dx_o[...] = dot(pick, dx[...].reshape(ROWS, WIDTH)).astype(BF)


def arrive(target, out, dx):
    return pl.pallas_call(
        arrive_kernel,
        name="arrive",
        out_shape=[sds((ROWS, WIDTH))] * 2,
        in_specs=[VMEM] * 4,
        out_specs=[VMEM] * 2,
        compiler_params=params(),
    )(target.reshape(1, ROWS), target.reshape(ROWS, 1), out, dx)


def layout(lengths):
    ends = jnp.cumsum(lengths)
    starts = (ends - lengths).astype(I32)
    slots = jnp.arange(GROUP, dtype=I32)
    first = jnp.max(jnp.where(starts[None, :] <= slots[:, None], starts[None, :], 0), axis=1)
    lo = first[::ROWS] // ROWS
    blocks = jnp.arange(NC, dtype=I32)
    hi = jnp.max(jnp.where(lo[None, :] <= blocks[:, None], blocks[None, :], 0), axis=1)
    return first, lo.astype(I32), hi.astype(I32)


def local(
    tokens, grad_out, target, lengths, attn_gain, ffn_gain, q_gain, k_gain,
    w_query, key_matrix, value_matrix, w_out, w_gate, w_up, w_down,
):
    col = lax.axis_index("col")
    first, lo, hi = layout(lengths[0])
    mine = lax.dynamic_slice(first, (col * ROWS,), (ROWS,))
    pos = (col * ROWS + jnp.arange(ROWS, dtype=I32) - mine).astype(F32)
    freq = ROPE_BASE ** (-jnp.arange(HEAD // 2, dtype=F32) * 2.0 / HEAD)
    angles = pos[:, None] * freq[None, :]
    cos, sin = jnp.cos(angles), jnp.sin(angles)
    cos = jnp.concatenate([cos, cos], axis=1)
    sin = jnp.concatenate([-sin, sin], axis=1)
    first2 = first.reshape(NC, 1, ROWS)
    first2 = jnp.concatenate([first2, first2], axis=2)
    again, fgain = attn_gain.reshape(1, WIDTH), ffn_gain.reshape(1, WIDTH)
    qgain, kgain = q_gain.reshape(1, HEAD), k_gain.reshape(1, HEAD)

    w_kv = jnp.concatenate([key_matrix, value_matrix], axis=1)
    tok, grd, slt, wq, wkv, wo = dispatch(target, tokens, grad_out, [w_query, w_kv, w_out.T])
    wg, wu, wd = gather([w_gate, w_up, w_down.T], 2, "gather_ffn")
    qkv, raw, x, dy, n1h, dyh = project(
        slt, tok, grd, again, qgain, kgain, cos, sin, wq, wkv
    )
    qkv = col_swap(qkv, 3, "swap_qkv")
    o, o_t, lse = attend(lo, qkv, first2)
    oa = col_swap(o, 4, "swap_o")
    out_s, dh, dhlh, n2h, act, d_o, gain_f = middle(slt, x, dy, oa, fgain, wo, wg, wu, wd)
    g_o, got_out, act_m, oa_m, n2_m, dy_m, dhl_m = back_swap(
        d_o, out_s, act, oa, n2h, dyh, dhlh
    )
    parts = ffn_grads(n2h, n2_m, dyh, dy_m, act, act_m)
    r_gate, r_up, r_down = scatter(parts, 6, "scatter_ffn")
    dqkv = attend_back(hi, qkv, first2, g_o, o_t, lse)
    dqkv = col_swap(dqkv, 9, "swap_dqkv")
    draw, dx_s, gain_a, gain_qk = project_back(
        slt, x, dh, again, qgain, kgain, cos, sin, raw, dqkv, wq, wkv
    )
    draw_m, n1_m = core_swap(draw, n1h)
    parts = attn_grads(n1h, n1_m, dhlh, dhl_m, draw, draw_m, oa, oa_m)
    gains = jnp.concatenate([gain_a, gain_f, gain_qk, jnp.zeros((1, 768), F32)], axis=1)
    r_q, r_kv, r_o, got_dx, gains = last(parts, dx_s, gains.reshape(24, HEAD))
    output, input_grad = arrive(target, got_out, got_dx)
    gains = gains.reshape(-1)
    return (
        output,
        input_grad,
        gains[0:1024],
        gains[1024:2048],
        gains[2048:2176],
        gains[2176:2304],
        r_q,
        r_kv[:, :HEAD],
        r_kv[:, HEAD:],
        r_o.T,
        r_gate,
        r_up,
        r_down.T,
    )


def solution(mesh):
    both = P(("row", "col"), None)
    by_row, by_col = P("row", "col"), P("col", "row")
    weights = (by_row, by_row, by_row, by_col, by_row, by_row, by_col)
    return jax.shard_map(
        local,
        mesh=mesh,
        in_specs=(both, both, P(("row", "col")), P("row", None), P(), P(), P(), P()) + weights,
        out_specs=(both, both, P(), P(), P(), P()) + weights,
        check_vma=False,
    )
```

time: 1340 us -> 477 us (0.36)
  waiting for transfers between devices: 682 us -> 0 us
  Pallas kernels: 0 us -> 458 us
  blocking collectives: 359 us -> 0 us
  matrix products: 144 us -> 0 us
  other arithmetic: 69.7 us -> 7.52 us
  local copies, waits for them, and re-layouts: 35.4 us -> 10.4 us
  starting transfers between devices: 22.9 us -> 0 us
  between operations: 16 us -> 0.81 us
    reduce_scatter x11 -> x0, waiting for transfers between devices: 610 us -> none  [the longest x1 67.3 us: local(): lax.psum_scatter(grad_gate.astype(jnp.bfloat16), 'row', scatter_dimension...]
    pallas_call x0 -> x17, Pallas kernels: none -> 458 us  [the longest x3 79.8 us: col_swap(): pl.pallas_call(col_swap_kernel, name=name, out_shape=sds(src.shape), in_s...]
    all_gather x7 -> x0, blocking collectives: 239 us -> none  [the longest x1 63.4 us: local(): lax.all_gather(w_gate, 'row', axis=0, tiled=True)]
    dot_general x45 -> x0, matrix products: 144 us -> none  [the longest x4 13.5 us: attend_back(): jnp.einsum('qcrd,kcd->crqk', grad_part, value_heads_rows[:block_stop], pr...]
    psum x1 -> x0, blocking collectives: 64.5 us -> none  [local(): lax.psum((grad_attn_gain, grad_ffn_gain, grad_q_gain, grad_k_gain), ('row...]
    all_to_all x1 -> x0, blocking collectives: 55.8 us -> none  [local(): lax.all_to_all(sent_grads, 'row', split_axis=0, concat_axis=0, tiled=True)]
    all_gather x4 -> x0, waiting for transfers between devices: 51.5 us -> none  [the longest x1 51.5 us: local(): lax.all_gather(grad_middle.astype(jnp.bfloat16), 'col', axis=0, tiled=True)]
    all_to_all x4 -> x0, starting transfers between devices: 21.8 us -> none  [the longest x1 7.97 us: local(): lax.all_to_all(sent_slots, 'row', split_axis=0, concat_axis=0, tiled=True)]
  transfers between devices with their start and end apart: 19 -> 0, of which waited for: 15 -> 0; matrix products, arithmetic and copies ran while one was open for 7% -> 0% of each run, Pallas kernels for 0% -> 0%
where the time goes in v1:
time: 477 us; the launch traced here: 476 us
  Pallas kernels  458 us (96%)
  local copies, waits for them, and re-layouts  10.4 us (2%)
  other arithmetic  7.52 us (2%)
    pallas_call x3, Pallas kernels, col_swap(): pl.pallas_call(col_swap_kernel, name=name, out_shape=sds(src.shape), in_s...  79.8 us
    pallas_call x1, Pallas kernels, dispatch(): pl.pallas_call(dispatch_kernel, name='dispatch', out_shape=[sds((NR, 16,...  63.4 us
    pallas_call x1, Pallas kernels, gather(): pl.pallas_call(gather_kernel, name=name, out_shape=[gather_shape(w)] * 3,...  62 us
    pallas_call x1, Pallas kernels, last(): pl.pallas_call(last_kernel, name='last', out_shape=[sds((64, w), F32)] *...  58.7 us
    pallas_call x1, Pallas kernels, scatter(): pl.pallas_call(functools.partial(scatter_kernel, w), name=name, out_shape...  50.8 us
    pallas_call x1, Pallas kernels, middle(): pl.pallas_call(middle_kernel, name='middle', grid=(3 * NC,), out_shape=[s...  33.5 us
    pallas_call x1, Pallas kernels, back_swap(): pl.pallas_call(back_swap_kernel, name='back_swap', out_shape=[sds(d_o.sha...  23.5 us
    pallas_call x1, Pallas kernels, attend_back(): pl.pallas_call(attend_back_kernel, name='attend_back', grid_spec=pltpu.Pr...  16.2 us

profile of v1, /device:TPU:0, one launch (start us, length us, event | category | flops | bytes accessed | tf_op | source)
XLA Modules:
  0.0 476.4 jit_solution(9174176104875991433)
XLA Ops:
  3.7 1.5 copy.31.t_col
  5.2 1.4 pad_maximum_fusion.2.l1
  6.6 63.4 %dispatch.1 = (bf16[16,16,1024]{2,1,0:T(8,128)(2,1)}, bf16[16,16,1024]{2,1,0:T(8,128)(2,1)}, s32[16,16,128]{2,1,0:T(8,128)}, bf16[4,2,4,2,2,64,256]{6,5,4,3,2,1,...) custom-call(s32[1,256]{1,0:T(1,128)} %bitcast.33, ...), custom_call_target="tpu_custom_call" | custom-call | tf_op jit(solution)/shard_map/dispatch/pallas_call | solution.py:546
  70.0 11.8 %project.1 = (bf16[8,256,512]{2,1,0:T(8,128)(2,1)}, f32[8,256,384]{2,1,0:T(8,128)}, bf16[256,1024]{1,0:T(8,128)(2,1)}, bf16[256,1024]{1,0:T(8,128)(2,1)}, bf16[2...) custom-call(s32[16,16,128]{2,1,0:T(8,128)} %get-tuple-element.67.slt, bf16[16,16,1024]{2,1,0:T(8,128)(2,1)} %get-tuple-element.68.tok, ...), custom_call_target="tpu_custom_call" | custom-call | tf_op jit(solution)/shard_map/project/pallas_call | solution.py:616
  81.7 36.2 %swap_qkv.1.qkv = bf16[8,256,512]{2,1,0:T(8,128)(2,1)} custom-call(bf16[8,256,512]{2,1,0:T(8,128)(2,1)} %get-tuple-element.74.src), custom_call_target="tpu_custom_call" | custom-call | tf_op jit(solution)/shard_map/swap_qkv/pallas_call | solution.py:480
  119.1 13.2 %attend.1 = (bf16[8,256,256]{2,1,0:T(8,128)(2,1)}, f32[8,128,512]{2,1,0:T(8,128)}, f32[8,1,512]{2,1,0:T(1,128)}) custom-call(s32[8]{0:T(128)} %and_select_fusion.lo, bf16[8,256,512]{2,1,0:T(8,128)(2,1)} %swap_qkv.1.qkv, s32[8,1,512]{2,1,0:T(1,128)} %pad_add_fusion.first), custom_call_target="tpu_custom_call" | custom-call | tf_op jit(solution)/shard_map/attend/pallas_call | solution.py:703
  132.3 15.9 %swap_o.1.oa = bf16[8,256,256]{2,1,0:T(8,128)(2,1)} custom-call(bf16[8,256,256]{2,1,0:T(8,128)(2,1)} %get-tuple-element.75.src), custom_call_target="tpu_custom_call" | custom-call | tf_op jit(solution)/shard_map/swap_o/pallas_call | solution.py:480
  148.2 62.0 %gather_ffn.1 = (bf16[4,2,4,2,2,64,384]{6,5,4,3,2,1,0:T(8,128)(2,1)}, bf16[4,2,4,2,2,64,384]{6,5,4,3,2,1,0:T(8,128)(2,1)}, bf16[4,2,4,2,2,64,384]{6,5,4,3,2,1,0:T(8,128)(2,1)}) custom-call(bf16[64,384]{1,0:T(8,128)(2,1)} %l0.3, bf16[64,384]{1,0:T(8,128)(2,1)} %l1.1, bf16[64,384]{1,0:T(8,128)(2,1)} %bitcast.27), custom_call_target="tpu_custom_call" | custom-call | tf_op jit(solution)/shard_map/gather_ffn/pallas_call | solution.py:206
  210.2 33.5 %middle.1 = (bf16[16,16,1024]{2,1,0:T(8,128)(2,1)}, f32[256,1024]{1,0:T(8,128)}, bf16[2,256,512]{2,1,0:T(8,128)(2,1)}, bf16[2,256,512]{2,1,0:T(8,128)(2,1)}, bf1...) custom-call(s32[16,16,128]{2,1,0:T(8,128)} %get-tuple-element.67.slt, ...), custom_call_target="tpu_custom_call" | custom-call | tf_op jit(solution)/shard_map/middle/pallas_call | solution.py:878
  243.7 23.5 %back_swap.1 = (bf16[8,256,256]{2,1,0:T(8,128)(2,1)}, bf16[16,16,1024]{2,1,0:T(8,128)(2,1)}, bf16[8,256,1152]{2,1,0:T(8,128)(2,1)}, bf16[8,256,256]{2,1,0:T(8,12...) custom-call(bf16[8,256,256]{2,1,0:T(8,128)(2,1)} %get-tuple-element.80.d_o, ...), custom_call_target="tpu_custom_call" | custom-call | tf_op jit(solution)/shard_map/back_swap/pallas_call | solution.py:947
  267.2 12.2 %ffn_grads.1 = (bf16[4,2,4,2,64,384]{5,4,3,2,1,0:T(8,128)(2,1)}, bf16[4,2,4,2,64,384]{5,4,3,2,1,0:T(8,128)(2,1)}, bf16[4,2,4,2,64,384]{5,4,3,2,1,0:T(8,128)(2,1)}) custom-call(bf16[2,256,512]{2,1,0:T(8,128)(2,1)} %get-tuple-element.83.n2h, bf16[256,512]{1,0:T(8,128)(2,1)} %get-tuple-element.112.n2_m, bf16[2,256,512]{2,1,0:T(8,128)(2,1)} %get-tuple-element.84.dyh, ...), custom_call_target="tpu_custom_call" | custom-call | tf_op jit(solution)/shard_map/ffn_grads/pallas_call | solution.py:985
  279.4 50.8 %scatter_ffn.1 = (f32[64,384]{1,0:T(8,128)}, f32[64,384]{1,0:T(8,128)}, f32[64,384]{1,0:T(8,128)}) custom-call(bf16[4,2,4,2,64,384]{5,4,3,2,1,0:T(8,128)(2,1)} %get-tuple-element.115.p0, bf16[4,2,4,2,64,384]{5,4,3,2,1,0:T(8,128)(2,1)} %get-tuple-element.116.p1, bf16[4,2,4,2,64,384]{5,4,3,2,1,0:T(8,128)(2,1)} %get-tuple-element.117.p2), custom_call_target="tpu_custom_call" | custom-call | tf_op jit(solution)/shard_map/scatter_ffn/pallas_call | solution.py:434
  330.9 16.2 %attend_back.1.src = bf16[8,256,512]{2,1,0:T(8,128)(2,1)} custom-call(s32[8]{0:T(128)} %select_reduce_fusion.1.hi, bf16[8,256,512]{2,1,0:T(8,128)(2,1)} %swap_qkv.1.qkv, s32[8,1,512]{2,1,0:T(1,128)} %pad_add_fusion.first, bf16[8,256,256]{2,1,0:T(8,128)(2,1)} %get-tuple-element.90.d_o, f32[8,128,512]{2,1,0:T(8,128)} %get-tuple-element.91.o_t, ...), custom_call_target="tpu_custom_call" | custom-call | tf_op jit(solution)/shard_map/attend_back/pallas_call | solution.py:768
  347.1 27.7 %swap_dqkv.1.dqkv = bf16[8,256,512]{2,1,0:T(8,128)(2,1)} custom-call(bf16[8,256,512]{2,1,0:T(8,128)(2,1)} %attend_back.1.src), custom_call_target="tpu_custom_call" | custom-call | tf_op jit(solution)/shard_map/swap_dqkv/pallas_call | solution.py:480
  374.9 14.8 %project_back.1 = (bf16[8,256,512]{2,1,0:T(8,128)(2,1)}, bf16[16,16,1024]{2,1,0:T(8,128)(2,1)}, f32[1,1024]{1,0:T(1,128)}, f32[1,256]{1,0:T(1,128)}) custom-call(s32[16,16,128]{2,1,0:T(8,128)} %get-tuple-element.67.slt, bf16[256,1024]{1,0:T(8,128)(2,1)} %get-tuple-element.72.x, f32[256,1024]{1,0:T(8,128)} %get-tuple-element.88.dh, f32[1,1024]{1,0:T(1,128)} %bitcast.31, ...), custom_call_target="tpu_custom_call" | custom-call | tf_op jit(solution)/shard_map/project_back/pallas_call | solution.py:1073
  389.7 1.3 maximum_maximum_fusion
  391.0 4.9 %core_swap.1 = (bf16[8,256,512]{2,1,0:T(8,128)(2,1)}, bf16[256,512]{1,0:T(8,128)(2,1)}) custom-call(bf16[8,256,512]{2,1,0:T(8,128)(2,1)} %get-tuple-element.93.dqkv, bf16[2,256,512]{2,1,0:T(8,128)(2,1)} %get-tuple-element.87.n1h), custom_call_target="tpu_custom_call" | custom-call | tf_op jit(solution)/shard_map/core_swap/pallas_call | solution.py:1127
  395.9 10.0 %attn_grads.1 = (bf16[4,2,4,2,64,256]{5,4,3,2,1,0:T(8,128)(2,1)}, bf16[4,2,4,2,64,256]{5,4,3,2,1,0:T(8,128)(2,1)}, bf16[4,2,4,2,64,256]{5,4,3,2,1,0:T(8,128)(2,1)}) custom-call(bf16[2,256,512]{2,1,0:T(8,128)(2,1)} %get-tuple-element.87.n1h, bf16[256,512]{1,0:T(8,128)(2,1)} %get-tuple-element.94.n1_m, bf16[2,256,512]{2,1,0:T(8,128)(2,1)} %get-tuple-element.85.dhlh, ...), custom_call_target="tpu_custom_call" | custom-call | tf_op jit(solution)/shard_map/attn_grads/pallas_call | solution.py:1018
  406.0 58.7 %last.1 = (f32[64,256]{1,0:T(8,128)}, f32[64,256]{1,0:T(8,128)}, f32[64,256]{1,0:T(8,128)}, bf16[16,16,1024]{2,1,0:T(8,128)(2,1)}, f32[24,128]{1,0:T(8,128)}) custom-call(bf16[4,2,4,2,64,256]{5,4,3,2,1,0:T(8,128)(2,1)} %get-tuple-element.98.p0, bf16[4,2,4,2,64,256]{5,4,3,2,1,0:T(8,128)(2,1)} %get-tuple-element.99.p1, ...), custom_call_target="tpu_custom_call" | custom-call | tf_op jit(solution)/shard_map/last/pallas_call | solution.py:1175
  464.6 2.9 arrive.1
  467.5 1.4 fusion.1
  468.9 1.3 slice_bitcast_fusion
  471.5 1.5 copy.37
  472.9 1.5 copy.38
  (27 shorter events, 8.2 us)
Async XLA Ops:
  279.4 50.8 %copy-start.4 = (s32[8]{0:T(128)S(1)}, s32[8]{0:T(128)}, u32[]{:S(2)}) copy-start(s32[8]{0:T(128)} %and_select_fusion.lo) | copy-start | bytes 100
  374.9 14.8 %copy-start.3 = (f32[1,1024]{1,0:T(1,128)S(1)}, f32[1,1024]{1,0:T(1,128)}, u32[]{:S(2)}) copy-start(f32[1,1024]{1,0:T(1,128)} %get-tuple-element.103) | copy-start | bytes 12292
  405.9 68.5 %copy-start.2 = (f32[64,384]{1,0:T(8,128)S(1)}, f32[64,384]{1,0:T(8,128)}, u32[]{:S(2)}) copy-start(f32[64,384]{1,0:T(8,128)} %get-tuple-element.155) | copy-start | bytes 294916
  405.9 69.1 %copy-start.1 = (f32[64,384]{1,0:T(8,128)S(1)}, f32[64,384]{1,0:T(8,128)}, u32[]{:S(2)}) copy-start(f32[64,384]{1,0:T(8,128)} %get-tuple-element.156) | copy-start | bytes 294916
  405.9 69.8 %copy-start = (f32[64,384]{1,0:T(8,128)S(1)}, f32[64,384]{1,0:T(8,128)}, u32[]{:S(2)}) copy-start(f32[64,384]{1,0:T(8,128)} %get-tuple-element.120) | copy-start | bytes 294916

commit v2 on v1

--- a/solution.py
+++ b/solution.py
@@ -3,6 +3,7 @@
 
 import jax
 import jax.numpy as jnp
+import numpy as np
 from jax import lax
 from jax.experimental import pallas as pl
 from jax.experimental.pallas import tpu as pltpu
@@ -99,119 +100,154 @@
     return idx if with_core is None else idx + (with_core,)
 
 
-def gather_phases(at, locs, outs, sems, late):
-    ssem, rsem, msem, nsem = sems
-    k = at["k"]
-    waits = []
-
-    def region(s, t, pos):
-        order = ORDERS[s]
-        sel = {a: at[a] for a in order[t + 1 :]}
-        sel[order[t]] = pos
-        return block_index(sel, k)
-
-    n = len(locs)
-    half = locs[0].shape[0] // 2
-    for t in range(3):
-        firsts = []
-        for s in range(n):
-            a = ORDERS[s][t]
-            p = at[a]
-            here = outs[s].at[region(s, t, p)]
-            src = locs[s] if t == 0 else here
-            pair = []
-            for d, step in enumerate((1, -1)):
-                cp = remote(
-                    src, here, ssem.at[s, t, d], rsem.at[s, t, d], device(moved(at, a, step))
+SHIFT = (0, -1, 1, 2)
+
+
+def piece_index(at, s, t, g, rel):
+    order = ORDERS[s]
+    sel = {a: at[a] for a in order[t + 1 :]}
+    if t > 0 and g is not None:
+        sel[order[t - 1]] = (at[order[t - 1]] + SHIFT[g]) % 4
+    sel[order[t]] = (at[order[t]] + rel) % 4
+    return block_index(sel, at["k"])
+
+
+class Gather:
+    def __init__(self, at, outs, sems):
+        self.at, self.outs = at, outs
+        self.ssem, self.rsem, self.msem, self.nsem = sems
+        self.n = len(outs)
+        self.half = outs[0].shape[5] // 2
+        self.late, self.sent = [], []
+
+    def copies(self, s, t, g):
+        ref = self.outs[s].at[piece_index(self.at, s, t, g, 0)]
+        a, i = ORDERS[s][t], t * 4 + (g or 0)
+        return [
+            remote(ref, ref, self.ssem.at[s, i, d], self.rsem.at[s, i, d], device(moved(self.at, a, step)))
+            for d, step in enumerate((1, -1))
+        ]
+
+    def forwards(self, s, t, g):
+        a, i = ORDERS[s][t], t * 4 + (g or 0)
+        out = []
+        for d, step in enumerate((1, -1)):
+            came = piece_index(self.at, s, t, g, -step) + (pl.ds(d * self.half, self.half),)
+            ref = self.outs[s].at[came]
+            out.append(
+                remote(
+                    ref,
+                    ref,
+                    self.ssem.at[s, i, 2 + d],
+                    self.rsem.at[s, i, 2 + d],
+                    device(moved(self.at, a, step)),
                 )
+            )
+        return out
+
+    def to_mate(self, s, g, rel):
+        slot = 4 * (g or 0) + SHIFT.index(rel)
+        ref = self.outs[s].at[piece_index(self.at, s, 2, g, rel)]
+        return remote(ref, ref, self.msem.at[s, slot], self.nsem.at[s, slot], device(mate(self.at)))
+
+    def share(self, s, g, rel):
+        cp = self.to_mate(s, g, rel)
+        cp.start()
+        self.late.append(cp)
+
+    def send(self, t, g):
+        for s in range(self.n):
+            for cp in self.copies(s, t, g):
                 cp.start()
-                pair.append(cp)
+                self.sent.append(cp)
             if t == 2:
-                cp = remote(here, here, msem.at[s, 0], nsem.at[s, 0], device(mate(at)))
+                self.share(s, g, 0)
+
+    def pass_on(self, t, g):
+        for s in range(self.n):
+            first = self.copies(s, t, g)
+            for d, cp in enumerate(self.forwards(s, t, g)):
+                first[d].wait_recv()
                 cp.start()
-                late.append(cp)
-            firsts.append(pair)
-        seconds = []
-        for s in range(n):
-            a = ORDERS[s][t]
-            p = at[a]
-            pair = []
-            for d, step in enumerate((1, -1)):
-                firsts[s][d].wait_recv()
-                came = region(s, t, (p - step) % 4)
-                rows = pl.ds(d * half, half)
-                cp = remote(
-                    outs[s].at[came + (rows,)],
-                    outs[s].at[came + (rows,)],
-                    ssem.at[s, t, 2 + d],
-                    rsem.at[s, t, 2 + d],
-                    device(moved(at, a, step)),
-                )
-                cp.start()
-                pair.append(cp)
+                self.sent.append(cp)
                 if t == 2:
-                    ref = outs[s].at[came]
-                    cp = remote(ref, ref, msem.at[s, 1 + d], nsem.at[s, 1 + d], device(mate(at)))
-                    cp.start()
-                    late.append(cp)
-            seconds.append(pair)
-        for s in range(n):
-            for cp in seconds[s]:
+                    self.share(s, g, (-1, 1)[d])
+
+    def arrived(self, t, g):
+        for s in range(self.n):
+            for cp in self.forwards(s, t, g):
                 cp.wait_recv()
             if t == 2:
-                p = at[ORDERS[s][t]]
-                ref = outs[s].at[region(s, t, (p + 2) % 4)]
-                cp = remote(ref, ref, msem.at[s, 3], nsem.at[s, 3], device(mate(at)))
-                cp.start()
-                late.append(cp)
-        waits += [c for pair in firsts + seconds for c in pair]
-    return waits
+                self.share(s, g, 2)
+
+    def drain(self):
+        for cp in self.late:
+            cp.wait()
+        for cp in self.sent:
+            cp.wait_send()
+
+    def lines(self):
+        self.send(0, None)
+        self.send(1, 0)
+        yield
+        self.pass_on(0, None)
+        self.send(1, 1)
+        self.send(1, 2)
+        yield
+        self.pass_on(1, 0)
+        self.arrived(0, None)
+        self.send(1, 3)
+        yield
+        self.pass_on(1, 1)
+        self.pass_on(1, 2)
+        self.pass_on(1, 3)
+        yield
+        for g in range(4):
+            self.arrived(1, g)
+
+    def all(self):
+        self.send(0, None)
+        self.send(1, 0)
+        yield
+        self.pass_on(0, None)
+        self.send(1, 1)
+        self.send(1, 2)
+        yield
+        self.pass_on(1, 0)
+        self.arrived(0, None)
+        self.send(1, 3)
+        self.send(2, 0)
+        yield
+        self.pass_on(1, 1)
+        self.pass_on(1, 2)
+        self.pass_on(1, 3)
+        self.send(2, 1)
+        self.send(2, 2)
+        yield
+        self.pass_on(2, 0)
+        for g in range(4):
+            self.arrived(1, g)
+        self.send(2, 3)
+        yield
+        self.pass_on(2, 1)
+        self.pass_on(2, 2)
+        yield
+        self.pass_on(2, 3)
+        yield
+        for g in range(4):
+            self.arrived(2, g)
 
 
 def gather_sems(n=3):
-    return [DMA((n, 3, 4)), DMA((n, 3, 4)), DMA((n, 4)), DMA((n, 4)), DMA((n,))]
+    return [DMA((n, 12, 4)), DMA((n, 12, 4)), DMA((n, 16)), DMA((n, 16))]
+
+
+def plane_sems(n=3):
+    return gather_sems(n)
 
 
 def gather_shape(w):
     return sds((4, 2, 4, 2, 2, 64, w))
-
-
-def run_gather(at, locs, outs, sems):
-    ssem, rsem, msem, nsem, lsem = sems
-    own = []
-    for s in range(len(locs)):
-        cp = pltpu.make_async_copy(
-            locs[s], outs[s].at[block_index({a: at[a] for a in "xyz"}, at["k"])], lsem.at[s]
-        )
-        cp.start()
-        own.append(cp)
-    for cp in own:
-        cp.wait()
-    late = []
-    waits = gather_phases(at, locs, outs, (ssem, rsem, msem, nsem), late)
-    for cp in late:
-        cp.wait()
-    for cp in waits:
-        cp.wait_send()
-
-
-def gather_kernel(l0, l1, l2, g0, g1, g2, *sems):
-    at = where_am_i()
-    meet(ring_peers(at) + [device(mate(at))])
-    run_gather(at, (l0, l1, l2), (g0, g1, g2), sems)
-
-
-def gather(blocks, cid, name):
-    w = blocks[0].shape[1]
-    return pl.pallas_call(
-        gather_kernel,
-        name=name,
-        out_shape=[gather_shape(w)] * 3,
-        in_specs=[HBM] * 3,
-        out_specs=[HBM] * 3,
-        scratch_shapes=gather_sems(),
-        compiler_params=params(cid),
-    )(*blocks)
 
 
 def lead_shape(axes):
@@ -267,179 +303,158 @@
             one(i)
 
 
-def scatter_buffers(w, n=3):
+def scatter_leads(s, t):
+    return lead_shape(ORDERS[s][: 2 - t])
+
+
+def scatter_buffers(w, t0=0, n=3):
     out = []
     for s in range(n):
-        for t in range(3):
-            lead = lead_shape(ORDERS[s][: 2 - t])
+        for t in range(t0, 3):
+            lead = scatter_leads(s, t)
             out.append(pltpu.VMEM((2,) + lead + (32, w), BF))
             out.append(pltpu.VMEM((2,) + lead + (64, w), BF))
             out.append(pltpu.VMEM((2,) + lead + (32, w), BF))
-            if t == 0:
-                out.append(pltpu.VMEM(lead + (64, w), BF))
-            elif t == 1:
-                out.append(pltpu.VMEM(lead + (64, w), BF))
+            out.append(pltpu.VMEM(lead + (64, w), BF))
     return out
-
-
-PER_STREAM = 11
 
 
 def scatter_sems(n=3):
     return [DMA((n, 3, 6)), DMA((n, 3, 6)), DMA((n, 3))]
 
 
-def run_scatter(at, parts, results, bufs, sems):
+LO, HI = pl.ds(0, 32), pl.ds(32, 32)
+
+
+def part_of(s, t, at, rel, rows):
+    a = ORDERS[s][2 - t]
+    return sub_index({a: (at[a] + rel) % 4}, ORDERS[s][: 3 - t]) + (rows,)
+
+
+def first_sends(s, t, at, ref, rel_in, piece_in, ssem, rsem):
+    a = ORDERS[s][2 - t]
+    right, left = device(moved(at, a, 1)), device(moved(at, a, -1))
+    allr = (slice(None),) * len(scatter_leads(s, t))
+
+    def src(rel, rows):
+        return ref.at[part_of(s, t, at, rel, rows)]
+
+    return [
+        remote(src(2, LO), rel_in.at[0], ssem.at[s, t, 0], rsem.at[s, t, 0], right),
+        remote(src(2, HI), rel_in.at[1], ssem.at[s, t, 1], rsem.at[s, t, 1], left),
+        remote(
+            src(1, HI), piece_in.at[(0,) + allr + (HI,)], ssem.at[s, t, 2], rsem.at[s, t, 2], right
+        ),
+        remote(
+            src(-1, LO), piece_in.at[(1,) + allr + (LO,)], ssem.at[s, t, 3], rsem.at[s, t, 3], left
+        ),
+    ]
+
+
+def second_send(s, t, at, d, rel_out, piece_in, ssem, rsem):
+    a = ORDERS[s][2 - t]
+    allr = (slice(None),) * len(scatter_leads(s, t))
+    return remote(
+        rel_out.at[d],
+        piece_in.at[(d,) + allr + ((LO, HI)[d],)],
+        ssem.at[s, t, 4 + d],
+        rsem.at[s, t, 4 + d],
+        device(moved(at, a, (1, -1)[d])),
+    )
+
+
+def side(d):
+    return lambda j: (d,) + j
+
+
+def same(j):
+    return j
+
+
+def run_scatter(at, parts, results, bufs, sems, t0=0):
     ssem, rsem, lsem = sems
     n = len(parts)
-    cur = [(parts[s], "xyz") for s in range(n)]
+    cur = list(parts)
     waits = []
-    lo, hi = pl.ds(0, 32), pl.ds(32, 32)
-    for t in range(3):
+    per = 4 * (3 - t0)
+    for t in range(t0, 3):
         st = []
         for s in range(n):
-            b = bufs[s * PER_STREAM : (s + 1) * PER_STREAM]
-            rel_in, piece_in, rel_out = b[4 * t : 4 * t + 3]
-            total = b[4 * t + 3] if t < 2 else None
-            a = ORDERS[s][2 - t]
-            rem = ORDERS[s][: 2 - t]
-            ref, axes = cur[s]
-            p = at[a]
-
-            def src(pos, rows, ref=ref, axes=axes, a=a):
-                return ref.at[sub_index({a: pos % 4}, axes) + (rows,)]
-
-            right, left = device(moved(at, a, 1)), device(moved(at, a, -1))
-            allr = (slice(None),) * len(lead_shape(rem))
-            cps = [
-                remote(src(p + 2, lo), rel_in.at[0], ssem.at[s, t, 0], rsem.at[s, t, 0], right),
-                remote(src(p + 2, hi), rel_in.at[1], ssem.at[s, t, 1], rsem.at[s, t, 1], left),
-                remote(
-                    src(p + 1, hi),
-                    piece_in.at[(0,) + allr + (hi,)],
-                    ssem.at[s, t, 2],
-                    rsem.at[s, t, 2],
-                    right,
-                ),
-                remote(
-                    src(p - 1, lo),
-                    piece_in.at[(1,) + allr + (lo,)],
-                    ssem.at[s, t, 3],
-                    rsem.at[s, t, 3],
-                    left,
-                ),
-            ]
+            i = s * per + 4 * (t - t0)
+            rel_in, piece_in, rel_out, total = bufs[i : i + 4]
+            cps = first_sends(s, t, at, cur[s], rel_in, piece_in, ssem, rsem)
             for cp in cps:
                 cp.start()
             loads = []
-            if t == 0:
-                loads = [
-                    pltpu.make_async_copy(src(p + 1, lo), rel_out.at[0], lsem.at[s, 0]),
-                    pltpu.make_async_copy(src(p - 1, hi), rel_out.at[1], lsem.at[s, 1]),
-                    pltpu.make_async_copy(src(p, slice(None)), total, lsem.at[s, 2]),
-                ]
-                for cp in loads:
+            if t == t0:
+                for j, (rel, rows, dst) in enumerate(
+                    ((1, LO, rel_out.at[0]), (-1, HI, rel_out.at[1]), (0, slice(None), total))
+                ):
+                    cp = pltpu.make_async_copy(
+                        cur[s].at[part_of(s, t, at, rel, rows)], dst, lsem.at[s, j]
+                    )
                     cp.start()
-            st.append((rel_in, piece_in, rel_out, total, a, rem, right, left, cps, loads, allr))
+                    loads.append(cp)
+            st.append((rel_in, piece_in, rel_out, total, cps, loads))
+        yield
         for s in range(n):
-            rel_in, piece_in, rel_out, total, a, rem, right, left, cps, loads, allr = st[s]
-            ref, axes = cur[s]
-            lead = lead_shape(rem)
-            p = at[a]
-            for d, (rows, pos, to) in enumerate(((lo, p + 1, right), (hi, p - 1, left))):
+            rel_in, piece_in, rel_out, total, cps, loads = st[s]
+            lead = scatter_leads(s, t)
+            for d in range(2):
                 cps[d].wait_recv()
-                if t == 0:
+                if t == t0:
                     loads[d].wait()
-                    mine = (rel_out, lambda j, d=d: (d,) + j)
+                    mine = (rel_out, side(d))
                 else:
-
-                    def pick(j, pos=pos, rows=rows, axes=axes, a=a, rem=rem):
-                        it = iter(j)
-                        out = ()
-                        for q in ("x", "zl", "y", "zh"):
-                            if q[0] not in axes:
-                                continue
-                            if q[0] == a:
-                                z = pos % 4
-                                out += (z % 2 if q == "zl" else z // 2 if q == "zh" else z,)
-                            else:
-                                out += (next(it),)
-                        return out + (rows,)
-
-                    mine = (ref, pick)
-                add_blocks(
-                    lead,
-                    (rel_out, lambda j, d=d: (d,) + j),
-                    [mine, (rel_in, lambda j, d=d: (d,) + j)],
-                )
-                cp = remote(
-                    rel_out.at[d],
-                    piece_in.at[(d,) + allr + (rows,)],
-                    ssem.at[s, t, 4 + d],
-                    rsem.at[s, t, 4 + d],
-                    to,
-                )
+                    mine = (cur[s], picker(s, t, at, (1, -1)[d], (LO, HI)[d]))
+                add_blocks(lead, (rel_out, side(d)), [mine, (rel_in, side(d))])
+                cp = second_send(s, t, at, d, rel_out, piece_in, ssem, rsem)
                 cp.start()
                 cps.append(cp)
+        yield
         for s in range(n):
-            rel_in, piece_in, rel_out, total, a, rem, right, left, cps, loads, allr = st[s]
-            ref, axes = cur[s]
-            lead = lead_shape(rem)
-            p = at[a]
+            rel_in, piece_in, rel_out, total, cps, loads = st[s]
+            lead = scatter_leads(s, t)
             for i in (2, 3, 4, 5):
                 cps[i].wait_recv()
-            if t == 0:
+            if t == t0:
                 loads[2].wait()
-                mine = (total, lambda j: j)
+                mine = (total, same)
             else:
-
-                def pick(j, pos=p, axes=axes, a=a):
-                    it = iter(j)
-                    out = ()
-                    for q in ("x", "zl", "y", "zh"):
-                        if q[0] not in axes:
-                            continue
-                        if q[0] == a:
-                            out += (pos % 2 if q == "zl" else pos // 2 if q == "zh" else pos,)
-                        else:
-                            out += (next(it),)
-                    return out
-
-                mine = (ref, pick)
-            dst = (total, lambda j: j) if t < 2 else (results[s], lambda j: (slice(None),) * 2)
-            add_blocks(
-                lead,
-                dst,
-                [
-                    mine,
-                    (piece_in, lambda j: (0,) + j),
-                    (piece_in, lambda j: (1,) + j),
-                ],
-            )
-            cur[s] = (total, rem)
+                mine = (cur[s], picker(s, t, at, 0, slice(None)))
+            dst = (total, same) if t < 2 else (results[s], lambda j: (slice(None),) * 2)
+            add_blocks(lead, dst, [mine, (piece_in, side(0)), (piece_in, side(1))])
+            cur[s] = total
             waits += cps
     for cp in waits:
         cp.wait_send()
 
 
-def scatter_kernel(w, p0, p1, p2, r0, r1, r2, *scratch):
-    at = where_am_i()
-    meet(ring_peers(at))
-    bufs, sems = scratch[: 3 * PER_STREAM], scratch[3 * PER_STREAM :]
-    run_scatter(at, (p0, p1, p2), (r0, r1, r2), bufs, sems)
-
-
-def scatter(parts, cid, name):
-    w = parts[0].shape[-1]
-    return pl.pallas_call(
-        functools.partial(scatter_kernel, w),
-        name=name,
-        out_shape=[sds((64, w), F32)] * 3,
-        in_specs=[HBM] * 3,
-        out_specs=[VMEM] * 3,
-        scratch_shapes=scatter_buffers(w) + scatter_sems(),
-        compiler_params=params(cid),
-    )(*parts)
+def picker(s, t, at, rel, rows):
+    a, axes = ORDERS[s][2 - t], ORDERS[s][: 3 - t]
+    pos = (at[a] + rel) % 4
+
+    def pick(j):
+        it = iter(j)
+        out = ()
+        for q in ("x", "zl", "y", "zh"):
+            if q[0] not in axes:
+                continue
+            if q[0] == a:
+                out += (pos % 2 if q == "zl" else pos // 2 if q == "zh" else pos,)
+            else:
+                out += (next(it),)
+        return out + (rows,)
+
+    return pick
+
+
+def in_turn(*steps):
+    live = list(steps)
+    while live:
+        for it in list(live):
+            if next(it, "end") == "end":
+                live.remove(it)
 
 
 def swap_over(axis, src, dst, ssem, rsem, lsem):
@@ -512,8 +527,14 @@
     return lax.rsqrt(jnp.mean(v * v, axis=-1, keepdims=True) + EPSILON)
 
 
-def slots_sent(target_row, target_col):
-    g_row, g_col = target_row // GROUP, target_col // GROUP
+def column(row):
+    eye = iota((ROWS, ROWS), 0) == iota((ROWS, ROWS), 1)
+    return jnp.sum(jnp.where(eye, row.astype(F32), 0.0), axis=1, keepdims=True).astype(I32)
+
+
+def slots_sent(target_row):
+    g_row = target_row // GROUP
+    g_col = column(g_row)
     same = g_row == g_col
     i0, i1 = iota((ROWS, ROWS), 0), iota((ROWS, ROWS), 1)
     before_row = jnp.sum((same & (i0 < i1)).astype(F32), axis=0, keepdims=True).astype(I32)
@@ -522,11 +543,34 @@
 
 
 def dispatch_kernel(
-    t_row, t_col, tokens, grads, l0, l1, l2, tok, grd, slt, g0, g1, g2, tok_s, grd_s, slt_s, *sems
+    t_row, tokens, grads, w_q, w_k, w_v, w_o, w_g, w_u, w_d,
+    tok, grd, slt, a0, a1, a2, f0, f1, f2,
+    tok_s, grd_s, slt_s, own_sem, *sems,
 ):
     at = where_am_i()
+    here = block_index({a: at[a] for a in "xyz"}, at["k"])
+    rows = (slice(None),)
+    own = [
+        (w_q, a0.at[here]),
+        (w_k, a1.at[here + rows + (pl.ds(0, HEAD),)]),
+        (w_v, a1.at[here + rows + (pl.ds(HEAD, HEAD),)]),
+        (w_o, a2.at[here]),
+        (w_g, f0.at[here]),
+        (w_u, f1.at[here]),
+        (w_d, f2.at[here]),
+    ]
+    own = [pltpu.make_async_copy(src, dst, own_sem.at[i]) for i, (src, dst) in enumerate(own)]
+    for cp in own:
+        cp.start()
     meet(ring_peers(at) + row_peers(at))
-    place, _ = slots_sent(t_row[...], t_col[...])
+    for cp in own:
+        cp.wait()
+    first = Gather(at, (a0, a1, a2), sems[9:13])
+    second = Gather(at, (f0, f1, f2), sems[13:17])
+    steps = first.all()
+    more = second.lines()
+    next(steps)
+    place, _ = slots_sent(t_row[...])
     sel = place == iota((ROWS, ROWS), 0)
     pick = onehot(sel)
     tok_s[...] = dot(pick, tokens[...]).astype(BF).reshape(tok_s.shape)
@@ -534,29 +578,37 @@
     slt_s[...] = jnp.broadcast_to(slot, (ROWS, HEAD)).astype(I32).reshape(slt_s.shape)
     cps = swap_over("row", tok_s, tok, *sems[0:3])
     cps += swap_over("row", slt_s, slt, *sems[6:9])
+    next(steps)
     grd_s[...] = dot(pick, grads[...]).astype(BF).reshape(grd_s.shape)
     cps += swap_over("row", grd_s, grd, *sems[3:6])
-    run_gather(at, (l0, l1, l2), (g0, g1, g2), sems[9:])
+    in_turn(steps, more)
     for cp in cps:
         cp.wait()
-
-
-def dispatch(target, tokens, grads, blocks):
-    w = blocks[0].shape[1]
+    first.drain()
+    second.drain()
+
+
+def dispatch(target, tokens, grads, w_q, w_k, w_v, w_o, w_g, w_u, w_d):
     return pl.pallas_call(
         dispatch_kernel,
         name="dispatch",
         out_shape=[sds((NR, 16, WIDTH))] * 2
         + [sds((NR, 16, HEAD), I32)]
-        + [gather_shape(w)] * 3,
-        in_specs=[VMEM] * 4 + [HBM] * 3,
-        out_specs=[HBM] * 6,
+        + [gather_shape(256)] * 3
+        + [gather_shape(384)] * 3,
+        in_specs=[VMEM] * 3 + [HBM] * 7,
+        out_specs=[HBM] * 9,
         scratch_shapes=[pltpu.VMEM((NR, 16, WIDTH), BF)] * 2
         + [pltpu.VMEM((NR, 16, HEAD), I32)]
+        + [DMA((7,))]
         + swap_sems("row") * 3
+        + gather_sems()
         + gather_sems(),
         compiler_params=params(1),
-    )(target.reshape(1, ROWS), target.reshape(ROWS, 1), tokens, grads, *blocks)
+    )(
+        target.reshape(1, ROWS), tokens, grads,
+        w_q, w_k, w_v, w_o, w_g, w_u, w_d,
+    )
 
 
 def halves_of(v):
@@ -569,13 +621,36 @@
     return jnp.concatenate(even, axis=1), jnp.concatenate(odd, axis=1)
 
 
+def first_slots(lens, slots):
+    start = jnp.int32(0)
+    out = jnp.zeros_like(slots)
+    for j in range(8):
+        out = jnp.where(slots >= start, start, out)
+        start = start + lens(j)
+    return out
+
+
 def project_kernel(
-    slt, tok, grd, again, qgain, kgain, cos, sin, wq, wkv, out, raw, x_o, dy_o, n1h, dyh, n1_s
+    lens, slt, tok, grd, again, qgain, kgain, freq, wq, wkv, i0, i1, i2,
+    out, raw, x_o, dy_o, n1h, dyh, cos, sin, f0, f1, f2, n1_s, *sems,
 ):
     c = pl.program_id(0)
+    at = where_am_i()
+    more = Gather(at, (f0, f1, f2), sems)
 
     @pl.when(c == 0)
     def _():
+        meet(ring_peers(at) + [device(mate(at))])
+        more.send(2, None)
+
+    @pl.when(c == 0)
+    def _():
+        slots = lax.axis_index("col") * ROWS + iota((ROWS, HEAD), 0)
+        pos = (slots - first_slots(lambda j: lens[0, j], slots)).astype(F32)
+        angle = pos * freq[...]
+        cos[...] = jnp.cos(angle)
+        sine = jnp.sin(angle)
+        sin[...] = jnp.where(iota((ROWS, HEAD), 1) < HEAD // 2, -sine, sine)
         local = slt[...].reshape(ROWS, HEAD)[:, :1] % ROWS
         put = onehot(local == iota((ROWS, ROWS), 1))
         x = dot(put, tok[...].reshape(ROWS, WIDTH), TN)
@@ -603,6 +678,12 @@
         out[0, :, i * HEAD : (i + 1) * HEAD] = n.astype(BF)
     out[0, :, 3 * HEAD :] = kv[:, HEAD:].astype(BF)
 
+    @pl.when(c == NC - 1)
+    def _():
+        for s in range(3):
+            for cp in more.copies(s, 2, None) + [more.to_mate(s, None, 0)]:
+                cp.wait()
+
 
 def slab(w):
     return pl.BlockSpec((1, 1, 4, 2, 2, 64, w), lambda c: (c % 4, c // 4, 0, 0, 0, 0, 0))
@@ -612,7 +693,8 @@
     return pl.BlockSpec(shape, lambda *_: (0,) * len(shape))
 
 
-def project(slt, tok, grd, again, qgain, kgain, cos, sin, wq, wkv):
+def project(lens, slt, tok, grd, again, qgain, kgain, wq, wkv, planes):
+    freq = ROPE_BASE ** (-(np.arange(HEAD) % (HEAD // 2)).astype(np.float32) * 2.0 / HEAD)
     return pl.pallas_call(
         project_kernel,
         name="project",
@@ -624,19 +706,23 @@
             sds((ROWS, WIDTH)),
             sds((2, ROWS, 512)),
             sds((2, ROWS, 512)),
-        ],
+            sds((ROWS, HEAD), F32),
+            sds((ROWS, HEAD), F32),
+        ]
+        + [gather_shape(384)] * 3,
         in_specs=[
+            pl.BlockSpec(memory_space=pltpu.SMEM),
             whole((NR, 16, HEAD)),
             whole((NR, 16, WIDTH)),
             whole((NR, 16, WIDTH)),
             whole((1, WIDTH)),
             whole((1, HEAD)),
             whole((1, HEAD)),
-            whole((ROWS, HEAD)),
-            whole((ROWS, HEAD)),
+            whole((1, HEAD)),
             slab(256),
             slab(256),
-        ],
+        ]
+        + [HBM] * 3,
         out_specs=[
             pl.BlockSpec((1, ROWS, 512), lambda c: (c, 0, 0)),
             pl.BlockSpec((1, ROWS, 384), lambda c: (c, 0, 0)),
@@ -644,10 +730,46 @@
             whole((ROWS, WIDTH)),
             whole((2, ROWS, 512)),
             whole((2, ROWS, 512)),
-        ],
-        scratch_shapes=[pltpu.VMEM((ROWS, WIDTH), BF)],
-        compiler_params=params(),
-    )(slt, tok, grd, again, qgain, kgain, cos, sin, wq, wkv)
+            whole((ROWS, HEAD)),
+            whole((ROWS, HEAD)),
+        ]
+        + [HBM] * 3,
+        input_output_aliases={10: 8, 11: 9, 12: 10},
+        scratch_shapes=[pltpu.VMEM((ROWS, WIDTH), BF)] + gather_sems(),
+        compiler_params=params(2),
+    )(
+        lens, slt, tok, grd, again, qgain, kgain,
+        jnp.asarray(freq.astype(np.float32).reshape(1, HEAD)), wq, wkv, *planes,
+    )
+
+
+def heads_kernel(src, i0, i1, i2, dst, f0, f1, f2, *sems):
+    at = where_am_i()
+    meet(ring_peers(at) + [device(mate(at))] + col_peers(at))
+    more = Gather(at, (f0, f1, f2), sems[3:])
+    cps = swap_over("col", src, dst, *sems[:3])
+    for s in range(3):
+        for d, cp in enumerate(more.forwards(s, 2, None)):
+            cp.start()
+            more.sent.append(cp)
+            more.share(s, None, (-1, 1)[d])
+    more.arrived(2, None)
+    for cp in cps:
+        cp.wait()
+    more.drain()
+
+
+def heads(src, planes):
+    return pl.pallas_call(
+        heads_kernel,
+        name="swap_qkv",
+        out_shape=[sds(src.shape)] + [gather_shape(384)] * 3,
+        in_specs=[HBM] * 4,
+        out_specs=[HBM] * 4,
+        input_output_aliases={1: 1, 2: 2, 3: 3},
+        scratch_shapes=swap_sems("col") + gather_sems(),
+        compiler_params=params(3),
+    )(src, *planes)
 
 
 LOG2E = math.log2(math.e)
@@ -656,6 +778,26 @@
 
 def stacked(v):
     return jnp.concatenate([v[:, :HEAD], v[:, HEAD : 2 * HEAD]], axis=0)
+
+
+def group_slots(i):
+    return i * ROWS + iota((1, QK), 1) % ROWS
+
+
+def first_block(lens, i):
+    start, out = jnp.int32(0), jnp.int32(0)
+    for j in range(8):
+        out = jnp.where(start <= i * ROWS, start, out)
+        start = start + lens[j]
+    return out // ROWS
+
+
+def last_block(lens, j):
+    end, out = jnp.int32(0), jnp.int32(GROUP)
+    for n in range(8):
+        end = end + lens[n]
+        out = jnp.where(end > (j + 1) * ROWS - 1, jnp.minimum(out, end), out)
+    return (out - 1) // ROWS
 
 
 def allowed(i, j, first):
@@ -664,11 +806,11 @@
     return (key <= query) & (key >= first)
 
 
-def attend_kernel(lo, qkv, first, out, o_t, lse):
+def attend_kernel(lens, qkv, out, o_t, lse):
     i = pl.program_id(0)
     scale = HEAD**-0.5 * LOG2E
     q = stacked(qkv[i, :, 0 : 2 * HEAD])
-    start = first[0]
+    start = first_slots(lambda j: lens[j], group_slots(i))
 
     def scores(j):
         s = dot(qkv[j, :, 2 * HEAD : 3 * HEAD], q, NT) * scale
@@ -691,7 +833,7 @@
         acc = acc * fade + dot(qkv[j, :, 3 * HEAD :], p.astype(BF), TN)
         return m2, total, acc
 
-    m, total, acc = lax.fori_loop(0, i - lo[i], step, (m, total, acc))
+    m, total, acc = lax.fori_loop(0, i - first_block(lens, i), step, (m, total, acc))
     o = acc / total
     o_t[0] = o
     lse[0] = m + jnp.log2(total)
@@ -699,7 +841,7 @@
     out[0] = jnp.concatenate([back[:ROWS], back[ROWS:]], axis=1).astype(BF)
 
 
-def attend(lo, qkv, first):
+def attend(lens, qkv):
     return pl.pallas_call(
         attend_kernel,
         name="attend",
@@ -708,7 +850,6 @@
             grid=(NC,),
             in_specs=[
                 pl.BlockSpec((NC, ROWS, 512), lambda i, lo: (0, 0, 0)),
-                pl.BlockSpec((1, 1, QK), lambda i, lo: (i, 0, 0)),
             ],
             out_specs=[
                 pl.BlockSpec((1, ROWS, 256), lambda i, lo: (i, 0, 0)),
@@ -722,10 +863,10 @@
             sds((NC, 1, QK), F32),
         ],
         compiler_params=params(),
-    )(lo, qkv, first)
-
-
-def attend_back_kernel(hi, qkv, first, d_o, o_t, lse, out, qs, dos, delta, dq):
+    )(lens, qkv)
+
+
+def attend_back_kernel(lens, qkv, d_o, o_t, lse, out, qs, dos, delta, dq, first):
     j = pl.program_id(0)
     scale = HEAD**-0.5
 
@@ -737,6 +878,7 @@
             dos[i] = g
             delta[i] = jnp.sum(g.astype(F32).T * o_t[i], axis=0, keepdims=True)
             dq[i] = jnp.zeros((HEAD, QK), F32)
+            first[i] = first_slots(lambda n: lens[n], group_slots(i))
 
     k = qkv[j, :, 2 * HEAD : 3 * HEAD]
     v = qkv[j, :, 3 * HEAD :]
@@ -753,7 +895,7 @@
         return dk, dv
 
     zero = jnp.zeros((ROWS, HEAD), F32)
-    dk, dv = lax.fori_loop(j, hi[j] + 1, step, (zero, zero))
+    dk, dv = lax.fori_loop(j, last_block(lens, j) + 1, step, (zero, zero))
     done = dq[j].T
     out[0, :, 0:HEAD] = done[:ROWS].astype(BF)
     out[0, :, HEAD : 2 * HEAD] = done[ROWS:].astype(BF)
@@ -761,7 +903,7 @@
     out[0, :, 3 * HEAD :] = dv.astype(BF)
 
 
-def attend_back(hi, qkv, first, d_o, o_t, lse):
+def attend_back(lens, qkv, d_o, o_t, lse):
     def full(shape):
         return pl.BlockSpec(shape, lambda j, hi: (0,) * len(shape))
 
@@ -773,7 +915,6 @@
             grid=(NC,),
             in_specs=[
                 full((NC, ROWS, 512)),
-                full((NC, 1, QK)),
                 full((NC, ROWS, 256)),
                 full((NC, HEAD, QK)),
                 full((NC, 1, QK)),
@@ -784,11 +925,12 @@
                 pltpu.VMEM((NC, QK, HEAD), BF),
                 pltpu.VMEM((NC, 1, QK), F32),
                 pltpu.VMEM((NC, HEAD, QK), F32),
+                pltpu.VMEM((NC, 1, QK), I32),
             ],
         ),
         out_shape=sds((NC, ROWS, 512)),
         compiler_params=params(),
-    )(hi, qkv, first, d_o, o_t, lse)
+    )(lens, qkv, d_o, o_t, lse)
 
 
 def middle_kernel(
@@ -1028,11 +1170,73 @@
     )(n1h, n1_m, dhlh, dhl_m, dqkv, dqkv_m, oa, oa_m)
 
 
+def later_shapes():
+    leads = [scatter_leads(s, 0) for s in range(3)]
+    return [sds((2,) + n + (32, 384)) for n in leads], [sds((2,) + n + (64, 384)) for n in leads]
+
+
+def heads_back_kernel(src, p0, p1, p2, dst, *rest):
+    rel_in, piece_in, sems = rest[0:3], rest[3:6], rest[6:]
+    at = where_am_i()
+    meet(ring_peers(at) + col_peers(at))
+    cps = swap_over("col", src, dst, *sems[:3])
+    for s, p in enumerate((p0, p1, p2)):
+        more = first_sends(s, 0, at, p, rel_in[s], piece_in[s], sems[3], sems[4])
+        for cp in more:
+            cp.start()
+        cps += more
+    for cp in cps:
+        cp.wait()
+
+
+def heads_back(src, parts):
+    rel, piece = later_shapes()
+    return pl.pallas_call(
+        heads_back_kernel,
+        name="swap_dqkv",
+        out_shape=[sds(src.shape)] + rel + piece,
+        in_specs=[HBM] * 4,
+        out_specs=[HBM] * 7,
+        scratch_shapes=swap_sems("col") + scatter_sems()[:2],
+        compiler_params=params(6),
+    )(src, *parts)
+
+
 def project_back_kernel(
-    slt, x, dh, again, qgain, kgain, cos, sin, raw, dqkv, wq, wkv,
-    d_o, dx_s, gain_o, qk_o, acc, gq, gk,
+    slt, x, dh, again, qgain, kgain, cos, sin, raw, dqkv, wq, wkv, p0, p1, p2, r0, r1, r2, i0, i1, i2,
+    d_o, dx_s, gain_o, qk_o, q0, q1, q2, acc, gq, gk, *rest,
 ):
     c = pl.program_id(0)
+    at = where_am_i()
+    rel_v, own_v, (ssem, rsem, lsem) = rest[0:3], rest[3:6], rest[6:]
+    parts, rel_in, piece_in = (p0, p1, p2), (r0, r1, r2), (q0, q1, q2)
+
+    def loads(s):
+        out = [pltpu.make_async_copy(rel_in[s], rel_v[s], lsem.at[s, 0])]
+        for d, (rel, rows) in enumerate(((1, LO), (-1, HI))):
+            src = parts[s].at[part_of(s, 0, at, rel, rows)]
+            out.append(pltpu.make_async_copy(src, own_v[s].at[d], lsem.at[s, 1 + d]))
+        return out
+
+    def sends(s):
+        return [second_send(s, 0, at, d, own_v[s], piece_in[s], ssem, rsem) for d in range(2)]
+
+    @pl.when(c == 0)
+    def _():
+        for s in range(3):
+            for cp in loads(s):
+                cp.start()
+        meet(ring_peers(at))
+
+    @pl.when(c == 1)
+    def _():
+        for s in range(3):
+            for cp in loads(s):
+                cp.wait()
+            lead = (2,) + scatter_leads(s, 0)
+            add_blocks(lead, (own_v[s], same), [(own_v[s], same), (rel_v[s], same)])
+            for cp in sends(s):
+                cp.start()
 
     @pl.when(c == 0)
     def _():
@@ -1067,9 +1271,12 @@
         take = onehot(local == iota((ROWS, ROWS), 1))
         dx_s[...] = dot(take, dx.astype(BF)).astype(BF).reshape(dx_s.shape)
         qk_o[...] = jnp.concatenate([gq[...], gk[...]], axis=1)
-
-
-def project_back(slt, x, dh, again, qgain, kgain, cos, sin, raw, dqkv, wq, wkv):
+        for s in range(3):
+            for cp in sends(s):
+                cp.wait()
+
+
+def project_back(slt, x, dh, again, qgain, kgain, cos, sin, raw, dqkv, wq, wkv, parts, rel, piece):
     return pl.pallas_call(
         project_back_kernel,
         name="project_back",
@@ -1079,7 +1286,8 @@
             sds((NR, 16, WIDTH)),
             sds((1, WIDTH), F32),
             sds((1, 2 * HEAD), F32),
-        ],
+        ]
+        + later_shapes()[1],
         in_specs=[
             whole((NR, 16, HEAD)),
             whole((ROWS, WIDTH)),
@@ -1093,24 +1301,40 @@
             pl.BlockSpec((1, ROWS, 512), lambda c: (c, 0, 0)),
             slab(256),
             slab(256),
-        ],
+        ]
+        + [HBM] * 9,
         out_specs=[
             pl.BlockSpec((1, ROWS, 512), lambda c: (c, 0, 0)),
             whole((NR, 16, WIDTH)),
             whole((1, WIDTH)),
             whole((1, 2 * HEAD)),
-        ],
+        ]
+        + [HBM] * 3,
+        input_output_aliases={18: 4, 19: 5, 20: 6},
         scratch_shapes=[
             pltpu.VMEM((ROWS, WIDTH), F32),
             pltpu.VMEM((1, HEAD), F32),
             pltpu.VMEM((1, HEAD), F32),
-        ],
-        compiler_params=params(),
-    )(slt, x, dh, again, qgain, kgain, cos, sin, raw, dqkv, wq, wkv)
-
-
-def core_swap_kernel(dqkv, n1h, dqkv_m, n1_m, ssem, rsem):
+        ]
+        + [pltpu.VMEM(r.shape, BF) for r in later_shapes()[0]] * 2
+        + scatter_sems(),
+        compiler_params=params(7),
+    )(slt, x, dh, again, qgain, kgain, cos, sin, raw, dqkv, wq, wkv, *parts, *rel, *piece)
+
+
+def core_swap_kernel(dqkv, n1h, p0, p1, p2, q0, q1, q2, dqkv_m, n1_m, s0, s1, s2, *rest):
+    own_v, piece_v, (ssem, rsem, lsem, osem) = rest[0:3], rest[3:6], rest[6:]
     at = where_am_i()
+    loads = []
+    for s, (p, q) in enumerate(((p0, q0), (p1, q1), (p2, q2))):
+        src = p.at[part_of(s, 0, at, 0, slice(None))]
+        pair = [
+            pltpu.make_async_copy(src, own_v[s], lsem.at[s, 0]),
+            pltpu.make_async_copy(q, piece_v[s], lsem.at[s, 1]),
+        ]
+        for cp in pair:
+            cp.start()
+        loads.append(pair)
     to = device(mate(at))
     meet([to])
     cps = [
@@ -1119,160 +1343,180 @@
     ]
     for cp in cps:
         cp.start()
+    for s, out in enumerate((s0, s1, s2)):
+        for cp in loads[s]:
+            cp.wait()
+        lead = scatter_leads(s, 0)
+        terms = [(own_v[s], same), (piece_v[s], side(0)), (piece_v[s], side(1))]
+        add_blocks(lead, (own_v[s], same), terms)
+        cp = pltpu.make_async_copy(own_v[s], out, osem.at[s])
+        cp.start()
+        cps.append(cp)
     for cp in cps:
         cp.wait()
 
 
-def core_swap(dqkv, n1h):
+def core_swap(dqkv, n1h, parts, piece):
+    sums = [sds(scatter_leads(s, 0) + (64, 384)) for s in range(3)]
     return pl.pallas_call(
         core_swap_kernel,
         name="core_swap",
-        out_shape=[sds(dqkv.shape), sds((ROWS, 512))],
-        in_specs=[HBM] * 2,
-        out_specs=[HBM] * 2,
-        scratch_shapes=[DMA((2,)), DMA((2,))],
-        compiler_params=params(7),
-    )(dqkv, n1h)
-
-
-def last_kernel(p0, p1, p2, dx_s, gains, r0, r1, r2, got, gsum, *scratch):
-    nb = 3 * PER_STREAM
-    bufs, rest = scratch[:nb], scratch[nb:]
-    room, ssem, rsem = rest[:3]
+        out_shape=[sds(dqkv.shape), sds((ROWS, 512))] + sums,
+        in_specs=[HBM] * 8,
+        out_specs=[HBM] * 5,
+        scratch_shapes=[pltpu.VMEM(r.shape, BF) for r in sums]
+        + [pltpu.VMEM(r.shape, BF) for r in later_shapes()[1]]
+        + [DMA((2,)), DMA((2,)), DMA((3, 2)), DMA((3,))],
+        compiler_params=params(8),
+    )(dqkv, n1h, *parts, *piece)
+
+
+def gain_steps(at, pieces, room, total, ssem, rsem):
+    p = at["x"]
+    lane = 0
+    for ref in pieces:
+        room[0, p, :, lane : lane + ref.shape[1]] = ref[...]
+        lane += ref.shape[1]
+    for t, a in enumerate("xyzk"):
+        p = at[a]
+        others = (1, 2, 3) if a != "k" else (1,)
+        if t > 0:
+            room[t, p] = total[...]
+        step = []
+        for d in others:
+            to = device(moved(at, a, d)) if a != "k" else device(mate(at))
+            sems = ssem.at[t, d - 1], rsem.at[t, d - 1]
+            cp = remote(room.at[t, p], room.at[t, p], *sems, to)
+            cp.start()
+            step.append(cp)
+        yield
+        for cp in step:
+            cp.wait()
+        acc = room[t, 0]
+        for j in range(1, len(others) + 1):
+            acc = acc + room[t, j]
+        total[...] = acc
+
+
+def last_kernel(
+    p0, p1, p2, s0, s1, s2, dx_s, ga, gf, gqk, r0, r1, r2, t0, t1, t2, got, gsum, *scratch
+):
+    na, nf = len(scatter_buffers(256)), len(scatter_buffers(384, 1))
+    bufs, more, rest = scratch[:na], scratch[na : na + nf], scratch[na + nf :]
     at = where_am_i()
     far = [device(moved(at, a, 2)) for a in "xyz"]
     meet(ring_peers(at) + far + row_peers(at))
-    cps = swap_over("row", dx_s, got, *rest[3:6])
-    gsum[...] = gains[...]
-    waits = []
-    for t, a in enumerate("xyz"):
-        p = at[a]
-        room[t, p] = gsum[...]
-        step = []
-        for d in (1, 2, 3):
-            cp = remote(
-                room.at[t, p], room.at[t, p], ssem.at[t, d - 1], rsem.at[t, d - 1],
-                device(moved(at, a, d)),
-            )
-            cp.start()
-            step.append(cp)
-        for cp in step:
-            cp.wait()
-        gsum[...] = room[t, 0] + room[t, 1] + room[t, 2] + room[t, 3]
-    k = at["k"]
-    room[3, k] = gsum[...]
-    cp = remote(room.at[3, k], room.at[3, k], ssem.at[3, 0], rsem.at[3, 0], device(mate(at)))
-    cp.start()
-    cp.wait()
-    gsum[...] = room[3, 0] + room[3, 1]
-    run_scatter(at, (p0, p1, p2), (r0, r1, r2), bufs, rest[6:])
+    cps = []
+
+    def rows():
+        yield
+        cps.extend(swap_over("row", dx_s, got, *rest[3:6]))
+
+    in_turn(
+        run_scatter(at, (p0, p1, p2), (r0, r1, r2), bufs, rest[6:9]),
+        rows(),
+        gain_steps(at, (ga, gf, gqk), rest[0], gsum, rest[1], rest[2]),
+        run_scatter(at, (s0, s1, s2), (t0, t1, t2), more, rest[9:12], 1),
+    )
     for cp in cps:
         cp.wait()
 
 
-def last(parts, dx_s, gains):
-    w = parts[0].shape[-1]
+def last(parts, sums, dx_s, gains):
+    total = 2 * WIDTH + 2 * HEAD
     return pl.pallas_call(
         last_kernel,
         name="last",
-        out_shape=[sds((64, w), F32)] * 3 + [sds(dx_s.shape), sds(gains.shape, F32)],
-        in_specs=[HBM] * 4 + [VMEM],
-        out_specs=[VMEM] * 3 + [HBM, VMEM],
-        scratch_shapes=scatter_buffers(w)
-        + [pltpu.VMEM((4, 4) + gains.shape, F32), DMA((4, 3)), DMA((4, 3))]
+        out_shape=[sds((64, 256), F32)] * 3
+        + [sds((64, 384), F32)] * 3
+        + [sds(dx_s.shape), sds((1, total), F32)],
+        in_specs=[HBM] * 7 + [VMEM] * 3,
+        out_specs=[VMEM] * 6 + [HBM, VMEM],
+        scratch_shapes=scatter_buffers(256)
+        + scatter_buffers(384, 1)
+        + [pltpu.VMEM((4, 4, 1, total), F32), DMA((4, 3)), DMA((4, 3))]
         + swap_sems("row")
+        + scatter_sems()
         + scatter_sems(),
-        compiler_params=params(8),
-    )(*parts, dx_s, gains)
-
-
-def arrive_kernel(t_row, t_col, out, dx, out_o, dx_o):
-    _, place = slots_sent(t_row[...], t_col[...])
+        compiler_params=params(9),
+    )(*parts, *sums, dx_s, *gains)
+
+
+def arrive_kernel(
+    t_row, out, dx, q, kv, o, g, u, d, gains,
+    out_o, dx_o, ga, gf, gq, gk, q_o, k_o, v_o, o_o, g_o, u_o, d_o,
+):
+    _, place = slots_sent(t_row[...])
     pick = onehot(place == iota((ROWS, ROWS), 1))
     out_o[...] = dot(pick, out[...].reshape(ROWS, WIDTH)).astype(BF)
     dx_o[...] = dot(pick, dx[...].reshape(ROWS, WIDTH)).astype(BF)
-
-
-def arrive(target, out, dx):
+    ga[...] = gains[:, 0:WIDTH]
+    gf[...] = gains[:, WIDTH : 2 * WIDTH]
+    gq[...] = gains[:, 2 * WIDTH : 2 * WIDTH + HEAD]
+    gk[...] = gains[:, 2 * WIDTH + HEAD :]
+    q_o[...] = q[...]
+    k_o[...] = kv[:, :HEAD]
+    v_o[...] = kv[:, HEAD:]
+    o_o[...] = o[...]
+    g_o[...] = g[...]
+    u_o[...] = u[...]
+    d_o[...] = d[...]
+
+
+def arrive(target, *args):
     return pl.pallas_call(
         arrive_kernel,
         name="arrive",
-        out_shape=[sds((ROWS, WIDTH))] * 2,
-        in_specs=[VMEM] * 4,
-        out_specs=[VMEM] * 2,
+        out_shape=[sds((ROWS, WIDTH))] * 2
+        + [sds((1, n), F32) for n in (WIDTH, WIDTH, HEAD, HEAD)]
+        + [
+            sds(n, F32)
+            for n in ((64, 256), (64, 128), (64, 128), (64, 256), (64, 384), (64, 384), (64, 384))
+        ],
+        in_specs=[VMEM] * 10,
+        out_specs=[VMEM] * 13,
         compiler_params=params(),
-    )(target.reshape(1, ROWS), target.reshape(ROWS, 1), out, dx)
-
-
-def layout(lengths):
-    ends = jnp.cumsum(lengths)
-    starts = (ends - lengths).astype(I32)
-    slots = jnp.arange(GROUP, dtype=I32)
-    first = jnp.max(jnp.where(starts[None, :] <= slots[:, None], starts[None, :], 0), axis=1)
-    lo = first[::ROWS] // ROWS
-    blocks = jnp.arange(NC, dtype=I32)
-    hi = jnp.max(jnp.where(lo[None, :] <= blocks[:, None], blocks[None, :], 0), axis=1)
-    return first, lo.astype(I32), hi.astype(I32)
+    )(target.reshape(1, ROWS), *args)
 
 
 def local(
     tokens, grad_out, target, lengths, attn_gain, ffn_gain, q_gain, k_gain,
     w_query, key_matrix, value_matrix, w_out, w_gate, w_up, w_down,
 ):
-    col = lax.axis_index("col")
-    first, lo, hi = layout(lengths[0])
-    mine = lax.dynamic_slice(first, (col * ROWS,), (ROWS,))
-    pos = (col * ROWS + jnp.arange(ROWS, dtype=I32) - mine).astype(F32)
-    freq = ROPE_BASE ** (-jnp.arange(HEAD // 2, dtype=F32) * 2.0 / HEAD)
-    angles = pos[:, None] * freq[None, :]
-    cos, sin = jnp.cos(angles), jnp.sin(angles)
-    cos = jnp.concatenate([cos, cos], axis=1)
-    sin = jnp.concatenate([-sin, sin], axis=1)
-    first2 = first.reshape(NC, 1, ROWS)
-    first2 = jnp.concatenate([first2, first2], axis=2)
     again, fgain = attn_gain.reshape(1, WIDTH), ffn_gain.reshape(1, WIDTH)
     qgain, kgain = q_gain.reshape(1, HEAD), k_gain.reshape(1, HEAD)
-
-    w_kv = jnp.concatenate([key_matrix, value_matrix], axis=1)
-    tok, grd, slt, wq, wkv, wo = dispatch(target, tokens, grad_out, [w_query, w_kv, w_out.T])
-    wg, wu, wd = gather([w_gate, w_up, w_down.T], 2, "gather_ffn")
-    qkv, raw, x, dy, n1h, dyh = project(
-        slt, tok, grd, again, qgain, kgain, cos, sin, wq, wkv
+    lens = lengths[0]
+
+    tok, grd, slt, wq, wkv, wo, *planes = dispatch(
+        target, tokens, grad_out, w_query, key_matrix, value_matrix, w_out.T, w_gate, w_up, w_down.T
     )
-    qkv = col_swap(qkv, 3, "swap_qkv")
-    o, o_t, lse = attend(lo, qkv, first2)
+    qkv, raw, x, dy, n1h, dyh, cos, sin, *planes = project(
+        lengths, slt, tok, grd, again, qgain, kgain, wq, wkv, planes
+    )
+    qkv, wg, wu, wd = heads(qkv, planes)
+    o, o_t, lse = attend(lens, qkv)
     oa = col_swap(o, 4, "swap_o")
     out_s, dh, dhlh, n2h, act, d_o, gain_f = middle(slt, x, dy, oa, fgain, wo, wg, wu, wd)
     g_o, got_out, act_m, oa_m, n2_m, dy_m, dhl_m = back_swap(
         d_o, out_s, act, oa, n2h, dyh, dhlh
     )
-    parts = ffn_grads(n2h, n2_m, dyh, dy_m, act, act_m)
-    r_gate, r_up, r_down = scatter(parts, 6, "scatter_ffn")
-    dqkv = attend_back(hi, qkv, first2, g_o, o_t, lse)
-    dqkv = col_swap(dqkv, 9, "swap_dqkv")
-    draw, dx_s, gain_a, gain_qk = project_back(
-        slt, x, dh, again, qgain, kgain, cos, sin, raw, dqkv, wq, wkv
+    f_parts = ffn_grads(n2h, n2_m, dyh, dy_m, act, act_m)
+    dqkv = attend_back(lens, qkv, g_o, o_t, lse)
+    dqkv, *later = heads_back(dqkv, f_parts)
+    draw, dx_s, gain_a, gain_qk, *piece = project_back(
+        slt, x, dh, again, qgain, kgain, cos, sin, raw, dqkv, wq, wkv,
+        f_parts, later[:3], later[3:],
     )
-    draw_m, n1_m = core_swap(draw, n1h)
-    parts = attn_grads(n1h, n1_m, dhlh, dhl_m, draw, draw_m, oa, oa_m)
-    gains = jnp.concatenate([gain_a, gain_f, gain_qk, jnp.zeros((1, 768), F32)], axis=1)
-    r_q, r_kv, r_o, got_dx, gains = last(parts, dx_s, gains.reshape(24, HEAD))
-    output, input_grad = arrive(target, got_out, got_dx)
-    gains = gains.reshape(-1)
+    draw_m, n1_m, *sums = core_swap(draw, n1h, f_parts, piece)
+    a_parts = attn_grads(n1h, n1_m, dhlh, dhl_m, draw, draw_m, oa, oa_m)
+    r_q, r_kv, r_o, r_g, r_u, r_d, got_dx, gains = last(
+        a_parts, sums, dx_s, (gain_a, gain_f, gain_qk)
+    )
+    output, input_grad, ga, gf, gq, gk, g_q, g_k, g_v, g_o, g_g, g_u, g_d = arrive(
+        target, got_out, got_dx, r_q, r_kv, r_o, r_g, r_u, r_d, gains
+    )
     return (
-        output,
-        input_grad,
-        gains[0:1024],
-        gains[1024:2048],
-        gains[2048:2176],
-        gains[2176:2304],
-        r_q,
-        r_kv[:, :HEAD],
-        r_kv[:, HEAD:],
-        r_o.T,
-        r_gate,
-        r_up,
-        r_down.T,
+        output, input_grad, ga[0], gf[0], gq[0], gk[0], g_q, g_k, g_v, g_o.T, g_g, g_u, g_d.T,
     )
 
 

time: 477 us -> 415 us (0.87)
  Pallas kernels: 458 us -> 415 us
  local copies, waits for them, and re-layouts: 10.4 us -> 0 us
  other arithmetic: 7.52 us -> 0 us
    pallas_call x3 -> x1, Pallas kernels: 79.8 us -> 16.4 us  [col_swap(): pl.pallas_call(col_swap_kernel, name=name, out_shape=sds(src.shape), in_s...]
    pallas_call x3, Pallas kernels: 171 us -> 152 us  [the longest x1 55 us: last(): pl.pallas_call(last_kernel, name='last', out_shape=[sds((64, 256), F32)]...]
    pallas_call x1, Pallas kernels: 11.8 us -> 30.2 us  [project(): pl.pallas_call(project_kernel, name='project', grid=(NC,), out_shape=[sds...]
    pallas_call x1, Pallas kernels: 14.8 us -> 24.4 us  [project_back(): pl.pallas_call(project_back_kernel, name='project_back', grid=(NC,), out_...]
    pallas_call x1, Pallas kernels: 63.4 us -> 69.2 us  [dispatch(): pl.pallas_call(dispatch_kernel, name='dispatch', out_shape=[sds((NR, 16,...]
    pallas_call x1, Pallas kernels: 23.5 us -> 28.8 us  [back_swap(): pl.pallas_call(back_swap_kernel, name='back_swap', out_shape=[sds(d_o.sha...]
    unnamed x15 -> x0, local copies, waits for them, and re-layouts: 4.89 us -> none
where the time goes in v2:
time: 415 us; the launch traced here: 416 us
  Pallas kernels  415 us (100%)
    pallas_call x1, Pallas kernels, dispatch(): pl.pallas_call(dispatch_kernel, name='dispatch', out_shape=[sds((NR, 16,...  69.2 us
    pallas_call x1, Pallas kernels, last(): pl.pallas_call(last_kernel, name='last', out_shape=[sds((64, 256), F32)]...  55 us
    pallas_call x1, Pallas kernels, heads_back(): pl.pallas_call(heads_back_kernel, name='swap_dqkv', out_shape=[sds(src.sh...  50.1 us
    pallas_call x1, Pallas kernels, heads(): pl.pallas_call(heads_kernel, name='swap_qkv', out_shape=[sds(src.shape)]...  46.5 us
    pallas_call x1, Pallas kernels, middle(): pl.pallas_call(middle_kernel, name='middle', grid=(3 * NC,), out_shape=[s...  33.4 us
    pallas_call x1, Pallas kernels, project(): pl.pallas_call(project_kernel, name='project', grid=(NC,), out_shape=[sds...  30.2 us
    pallas_call x1, Pallas kernels, back_swap(): pl.pallas_call(back_swap_kernel, name='back_swap', out_shape=[sds(d_o.sha...  28.8 us
    pallas_call x1, Pallas kernels, project_back(): pl.pallas_call(project_back_kernel, name='project_back', grid=(NC,), out_...  24.4 us

profile of v2, /device:TPU:0, one launch (start us, length us, event | category | flops | bytes accessed | tf_op | source)
XLA Modules:
  0.0 415.9 jit_solution(3667731282742566855)
XLA Ops:
  0.6 69.2 %dispatch.1 = (bf16[16,16,1024]{2,1,0:T(8,128)(2,1)}, bf16[16,16,1024]{2,1,0:T(8,128)(2,1)}, s32[16,16,128]{2,1,0:T(8,128)}, bf16[4,2,4,2,2,64,256]{6,5,4,3,2,1,...) custom-call(s32[1,256]{1,0:T(1,128)} %bitcast.20, ...), custom_call_target="tpu_custom_call" | custom-call | tf_op jit(solution)/shard_map/dispatch/pallas_call | solution.py:592
  69.9 30.2 %project.1 = (bf16[8,256,512]{2,1,0:T(8,128)(2,1)}, f32[8,256,384]{2,1,0:T(8,128)}, bf16[256,1024]{1,0:T(8,128)(2,1)}, bf16[256,1024]{1,0:T(8,128)(2,1)}, bf16[2...) custom-call(s32[1,8]{1,0:T(1,128)} %lens.1, ...), custom_call_target="tpu_custom_call", output_to_operand_aliasing={{8}: (10, {}), {9}: (11, {}), {10}: (12, {})} | custom-call | tf_op jit(solution)/shard_map/project/pallas_call | solution.py:698
  100.0 46.5 %swap_qkv.1 = (bf16[8,256,512]{2,1,0:T(8,128)(2,1)}, bf16[4,2,4,2,2,64,384]{6,5,4,3,2,1,0:T(8,128)(2,1)}, bf16[4,2,4,2,2,64,384]{6,5,4,3,2,1,0:T(8,128)(2,1)}, bf16[4,2,4,2,2,64,384]{6,5,4,3,2,1,0:T(8,128)(2,1)}) custom-call(bf16[8,256,512]{2,1,0:T(8,128)(2,1)} %get-tuple-element.110.src, ...), custom_call_target="tpu_custom_call", output_to_operand_aliasing={{1}: (1, {}), {2}: (2, {}), {3}: (3, {})} | custom-call | tf_op jit(solution)/shard_map/swap_qkv/pallas_call | solution.py:763
  146.5 13.6 %attend.1 = (bf16[8,256,256]{2,1,0:T(8,128)(2,1)}, f32[8,128,512]{2,1,0:T(8,128)}, f32[8,1,512]{2,1,0:T(1,128)}) custom-call(s32[8]{0:T(128)} %bitcast.18, bf16[8,256,512]{2,1,0:T(8,128)(2,1)} %get-tuple-element.114.qkv), custom_call_target="tpu_custom_call" | custom-call | tf_op jit(solution)/shard_map/attend/pallas_call | solution.py:845
  160.2 16.4 %swap_o.1.oa = bf16[8,256,256]{2,1,0:T(8,128)(2,1)} custom-call(bf16[8,256,256]{2,1,0:T(8,128)(2,1)} %get-tuple-element.115.src), custom_call_target="tpu_custom_call" | custom-call | tf_op jit(solution)/shard_map/swap_o/pallas_call | solution.py:495
  176.6 33.4 %middle.1 = (bf16[16,16,1024]{2,1,0:T(8,128)(2,1)}, f32[256,1024]{1,0:T(8,128)}, bf16[2,256,512]{2,1,0:T(8,128)(2,1)}, bf16[2,256,512]{2,1,0:T(8,128)(2,1)}, bf1...) custom-call(s32[16,16,128]{2,1,0:T(8,128)} %get-tuple-element.100.slt, ...), custom_call_target="tpu_custom_call" | custom-call | tf_op jit(solution)/shard_map/middle/pallas_call | solution.py:1020
  210.0 28.8 %back_swap.1 = (bf16[8,256,256]{2,1,0:T(8,128)(2,1)}, bf16[16,16,1024]{2,1,0:T(8,128)(2,1)}, bf16[8,256,1152]{2,1,0:T(8,128)(2,1)}, bf16[8,256,256]{2,1,0:T(8,12...) custom-call(bf16[8,256,256]{2,1,0:T(8,128)(2,1)} %get-tuple-element.120.d_o, ...), custom_call_target="tpu_custom_call" | custom-call | tf_op jit(solution)/shard_map/back_swap/pallas_call | solution.py:1089
  238.8 16.6 %attend_back.1.src = bf16[8,256,512]{2,1,0:T(8,128)(2,1)} custom-call(s32[8]{0:T(128)} %bitcast.19, bf16[8,256,512]{2,1,0:T(8,128)(2,1)} %get-tuple-element.114.qkv, bf16[8,256,256]{2,1,0:T(8,128)(2,1)} %get-tuple-element.132.d_o, f32[8,128,512]{2,1,0:T(8,128)} %get-tuple-element.133.o_t, f32[8,1,512]{2,1,0:T(1,128)} %get-tuple-element.134.lse), custom_call_target="tpu_custom_call" | custom-call | tf_op jit(solution)/shard_map/attend_back/pallas_call | solution.py:910
  255.5 12.4 %ffn_grads.1 = (bf16[4,2,4,2,64,384]{5,4,3,2,1,0:T(8,128)(2,1)}, bf16[4,2,4,2,64,384]{5,4,3,2,1,0:T(8,128)(2,1)}, bf16[4,2,4,2,64,384]{5,4,3,2,1,0:T(8,128)(2,1)}) custom-call(bf16[2,256,512]{2,1,0:T(8,128)(2,1)} %get-tuple-element.123.n2h, bf16[256,512]{1,0:T(8,128)(2,1)} %get-tuple-element.135.n2_m, bf16[2,256,512]{2,1,0:T(8,128)(2,1)} %get-tuple-element.124.dyh, ...), custom_call_target="tpu_custom_call" | custom-call | tf_op jit(solution)/shard_map/ffn_grads/pallas_call | solution.py:1127
  267.9 50.1 %swap_dqkv.1 = (bf16[8,256,512]{2,1,0:T(8,128)(2,1)}, bf16[2,4,4,32,384]{4,3,2,1,0:T(8,128)(2,1)}, bf16[2,2,4,2,32,384]{5,4,3,2,1,0:T(8,128)(2,1)}, bf16[2,4,2,2...) custom-call(bf16[8,256,512]{2,1,0:T(8,128)(2,1)} %attend_back.1.src,, ...), custom_call_target="tpu_custom_call" | custom-call | tf_op jit(solution)/shard_map/swap_dqkv/pallas_call | solution.py:1194
  318.0 24.4 %project_back.1 = (bf16[8,256,512]{2,1,0:T(8,128)(2,1)}, bf16[16,16,1024]{2,1,0:T(8,128)(2,1)}, f32[1,1024]{1,0:T(1,128)}, f32[1,256]{1,0:T(1,128)}, bf16[2,4,4,...) custom-call(s32[16,16,128]{2,1,0:T(8,128)} %get-tuple-element.100.sl, ...), custom_call_target="tpu_custom_call", output_to_operand_aliasing={{4}: (18, {}), {5}: (19, {}), {6}: (20, {})} | custom-call | tf_op jit(solution)/shard_map/project_back/pallas_call | solution.py:1280
  342.4 5.1 %core_swap.1 = (bf16[8,256,512]{2,1,0:T(8,128)(2,1)}, bf16[256,512]{1,0:T(8,128)(2,1)}, bf16[4,4,64,384]{3,2,1,0:T(8,128)(2,1)}, bf16[2,4,2,64,384]{4,3,2,1,0:T(8,128)(2,1)}, bf16[4,2,2,64,384]{4,3,2,1,0:T(8,128)(2,1)}) custom-call(bf16[8,256,512]{2,1,0:T(8,128)(2,1)} %get-tuple-element.148.dqkv, bf16[2,256,512]{2,1,0:T(8,128)(2,1)} %get-tuple-element.127.n1h, ...), custom_call_target="tpu_custom_call" | custom-call | tf_op jit(solution)/shard_map/core_swap/pallas_call | solution.py:1361
  347.6 10.1 %attn_grads.1 = (bf16[4,2,4,2,64,256]{5,4,3,2,1,0:T(8,128)(2,1)}, bf16[4,2,4,2,64,256]{5,4,3,2,1,0:T(8,128)(2,1)}, bf16[4,2,4,2,64,256]{5,4,3,2,1,0:T(8,128)(2,1)}) custom-call(bf16[2,256,512]{2,1,0:T(8,128)(2,1)} %get-tuple-element.127.n1h, bf16[256,512]{1,0:T(8,128)(2,1)} %get-tuple-element.152.n1_m, bf16[2,256,512]{2,1,0:T(8,128)(2,1)} %get-tuple-element.125.dhlh, ...), custom_call_target="tpu_custom_call" | custom-call | tf_op jit(solution)/shard_map/attn_grads/pallas_call | solution.py:1160
  357.6 55.0 %last.1 = (f32[64,256]{1,0:T(8,128)}, f32[64,256]{1,0:T(8,128)}, f32[64,256]{1,0:T(8,128)}, f32[64,384]{1,0:T(8,128)}, f32[64,384]{1,0:T(8,128)}, /*index=5*/f32...) custom-call(bf16[4,2,4,2,64,256]{5,4,3,2,1,0:T(8,128)(2,1)} %get-tuple-element.156.p0, ...), custom_call_target="tpu_custom_call" | custom-call | tf_op jit(solution)/shard_map/last/pallas_call | solution.py:1427
  412.6 3.1 arrive.1

commit v3 on v2

--- a/solution.py
+++ b/solution.py
@@ -113,8 +113,9 @@
 
 
 class Gather:
-    def __init__(self, at, outs, sems):
-        self.at, self.outs = at, outs
+    def __init__(self, at, outs, sems, phases=(0, 1, 2), own=None):
+        self.at, self.outs, self.own = at, outs, own
+        self.base = {t: sum(4 if p == 0 else 16 for p in phases if p < t) for t in phases}
         self.ssem, self.rsem, self.msem, self.nsem = sems
         self.n = len(outs)
         self.half = outs[0].shape[5] // 2
@@ -122,14 +123,15 @@
 
     def copies(self, s, t, g):
         ref = self.outs[s].at[piece_index(self.at, s, t, g, 0)]
-        a, i = ORDERS[s][t], t * 4 + (g or 0)
+        a, i = ORDERS[s][t], self.base[t] + 4 * (g or 0)
+        src = self.own[s] if self.own and (t == 0 or (t == 1 and g == 0)) else ref
         return [
-            remote(ref, ref, self.ssem.at[s, i, d], self.rsem.at[s, i, d], device(moved(self.at, a, step)))
+            remote(src, ref, self.ssem.at[s, i + d], self.rsem.at[s, i + d], device(moved(self.at, a, step)))
             for d, step in enumerate((1, -1))
         ]
 
     def forwards(self, s, t, g):
-        a, i = ORDERS[s][t], t * 4 + (g or 0)
+        a, i = ORDERS[s][t], self.base[t] + 4 * (g or 0) + 2
         out = []
         for d, step in enumerate((1, -1)):
             came = piece_index(self.at, s, t, g, -step) + (pl.ds(d * self.half, self.half),)
@@ -138,8 +140,8 @@
                 remote(
                     ref,
                     ref,
-                    self.ssem.at[s, i, 2 + d],
-                    self.rsem.at[s, i, 2 + d],
+                    self.ssem.at[s, i + d],
+                    self.rsem.at[s, i + d],
                     device(moved(self.at, a, step)),
                 )
             )
@@ -238,12 +240,8 @@
             self.arrived(2, g)
 
 
-def gather_sems(n=3):
-    return [DMA((n, 12, 4)), DMA((n, 12, 4)), DMA((n, 16)), DMA((n, 16))]
-
-
-def plane_sems(n=3):
-    return gather_sems(n)
+def gather_sems(steps, shares, n=3):
+    return [DMA((n, steps)), DMA((n, steps)), DMA((n, max(shares, 1))), DMA((n, max(shares, 1)))]
 
 
 def gather_shape(w):
@@ -319,8 +317,8 @@
     return out
 
 
-def scatter_sems(n=3):
-    return [DMA((n, 3, 6)), DMA((n, 3, 6)), DMA((n, 3))]
+def scatter_sems(phases=3, n=3):
+    return [DMA((n, phases, 6)), DMA((n, phases, 6)), DMA((n, 3))]
 
 
 LO, HI = pl.ds(0, 32), pl.ds(32, 32)
@@ -331,7 +329,7 @@
     return sub_index({a: (at[a] + rel) % 4}, ORDERS[s][: 3 - t]) + (rows,)
 
 
-def first_sends(s, t, at, ref, rel_in, piece_in, ssem, rsem):
+def first_sends(s, t, at, ref, rel_in, piece_in, ssem, rsem, t0=0):
     a = ORDERS[s][2 - t]
     right, left = device(moved(at, a, 1)), device(moved(at, a, -1))
     allr = (slice(None),) * len(scatter_leads(s, t))
@@ -340,25 +338,25 @@
         return ref.at[part_of(s, t, at, rel, rows)]
 
     return [
-        remote(src(2, LO), rel_in.at[0], ssem.at[s, t, 0], rsem.at[s, t, 0], right),
-        remote(src(2, HI), rel_in.at[1], ssem.at[s, t, 1], rsem.at[s, t, 1], left),
+        remote(src(2, LO), rel_in.at[0], ssem.at[s, t - t0, 0], rsem.at[s, t - t0, 0], right),
+        remote(src(2, HI), rel_in.at[1], ssem.at[s, t - t0, 1], rsem.at[s, t - t0, 1], left),
         remote(
-            src(1, HI), piece_in.at[(0,) + allr + (HI,)], ssem.at[s, t, 2], rsem.at[s, t, 2], right
+            src(1, HI), piece_in.at[(0,) + allr + (HI,)], ssem.at[s, t - t0, 2], rsem.at[s, t - t0, 2], right
         ),
         remote(
-            src(-1, LO), piece_in.at[(1,) + allr + (LO,)], ssem.at[s, t, 3], rsem.at[s, t, 3], left
+            src(-1, LO), piece_in.at[(1,) + allr + (LO,)], ssem.at[s, t - t0, 3], rsem.at[s, t - t0, 3], left
         ),
     ]
 
 
-def second_send(s, t, at, d, rel_out, piece_in, ssem, rsem):
+def second_send(s, t, at, d, rel_out, piece_in, ssem, rsem, t0=0):
     a = ORDERS[s][2 - t]
     allr = (slice(None),) * len(scatter_leads(s, t))
     return remote(
         rel_out.at[d],
         piece_in.at[(d,) + allr + ((LO, HI)[d],)],
-        ssem.at[s, t, 4 + d],
-        rsem.at[s, t, 4 + d],
+        ssem.at[s, t - t0, 4 + d],
+        rsem.at[s, t - t0, 4 + d],
         device(moved(at, a, (1, -1)[d])),
     )
 
@@ -382,7 +380,7 @@
         for s in range(n):
             i = s * per + 4 * (t - t0)
             rel_in, piece_in, rel_out, total = bufs[i : i + 4]
-            cps = first_sends(s, t, at, cur[s], rel_in, piece_in, ssem, rsem)
+            cps = first_sends(s, t, at, cur[s], rel_in, piece_in, ssem, rsem, t0)
             for cp in cps:
                 cp.start()
             loads = []
@@ -408,7 +406,7 @@
                 else:
                     mine = (cur[s], picker(s, t, at, (1, -1)[d], (LO, HI)[d]))
                 add_blocks(lead, (rel_out, side(d)), [mine, (rel_in, side(d))])
-                cp = second_send(s, t, at, d, rel_out, piece_in, ssem, rsem)
+                cp = second_send(s, t, at, d, rel_out, piece_in, ssem, rsem, t0)
                 cp.start()
                 cps.append(cp)
         yield
@@ -542,75 +540,6 @@
     return g_row * (ROWS // NR) + before_row, g_col * (ROWS // NR) + before_col
 
 
-def dispatch_kernel(
-    t_row, tokens, grads, w_q, w_k, w_v, w_o, w_g, w_u, w_d,
-    tok, grd, slt, a0, a1, a2, f0, f1, f2,
-    tok_s, grd_s, slt_s, own_sem, *sems,
-):
-    at = where_am_i()
-    here = block_index({a: at[a] for a in "xyz"}, at["k"])
-    rows = (slice(None),)
-    own = [
-        (w_q, a0.at[here]),
-        (w_k, a1.at[here + rows + (pl.ds(0, HEAD),)]),
-        (w_v, a1.at[here + rows + (pl.ds(HEAD, HEAD),)]),
-        (w_o, a2.at[here]),
-        (w_g, f0.at[here]),
-        (w_u, f1.at[here]),
-        (w_d, f2.at[here]),
-    ]
-    own = [pltpu.make_async_copy(src, dst, own_sem.at[i]) for i, (src, dst) in enumerate(own)]
-    for cp in own:
-        cp.start()
-    meet(ring_peers(at) + row_peers(at))
-    for cp in own:
-        cp.wait()
-    first = Gather(at, (a0, a1, a2), sems[9:13])
-    second = Gather(at, (f0, f1, f2), sems[13:17])
-    steps = first.all()
-    more = second.lines()
-    next(steps)
-    place, _ = slots_sent(t_row[...])
-    sel = place == iota((ROWS, ROWS), 0)
-    pick = onehot(sel)
-    tok_s[...] = dot(pick, tokens[...]).astype(BF).reshape(tok_s.shape)
-    slot = jnp.sum(jnp.where(sel, t_row[...], 0).astype(F32), axis=1, keepdims=True)
-    slt_s[...] = jnp.broadcast_to(slot, (ROWS, HEAD)).astype(I32).reshape(slt_s.shape)
-    cps = swap_over("row", tok_s, tok, *sems[0:3])
-    cps += swap_over("row", slt_s, slt, *sems[6:9])
-    next(steps)
-    grd_s[...] = dot(pick, grads[...]).astype(BF).reshape(grd_s.shape)
-    cps += swap_over("row", grd_s, grd, *sems[3:6])
-    in_turn(steps, more)
-    for cp in cps:
-        cp.wait()
-    first.drain()
-    second.drain()
-
-
-def dispatch(target, tokens, grads, w_q, w_k, w_v, w_o, w_g, w_u, w_d):
-    return pl.pallas_call(
-        dispatch_kernel,
-        name="dispatch",
-        out_shape=[sds((NR, 16, WIDTH))] * 2
-        + [sds((NR, 16, HEAD), I32)]
-        + [gather_shape(256)] * 3
-        + [gather_shape(384)] * 3,
-        in_specs=[VMEM] * 3 + [HBM] * 7,
-        out_specs=[HBM] * 9,
-        scratch_shapes=[pltpu.VMEM((NR, 16, WIDTH), BF)] * 2
-        + [pltpu.VMEM((NR, 16, HEAD), I32)]
-        + [DMA((7,))]
-        + swap_sems("row") * 3
-        + gather_sems()
-        + gather_sems(),
-        compiler_params=params(1),
-    )(
-        target.reshape(1, ROWS), tokens, grads,
-        w_q, w_k, w_v, w_o, w_g, w_u, w_d,
-    )
-
-
 def halves_of(v):
     even, odd = [], []
     low = iota((v.shape[0], HEAD), 1) < HEAD // 2
@@ -630,61 +559,6 @@
     return out
 
 
-def project_kernel(
-    lens, slt, tok, grd, again, qgain, kgain, freq, wq, wkv, i0, i1, i2,
-    out, raw, x_o, dy_o, n1h, dyh, cos, sin, f0, f1, f2, n1_s, *sems,
-):
-    c = pl.program_id(0)
-    at = where_am_i()
-    more = Gather(at, (f0, f1, f2), sems)
-
-    @pl.when(c == 0)
-    def _():
-        meet(ring_peers(at) + [device(mate(at))])
-        more.send(2, None)
-
-    @pl.when(c == 0)
-    def _():
-        slots = lax.axis_index("col") * ROWS + iota((ROWS, HEAD), 0)
-        pos = (slots - first_slots(lambda j: lens[0, j], slots)).astype(F32)
-        angle = pos * freq[...]
-        cos[...] = jnp.cos(angle)
-        sine = jnp.sin(angle)
-        sin[...] = jnp.where(iota((ROWS, HEAD), 1) < HEAD // 2, -sine, sine)
-        local = slt[...].reshape(ROWS, HEAD)[:, :1] % ROWS
-        put = onehot(local == iota((ROWS, ROWS), 1))
-        x = dot(put, tok[...].reshape(ROWS, WIDTH), TN)
-        dy = dot(put, grd[...].reshape(ROWS, WIDTH), TN)
-        x_o[...] = x.astype(BF)
-        dy_o[...] = dy.astype(BF)
-        n1 = x * mean_square_scale(x) * again[...]
-        n1_s[...] = n1.astype(BF)
-        a, b = halves_of(n1)
-        n1h[0] = a.astype(BF)
-        n1h[1] = b.astype(BF)
-        a, b = halves_of(dy)
-        dyh[0] = a.astype(BF)
-        dyh[1] = b.astype(BF)
-
-    n1 = n1_s[...]
-    q = dot(n1, wq[0, 0].reshape(WIDTH, 256))
-    kv = dot(n1, wkv[0, 0].reshape(WIDTH, 256))
-    raw[0, :, 0:256] = q
-    raw[0, :, 256:384] = kv[:, :HEAD]
-    pieces = ((q[:, :HEAD], qgain), (q[:, HEAD:], qgain), (kv[:, :HEAD], kgain))
-    for i, (v, gain) in enumerate(pieces):
-        n = v * mean_square_scale(v) * gain[...]
-        n = n * cos[...] + pltpu.roll(n, HEAD // 2, 1) * sin[...]
-        out[0, :, i * HEAD : (i + 1) * HEAD] = n.astype(BF)
-    out[0, :, 3 * HEAD :] = kv[:, HEAD:].astype(BF)
-
-    @pl.when(c == NC - 1)
-    def _():
-        for s in range(3):
-            for cp in more.copies(s, 2, None) + [more.to_mate(s, None, 0)]:
-                cp.wait()
-
-
 def slab(w):
     return pl.BlockSpec((1, 1, 4, 2, 2, 64, w), lambda c: (c % 4, c // 4, 0, 0, 0, 0, 0))
 
@@ -693,12 +567,138 @@
     return pl.BlockSpec(shape, lambda *_: (0,) * len(shape))
 
 
-def project(lens, slt, tok, grd, again, qgain, kgain, wq, wkv, planes):
+def front_kernel(
+    t_row, lens, tokens, grads, again, qgain, kgain, freq, w_q, w_k, w_v, w_o, w_g, w_u, w_d,
+    qkv, raw, x_o, dy_o, n1h, dyh, cos, sin, slt, a0, a1, a2, f0, f1, f2,
+    sent, came, kv_s, n1_s, src_s, raw_s, wq_v, wkv_v,
+    own_sem, w_sem, raw_sem, out_ssem, out_rsem, out_lsem, *sems,
+):
+    at = where_am_i()
+    row, col = lax.axis_index("row"), lax.axis_index("col")
+    here = block_index({a: at[a] for a in "xyz"}, at["k"])
+    kv_s[:, :HEAD] = w_k[...]
+    kv_s[:, HEAD:] = w_v[...]
+    pairs = zip((w_q, kv_s, w_o, w_g, w_u, w_d), (a0, a1, a2, f0, f1, f2))
+    own = [
+        pltpu.make_async_copy(src, dst.at[here], own_sem.at[i])
+        for i, (src, dst) in enumerate(pairs)
+    ]
+    for cp in own:
+        cp.start()
+    near = [device(moved(at, "z", 1)), device(moved(at, "z", -1))]
+    meet(near + row_peers(at) + col_peers(at))
+    first = Gather(at, (a0, a1, a2), sems[3:7], own=(w_q, kv_s, w_o))
+    second = Gather(at, (f0, f1, f2), sems[7:11], (0, 1), own=(w_g, w_u, w_d))
+    steps = first.all()
+    more = second.lines()
+    next(steps)
+    place, _ = slots_sent(t_row[...])
+    sel = place == iota((ROWS, ROWS), 0)
+    pick = onehot(sel)
+    slot = jnp.sum(jnp.where(sel, t_row[...] % ROWS, 0).astype(F32), axis=1, keepdims=True)
+    message = (NR, 16, WIDTH)
+    sent[:, :, 0:WIDTH] = dot(pick, tokens[...]).astype(BF).reshape(message)
+    sent[:, :, WIDTH : 2 * WIDTH] = dot(pick, grads[...]).astype(BF).reshape(message)
+    sent[:, :, 2 * WIDTH :] = (
+        jnp.broadcast_to(slot, (ROWS, HEAD)).astype(BF).reshape((NR, 16, HEAD))
+    )
+    cps = swap_over("row", sent, came, *sems[0:3])
+    next(steps)
+    for cp in own:
+        cp.wait()
+    for _ in range(5):
+        next(steps)
+        next(more, None)
+
+    slots = col * ROWS + iota((ROWS, HEAD), 0)
+    pos = (slots - first_slots(lambda j: lens[0, j], slots)).astype(F32)
+    angle = pos * freq[...]
+    cos[...] = jnp.cos(angle)
+    sine = jnp.sin(angle)
+    sin[...] = jnp.where(iota((ROWS, HEAD), 1) < HEAD // 2, -sine, sine)
+    for cp in cps:
+        cp.wait()
+    local = came[:, :, 2 * WIDTH :].reshape(ROWS, HEAD)
+    slt[...] = local
+    put = onehot(local[:, :1].astype(F32).astype(I32) == iota((ROWS, ROWS), 1))
+    x = dot(put, came[:, :, 0:WIDTH].reshape(ROWS, WIDTH), TN)
+    x_o[...] = x.astype(BF)
+    n1 = x * mean_square_scale(x) * again[...]
+    n1_s[...] = n1.astype(BF)
+    a, b = halves_of(n1)
+    n1h[0] = a.astype(BF)
+    n1h[1] = b.astype(BF)
+    dy = dot(put, came[:, :, WIDTH : 2 * WIDTH].reshape(ROWS, WIDTH), TN)
+    dy_o[...] = dy.astype(BF)
+    a, b = halves_of(dy)
+    dyh[0] = a.astype(BF)
+    dyh[1] = b.astype(BF)
+
+    in_turn(steps, more)
+    first.drain()
+    second.drain()
+
+    def block_at(i):
+        return (col + 1 + i) % NC
+
+    def loads(i):
+        c, slot = block_at(i), i % 2
+        return [
+            pltpu.make_async_copy(a0.at[c % 4, c // 4], wq_v.at[slot], w_sem.at[0, slot]),
+            pltpu.make_async_copy(a1.at[c % 4, c // 4], wkv_v.at[slot], w_sem.at[1, slot]),
+        ]
+
+    def sends(i):
+        c = block_at(i)
+        return remote(src_s.at[c], qkv.at[col], out_ssem.at[i], out_rsem.at[i], (row, c))
+
+    for cp in loads(0):
+        cp.start()
+
+    @pl.loop(0, NC)
+    def _(i):
+        c = block_at(i)
+
+        @pl.when(i < NC - 1)
+        def _():
+            for cp in loads(i + 1):
+                cp.start()
+
+        for cp in loads(i):
+            cp.wait()
+        n = n1_s[...]
+        q = dot(n, wq_v[i % 2].reshape(WIDTH, 256))
+        kv = dot(n, wkv_v[i % 2].reshape(WIDTH, 256))
+        raw_s[c, :, 0:256] = q
+        raw_s[c, :, 256:384] = kv[:, :HEAD]
+        pieces = ((q[:, :HEAD], qgain), (q[:, HEAD:], qgain), (kv[:, :HEAD], kgain))
+        for j, (v, gain) in enumerate(pieces):
+            v = v * mean_square_scale(v) * gain[...]
+            v = v * cos[...] + pltpu.roll(v, HEAD // 2, 1) * sin[...]
+            src_s[c, :, j * HEAD : (j + 1) * HEAD] = v.astype(BF)
+        src_s[c, :, 3 * HEAD :] = kv[:, HEAD:].astype(BF)
+
+        @pl.when(i < NC - 1)
+        def _():
+            sends(i).start()
+
+    mine = pltpu.make_async_copy(src_s.at[col], qkv.at[col], out_lsem)
+    mine.start()
+    keep = pltpu.make_async_copy(raw_s, raw, raw_sem)
+    keep.start()
+    for i in range(NC - 1):
+        sends(i).wait()
+    mine.wait()
+    keep.wait()
+
+
+def front(target, lens, tokens, grads, again, qgain, kgain, *weights):
     freq = ROPE_BASE ** (-(np.arange(HEAD) % (HEAD // 2)).astype(np.float32) * 2.0 / HEAD)
+    freq = jnp.asarray(freq.astype(np.float32).reshape(1, HEAD))
+    rows = pltpu.VMEM((NR, 16, 2 * WIDTH + HEAD), BF)
     return pl.pallas_call(
-        project_kernel,
-        name="project",
-        grid=(NC,),
+        front_kernel,
+        name="front",
         out_shape=[
             sds((NC, ROWS, 512)),
             sds((NC, ROWS, 384), F32),
@@ -708,68 +708,29 @@
             sds((2, ROWS, 512)),
             sds((ROWS, HEAD), F32),
             sds((ROWS, HEAD), F32),
+            sds((ROWS, HEAD)),
         ]
+        + [gather_shape(256)] * 3
         + [gather_shape(384)] * 3,
-        in_specs=[
-            pl.BlockSpec(memory_space=pltpu.SMEM),
-            whole((NR, 16, HEAD)),
-            whole((NR, 16, WIDTH)),
-            whole((NR, 16, WIDTH)),
-            whole((1, WIDTH)),
-            whole((1, HEAD)),
-            whole((1, HEAD)),
-            whole((1, HEAD)),
-            slab(256),
-            slab(256),
+        in_specs=[VMEM, pl.BlockSpec(memory_space=pltpu.SMEM)]
+        + [VMEM] * 6
+        + [HBM, VMEM, VMEM]
+        + [HBM] * 4,
+        out_specs=[HBM] * 2 + [VMEM] * 7 + [HBM] * 6,
+        scratch_shapes=[rows, rows, pltpu.VMEM((64, 256), BF)]
+        + [
+            pltpu.VMEM((ROWS, WIDTH), BF),
+            pltpu.VMEM((NC, ROWS, 512), BF),
+            pltpu.VMEM((NC, ROWS, 384), F32),
+            pltpu.VMEM((2, 4, 2, 2, 64, 256), BF),
+            pltpu.VMEM((2, 4, 2, 2, 64, 256), BF),
         ]
-        + [HBM] * 3,
-        out_specs=[
-            pl.BlockSpec((1, ROWS, 512), lambda c: (c, 0, 0)),
-            pl.BlockSpec((1, ROWS, 384), lambda c: (c, 0, 0)),
-            whole((ROWS, WIDTH)),
-            whole((ROWS, WIDTH)),
-            whole((2, ROWS, 512)),
-            whole((2, ROWS, 512)),
-            whole((ROWS, HEAD)),
-            whole((ROWS, HEAD)),
-        ]
-        + [HBM] * 3,
-        input_output_aliases={10: 8, 11: 9, 12: 10},
-        scratch_shapes=[pltpu.VMEM((ROWS, WIDTH), BF)] + gather_sems(),
-        compiler_params=params(2),
-    )(
-        lens, slt, tok, grd, again, qgain, kgain,
-        jnp.asarray(freq.astype(np.float32).reshape(1, HEAD)), wq, wkv, *planes,
-    )
-
-
-def heads_kernel(src, i0, i1, i2, dst, f0, f1, f2, *sems):
-    at = where_am_i()
-    meet(ring_peers(at) + [device(mate(at))] + col_peers(at))
-    more = Gather(at, (f0, f1, f2), sems[3:])
-    cps = swap_over("col", src, dst, *sems[:3])
-    for s in range(3):
-        for d, cp in enumerate(more.forwards(s, 2, None)):
-            cp.start()
-            more.sent.append(cp)
-            more.share(s, None, (-1, 1)[d])
-    more.arrived(2, None)
-    for cp in cps:
-        cp.wait()
-    more.drain()
-
-
-def heads(src, planes):
-    return pl.pallas_call(
-        heads_kernel,
-        name="swap_qkv",
-        out_shape=[sds(src.shape)] + [gather_shape(384)] * 3,
-        in_specs=[HBM] * 4,
-        out_specs=[HBM] * 4,
-        input_output_aliases={1: 1, 2: 2, 3: 3},
-        scratch_shapes=swap_sems("col") + gather_sems(),
-        compiler_params=params(3),
-    )(src, *planes)
+        + [DMA((6,)), DMA((2, 2)), DMA, DMA((NC - 1,)), DMA((NC - 1,)), DMA]
+        + swap_sems("row")
+        + gather_sems(36, 16)
+        + gather_sems(20, 0),
+        compiler_params=params(1),
+    )(target.reshape(1, ROWS), lens, tokens, grads, again, qgain, kgain, freq, *weights)
 
 
 LOG2E = math.log2(math.e)
@@ -780,157 +741,218 @@
     return jnp.concatenate([v[:, :HEAD], v[:, HEAD : 2 * HEAD]], axis=0)
 
 
+SPAN = 5
+
+
 def group_slots(i):
     return i * ROWS + iota((1, QK), 1) % ROWS
 
 
-def first_block(lens, i):
-    start, out = jnp.int32(0), jnp.int32(0)
-    for j in range(8):
-        out = jnp.where(start <= i * ROWS, start, out)
-        start = start + lens[j]
-    return out // ROWS
-
-
-def last_block(lens, j):
-    end, out = jnp.int32(0), jnp.int32(GROUP)
-    for n in range(8):
-        end = end + lens[n]
-        out = jnp.where(end > (j + 1) * ROWS - 1, jnp.minimum(out, end), out)
-    return (out - 1) // ROWS
-
-
 def allowed(i, j, first):
     key = j * ROWS + iota((ROWS, QK), 0)
-    query = i * ROWS + iota((ROWS, QK), 1) % ROWS
-    return (key <= query) & (key >= first)
-
-
-def attend_kernel(lens, qkv, out, o_t, lse):
-    i = pl.program_id(0)
+    return (key <= group_slots(i)) & (key >= first)
+
+
+def attend_kernel(
+    lens, qkv, i0, i1, i2, oa, o_t, lse, f0, f1, f2, o_s, s_v, ssem, rsem, lsem, *sems
+):
+    at = where_am_i()
+    row, col = lax.axis_index("row"), lax.axis_index("col")
+    meet(ring_peers(at) + [device(mate(at))] + col_peers(at))
+    more = Gather(at, (f0, f1, f2), sems, (2,))
+    more.send(2, None)
     scale = HEAD**-0.5 * LOG2E
-    q = stacked(qkv[i, :, 0 : 2 * HEAD])
-    start = first_slots(lambda j: lens[j], group_slots(i))
-
-    def scores(j):
-        s = dot(qkv[j, :, 2 * HEAD : 3 * HEAD], q, NT) * scale
-        return jnp.where(allowed(i, j, start), s, -1e30)
-
-    s = scores(i)
-    m = jnp.max(s, axis=0, keepdims=True)
-    p = jnp.exp2(s - m)
-    total = jnp.sum(p, axis=0, keepdims=True)
-    acc = dot(qkv[i, :, 3 * HEAD :], p.astype(BF), TN)
-
-    def step(d, carry):
-        m, total, acc = carry
-        j = i - 1 - d
-        s = scores(j)
-        m2 = jnp.maximum(m, jnp.max(s, axis=0, keepdims=True))
-        fade = jnp.exp2(m - m2)
-        p = jnp.exp2(s - m2)
-        total = total * fade + jnp.sum(p, axis=0, keepdims=True)
-        acc = acc * fade + dot(qkv[j, :, 3 * HEAD :], p.astype(BF), TN)
-        return m2, total, acc
-
-    m, total, acc = lax.fori_loop(0, i - first_block(lens, i), step, (m, total, acc))
-    o = acc / total
-    o_t[0] = o
-    lse[0] = m + jnp.log2(total)
-    back = o.T
-    out[0] = jnp.concatenate([back[:ROWS], back[ROWS:]], axis=1).astype(BF)
-
-
-def attend(lens, qkv):
+
+    def block_at(n):
+        return (col + 1 + n) % NC
+
+    def sends(n):
+        c = block_at(n)
+        return remote(o_s.at[c], oa.at[col], ssem.at[n], rsem.at[n], (row, c))
+
+    @pl.loop(0, NC)
+    def _(n):
+        i = block_at(n)
+        q = stacked(qkv[i, :, 0 : 2 * HEAD])
+        start = first_slots(lambda j: lens[0, j], group_slots(i))
+        j0 = jnp.maximum(i - (SPAN - 1), 0)
+        m = None
+        for d in range(SPAN):
+            s = dot(qkv[j0 + d, :, 2 * HEAD : 3 * HEAD], q, NT) * scale
+            s = jnp.where(allowed(i, j0 + d, start), s, -1e30)
+            s_v[d] = s
+            top = jnp.max(s, axis=0, keepdims=True)
+            m = top if m is None else jnp.maximum(m, top)
+        total = jnp.zeros((1, QK), F32)
+        acc = jnp.zeros((HEAD, QK), F32)
+        for d in range(SPAN):
+            p = jnp.exp2(s_v[d] - m)
+            total = total + jnp.sum(p, axis=0, keepdims=True)
+            acc = acc + dot(qkv[j0 + d, :, 3 * HEAD :], p.astype(BF), TN)
+        o = acc / total
+        o_t[i] = o
+        lse[i] = m + jnp.log2(total)
+        back = o.T
+        o_s[i] = jnp.concatenate([back[:ROWS], back[ROWS:]], axis=1).astype(BF)
+
+        @pl.when(n < NC - 1)
+        def _():
+            sends(n).start()
+
+        @pl.when(n == NC - 2)
+        def _():
+            more.pass_on(2, None)
+
+    mine = pltpu.make_async_copy(o_s.at[col], oa.at[col], lsem)
+    mine.start()
+    more.arrived(2, None)
+    for n in range(NC - 1):
+        sends(n).wait()
+    mine.wait()
+    for s in range(3):
+        for cp in more.copies(s, 2, None) + more.forwards(s, 2, None):
+            cp.wait_send()
+        for rel in SHIFT:
+            more.to_mate(s, None, rel).wait()
+
+
+def attend(lens, qkv, planes):
     return pl.pallas_call(
         attend_kernel,
         name="attend",
-        grid_spec=pltpu.PrefetchScalarGridSpec(
-            num_scalar_prefetch=1,
-            grid=(NC,),
-            in_specs=[
-                pl.BlockSpec((NC, ROWS, 512), lambda i, lo: (0, 0, 0)),
-            ],
-            out_specs=[
-                pl.BlockSpec((1, ROWS, 256), lambda i, lo: (i, 0, 0)),
-                pl.BlockSpec((1, HEAD, QK), lambda i, lo: (i, 0, 0)),
-                pl.BlockSpec((1, 1, QK), lambda i, lo: (i, 0, 0)),
-            ],
-        ),
         out_shape=[
             sds((NC, ROWS, 256)),
             sds((NC, HEAD, QK), F32),
             sds((NC, 1, QK), F32),
-        ],
-        compiler_params=params(),
-    )(lens, qkv)
-
-
-def attend_back_kernel(lens, qkv, d_o, o_t, lse, out, qs, dos, delta, dq, first):
-    j = pl.program_id(0)
+        ]
+        + [gather_shape(384)] * 3,
+        in_specs=[pl.BlockSpec(memory_space=pltpu.SMEM), VMEM] + [HBM] * 3,
+        out_specs=[HBM, VMEM, VMEM] + [HBM] * 3,
+        input_output_aliases={2: 3, 3: 4, 4: 5},
+        scratch_shapes=[pltpu.VMEM((NC, ROWS, 256), BF), pltpu.VMEM((SPAN, ROWS, QK), F32)]
+        + swap_sems("col")
+        + gather_sems(4, 4),
+        compiler_params=params(2),
+    )(lens, qkv, *planes)
+
+
+def later_shapes():
+    leads = [scatter_leads(s, 0) for s in range(3)]
+    return [sds((2,) + n + (32, 384)) for n in leads], [sds((2,) + n + (64, 384)) for n in leads]
+
+
+def attend_back_kernel(lens, qkv, d_o, o_t, lse, p0, p1, p2, dst, *rest):
+    rel_in, piece_in, rest = rest[0:3], rest[3:6], rest[6:]
+    out_s, qs, dos, delta, dq, first, kv_ssem, kv_rsem, kv_lsem = rest[:9]
+    q_ssem, q_rsem, q_lsem, ssem, rsem, _ = rest[9:]
+    at = where_am_i()
+    row, col = lax.axis_index("row"), lax.axis_index("col")
+    meet(ring_peers(at) + col_peers(at))
+    cps = []
+    for s, p in enumerate((p0, p1, p2)):
+        more = first_sends(s, 0, at, p, rel_in[s], piece_in[s], ssem, rsem)
+        for cp in more:
+            cp.start()
+        cps += more
     scale = HEAD**-0.5
 
-    @pl.when(j == 0)
-    def _():
-        for i in range(NC):
-            qs[i] = stacked(qkv[i, :, 0 : 2 * HEAD])
-            g = stacked(d_o[i])
-            dos[i] = g
-            delta[i] = jnp.sum(g.astype(F32).T * o_t[i], axis=0, keepdims=True)
-            dq[i] = jnp.zeros((HEAD, QK), F32)
-            first[i] = first_slots(lambda n: lens[n], group_slots(i))
-
-    k = qkv[j, :, 2 * HEAD : 3 * HEAD]
-    v = qkv[j, :, 3 * HEAD :]
-    k_t = k.astype(F32).T.astype(BF)
-
-    def step(i, carry):
-        dk, dv = carry
-        s = dot(k, qs[i], NT) * (scale * LOG2E) - lse[i]
-        p = jnp.where(allowed(i, j, first[i]), jnp.exp2(s), 0.0)
-        ds = (p * (dot(v, dos[i], NT) - delta[i]) * scale).astype(BF)
-        dv = dv + dot(p.astype(BF), dos[i])
-        dk = dk + dot(ds, qs[i])
-        dq[i] += dot(k_t, ds)
-        return dk, dv
-
-    zero = jnp.zeros((ROWS, HEAD), F32)
-    dk, dv = lax.fori_loop(j, last_block(lens, j) + 1, step, (zero, zero))
-    done = dq[j].T
-    out[0, :, 0:HEAD] = done[:ROWS].astype(BF)
-    out[0, :, HEAD : 2 * HEAD] = done[ROWS:].astype(BF)
-    out[0, :, 2 * HEAD : 3 * HEAD] = dk.astype(BF)
-    out[0, :, 3 * HEAD :] = dv.astype(BF)
-
-
-def attend_back(lens, qkv, d_o, o_t, lse):
-    def full(shape):
-        return pl.BlockSpec(shape, lambda j, hi: (0,) * len(shape))
-
+    @pl.loop(0, NC)
+    def _(i):
+        qs[i] = stacked(qkv[i, :, 0 : 2 * HEAD])
+        g = stacked(d_o[i])
+        dos[i] = g
+        delta[i] = jnp.sum(g.astype(F32).T * o_t[i], axis=0, keepdims=True)
+        dq[i] = jnp.zeros((HEAD, QK), F32)
+        first[i] = first_slots(lambda n: lens[0, n], group_slots(i))
+
+    def block_at(n):
+        return (col + 1 + n) % NC
+
+    lanes_q, lanes_kv = pl.ds(0, 2 * HEAD), pl.ds(2 * HEAD, 2 * HEAD)
+    whole_rows = (slice(None),)
+
+    def sends(n, lanes, ssem, rsem):
+        c = block_at(n)
+        return remote(
+            out_s.at[(c,) + whole_rows + (lanes,)],
+            dst.at[(col,) + whole_rows + (lanes,)],
+            ssem.at[n],
+            rsem.at[n],
+            (row, c),
+        )
+
+    def keeps(lanes, sem):
+        return pltpu.make_async_copy(
+            out_s.at[(col,) + whole_rows + (lanes,)], dst.at[(col,) + whole_rows + (lanes,)], sem
+        )
+
+    @pl.loop(0, NC)
+    def _(n):
+        j = block_at(n)
+        k = qkv[j, :, 2 * HEAD : 3 * HEAD]
+        v = qkv[j, :, 3 * HEAD :]
+        k_t = k.astype(F32).T.astype(BF)
+
+        def step(i, carry):
+            dk, dv = carry
+            s = dot(k, qs[i], NT) * (scale * LOG2E) - lse[i]
+            p = jnp.where(allowed(i, j, first[i]), jnp.exp2(s), 0.0)
+            ds = (p * (dot(v, dos[i], NT) - delta[i]) * scale).astype(BF)
+            dv = dv + dot(p.astype(BF), dos[i])
+            dk = dk + dot(ds, qs[i])
+            dq[i] += dot(k_t, ds)
+            return dk, dv
+
+        zero = jnp.zeros((ROWS, HEAD), F32)
+        dk, dv = lax.fori_loop(j, jnp.minimum(j + SPAN, NC), step, (zero, zero))
+        out_s[j, :, 2 * HEAD : 3 * HEAD] = dk.astype(BF)
+        out_s[j, :, 3 * HEAD :] = dv.astype(BF)
+
+        @pl.when(n < NC - 1)
+        def _():
+            sends(n, lanes_kv, kv_ssem, kv_rsem).start()
+
+    @pl.loop(0, NC)
+    def _(n):
+        i = block_at(n)
+        done = dq[i].T
+        out_s[i, :, 0:HEAD] = done[:ROWS].astype(BF)
+        out_s[i, :, HEAD : 2 * HEAD] = done[ROWS:].astype(BF)
+
+        @pl.when(n < NC - 1)
+        def _():
+            sends(n, lanes_q, q_ssem, q_rsem).start()
+
+    mine = [keeps(lanes_kv, kv_lsem), keeps(lanes_q, q_lsem)]
+    for cp in mine:
+        cp.start()
+    for cp in mine + cps:
+        cp.wait()
+    for n in range(NC - 1):
+        sends(n, lanes_kv, kv_ssem, kv_rsem).wait()
+        sends(n, lanes_q, q_ssem, q_rsem).wait()
+
+
+def attend_back(lens, qkv, d_o, o_t, lse, parts):
+    rel, piece = later_shapes()
     return pl.pallas_call(
         attend_back_kernel,
         name="attend_back",
-        grid_spec=pltpu.PrefetchScalarGridSpec(
-            num_scalar_prefetch=1,
-            grid=(NC,),
-            in_specs=[
-                full((NC, ROWS, 512)),
-                full((NC, ROWS, 256)),
-                full((NC, HEAD, QK)),
-                full((NC, 1, QK)),
-            ],
-            out_specs=pl.BlockSpec((1, ROWS, 512), lambda j, hi: (j, 0, 0)),
-            scratch_shapes=[
-                pltpu.VMEM((NC, QK, HEAD), BF),
-                pltpu.VMEM((NC, QK, HEAD), BF),
-                pltpu.VMEM((NC, 1, QK), F32),
-                pltpu.VMEM((NC, HEAD, QK), F32),
-                pltpu.VMEM((NC, 1, QK), I32),
-            ],
-        ),
-        out_shape=sds((NC, ROWS, 512)),
-        compiler_params=params(),
-    )(lens, qkv, d_o, o_t, lse)
+        out_shape=[sds((NC, ROWS, 512))] + rel + piece,
+        in_specs=[pl.BlockSpec(memory_space=pltpu.SMEM)] + [VMEM] * 4 + [HBM] * 3,
+        out_specs=[HBM] * 7,
+        scratch_shapes=[
+            pltpu.VMEM((NC, ROWS, 512), BF),
+            pltpu.VMEM((NC, QK, HEAD), BF),
+            pltpu.VMEM((NC, QK, HEAD), BF),
+            pltpu.VMEM((NC, 1, QK), F32),
+            pltpu.VMEM((NC, HEAD, QK), F32),
+            pltpu.VMEM((NC, 1, QK), I32),
+        ]
+        + swap_sems("col") * 2
+        + scatter_sems(1),
+        compiler_params=params(6),
+    )(lens, qkv, d_o, o_t, lse, *parts)
 
 
 def middle_kernel(
@@ -984,8 +1006,7 @@
 
     @pl.when(i == 2 * NC - 1)
     def _():
-        local = slt[...].reshape(ROWS, HEAD)[:, :1] % ROWS
-        take = onehot(local == iota((ROWS, ROWS), 1))
+        take = onehot(slt[:, :1].astype(F32).astype(I32) == iota((ROWS, ROWS), 1))
         out_s[...] = dot(take, acc[...].astype(BF)).astype(BF).reshape(out_s.shape)
         h = h_s[...]
         r2 = mean_square_scale(h)
@@ -1031,7 +1052,7 @@
             sds((1, WIDTH), F32),
         ],
         in_specs=[
-            whole((NR, 16, HEAD)),
+            whole((ROWS, HEAD)),
             whole((ROWS, WIDTH)),
             whole((ROWS, WIDTH)),
             pl.BlockSpec((1, ROWS, 256), lambda i: (jnp.minimum(i, NC - 1), 0, 0)),
@@ -1170,38 +1191,6 @@
     )(n1h, n1_m, dhlh, dhl_m, dqkv, dqkv_m, oa, oa_m)
 
 
-def later_shapes():
-    leads = [scatter_leads(s, 0) for s in range(3)]
-    return [sds((2,) + n + (32, 384)) for n in leads], [sds((2,) + n + (64, 384)) for n in leads]
-
-
-def heads_back_kernel(src, p0, p1, p2, dst, *rest):
-    rel_in, piece_in, sems = rest[0:3], rest[3:6], rest[6:]
-    at = where_am_i()
-    meet(ring_peers(at) + col_peers(at))
-    cps = swap_over("col", src, dst, *sems[:3])
-    for s, p in enumerate((p0, p1, p2)):
-        more = first_sends(s, 0, at, p, rel_in[s], piece_in[s], sems[3], sems[4])
-        for cp in more:
-            cp.start()
-        cps += more
-    for cp in cps:
-        cp.wait()
-
-
-def heads_back(src, parts):
-    rel, piece = later_shapes()
-    return pl.pallas_call(
-        heads_back_kernel,
-        name="swap_dqkv",
-        out_shape=[sds(src.shape)] + rel + piece,
-        in_specs=[HBM] * 4,
-        out_specs=[HBM] * 7,
-        scratch_shapes=swap_sems("col") + scatter_sems()[:2],
-        compiler_params=params(6),
-    )(src, *parts)
-
-
 def project_back_kernel(
     slt, x, dh, again, qgain, kgain, cos, sin, raw, dqkv, wq, wkv, p0, p1, p2, r0, r1, r2, i0, i1, i2,
     d_o, dx_s, gain_o, qk_o, q0, q1, q2, acc, gq, gk, *rest,
@@ -1267,8 +1256,7 @@
         gain_o[...] = jnp.sum(e * xn, axis=0, keepdims=True)
         e = e * again[...]
         dx = dh[...] + r1 * (e - xn * jnp.mean(e * xn, axis=-1, keepdims=True))
-        local = slt[...].reshape(ROWS, HEAD)[:, :1] % ROWS
-        take = onehot(local == iota((ROWS, ROWS), 1))
+        take = onehot(slt[:, :1].astype(F32).astype(I32) == iota((ROWS, ROWS), 1))
         dx_s[...] = dot(take, dx.astype(BF)).astype(BF).reshape(dx_s.shape)
         qk_o[...] = jnp.concatenate([gq[...], gk[...]], axis=1)
         for s in range(3):
@@ -1289,7 +1277,7 @@
         ]
         + later_shapes()[1],
         in_specs=[
-            whole((NR, 16, HEAD)),
+            whole((ROWS, HEAD)),
             whole((ROWS, WIDTH)),
             whole((ROWS, WIDTH)),
             whole((1, WIDTH)),
@@ -1317,7 +1305,7 @@
             pltpu.VMEM((1, HEAD), F32),
         ]
         + [pltpu.VMEM(r.shape, BF) for r in later_shapes()[0]] * 2
-        + scatter_sems(),
+        + scatter_sems(1),
         compiler_params=params(7),
     )(slt, x, dh, again, qgain, kgain, cos, sin, raw, dqkv, wq, wkv, *parts, *rel, *piece)
 
@@ -1437,7 +1425,7 @@
         + [pltpu.VMEM((4, 4, 1, total), F32), DMA((4, 3)), DMA((4, 3))]
         + swap_sems("row")
         + scatter_sems()
-        + scatter_sems(),
+        + scatter_sems(2),
         compiler_params=params(9),
     )(*parts, *sums, dx_s, *gains)
 
@@ -1485,24 +1473,18 @@
 ):
     again, fgain = attn_gain.reshape(1, WIDTH), ffn_gain.reshape(1, WIDTH)
     qgain, kgain = q_gain.reshape(1, HEAD), k_gain.reshape(1, HEAD)
-    lens = lengths[0]
-
-    tok, grd, slt, wq, wkv, wo, *planes = dispatch(
-        target, tokens, grad_out, w_query, key_matrix, value_matrix, w_out.T, w_gate, w_up, w_down.T
+
+    qkv, raw, x, dy, n1h, dyh, cos, sin, slt, wq, wkv, wo, *planes = front(
+        target, lengths, tokens, grad_out, again, qgain, kgain,
+        w_query, key_matrix, value_matrix, w_out.T, w_gate, w_up, w_down.T,
     )
-    qkv, raw, x, dy, n1h, dyh, cos, sin, *planes = project(
-        lengths, slt, tok, grd, again, qgain, kgain, wq, wkv, planes
-    )
-    qkv, wg, wu, wd = heads(qkv, planes)
-    o, o_t, lse = attend(lens, qkv)
-    oa = col_swap(o, 4, "swap_o")
+    oa, o_t, lse, wg, wu, wd = attend(lengths, qkv, planes)
     out_s, dh, dhlh, n2h, act, d_o, gain_f = middle(slt, x, dy, oa, fgain, wo, wg, wu, wd)
     g_o, got_out, act_m, oa_m, n2_m, dy_m, dhl_m = back_swap(
         d_o, out_s, act, oa, n2h, dyh, dhlh
     )
     f_parts = ffn_grads(n2h, n2_m, dyh, dy_m, act, act_m)
-    dqkv = attend_back(lens, qkv, g_o, o_t, lse)
-    dqkv, *later = heads_back(dqkv, f_parts)
+    dqkv, *later = attend_back(lengths, qkv, g_o, o_t, lse, f_parts)
     draw, dx_s, gain_a, gain_qk, *piece = project_back(
         slt, x, dh, again, qgain, kgain, cos, sin, raw, dqkv, wq, wkv,
         f_parts, later[:3], later[3:],

time: 415 us -> 366 us (0.88)
  Pallas kernels: 415 us -> 364 us
    pallas_call x7 -> x3, Pallas kernels: 243 us -> 201 us  [the longest x1 103 us: front(): pl.pallas_call(front_kernel, name='front', out_shape=[sds((NC, ROWS, 512)...]
    pallas_call x1, Pallas kernels: 28.8 us -> 23.6 us  [back_swap(): pl.pallas_call(back_swap_kernel, name='back_swap', out_shape=[sds(d_o.sha...]
where the time goes in v3:
time: 366 us; the launch traced here: 365 us
  Pallas kernels  364 us (99%)
    pallas_call x1, Pallas kernels, front(): pl.pallas_call(front_kernel, name='front', out_shape=[sds((NC, ROWS, 512)...  103 us
    pallas_call x1, Pallas kernels, last(): pl.pallas_call(last_kernel, name='last', out_shape=[sds((64, 256), F32)]...  54.7 us
    pallas_call x1, Pallas kernels, attend_back(): pl.pallas_call(attend_back_kernel, name='attend_back', out_shape=[sds((NC...  50.2 us
    pallas_call x1, Pallas kernels, attend(): pl.pallas_call(attend_kernel, name='attend', out_shape=[sds((NC, ROWS, 25...  48.1 us
    pallas_call x1, Pallas kernels, middle(): pl.pallas_call(middle_kernel, name='middle', grid=(3 * NC,), out_shape=[s...  33.4 us
    pallas_call x1, Pallas kernels, back_swap(): pl.pallas_call(back_swap_kernel, name='back_swap', out_shape=[sds(d_o.sha...  23.6 us
    pallas_call x1, Pallas kernels, project_back(): pl.pallas_call(project_back_kernel, name='project_back', grid=(NC,), out_...  20.9 us
    pallas_call x1, Pallas kernels, ffn_grads(): pl.pallas_call(ffn_grads_kernel, name='ffn_grads', grid=(NC,), out_shape=...  12.4 us

profile of v3, /device:TPU:0, one launch (start us, length us, event | category | flops | bytes accessed | tf_op | source)
XLA Modules:
  0.0 365.2 jit_solution(13033051660853930668)
XLA Ops:
  0.6 102.9 %front.1 = (bf16[8,256,512]{2,1,0:T(8,128)(2,1)}, f32[8,256,384]{2,1,0:T(8,128)}, bf16[256,1024]{1,0:T(8,128)(2,1)}, bf16[256,1024]{1,0:T(8,128)(2,1)}, bf16[2,2...) custom-call(s32[1,256]{1,0:T(1,128)} %bitcast.17, ...), custom_call_target="tpu_custom_call" | custom-call | tf_op jit(solution)/shard_map/front/pallas_call | solution.py:699
  103.5 48.1 %attend.1 = (bf16[8,256,256]{2,1,0:T(8,128)(2,1)}, f32[8,128,512]{2,1,0:T(8,128)}, f32[8,1,512]{2,1,0:T(1,128)}, bf16[4,2,4,2,2,64,384]{6,5,4,3,2,1,0:T(8,128)(2...) custom-call(s32[1,8]{1,0:T(1,128)} %lens.5, ...), custom_call_target="tpu_custom_call", output_to_operand_aliasing={{3}: (2, {}), {4}: (3, {}), {5}: (4, {})} | custom-call | tf_op jit(solution)/shard_map/attend/pallas_call | solution.py:820
  151.6 33.4 %middle.1 = (bf16[16,16,1024]{2,1,0:T(8,128)(2,1)}, f32[256,1024]{1,0:T(8,128)}, bf16[2,256,512]{2,1,0:T(8,128)(2,1)}, bf16[2,256,512]{2,1,0:T(8,128)(2,1)}, bf1...) custom-call(bf16[256,128]{1,0:T(8,128)(2,1)} %get-tuple-element.94.slt, ...), custom_call_target="tpu_custom_call" | custom-call | tf_op jit(solution)/shard_map/middle/pallas_call | solution.py:1041
  185.0 23.6 %back_swap.1 = (bf16[8,256,256]{2,1,0:T(8,128)(2,1)}, bf16[16,16,1024]{2,1,0:T(8,128)(2,1)}, bf16[8,256,1152]{2,1,0:T(8,128)(2,1)}, bf16[8,256,256]{2,1,0:T(8,12...) custom-call(bf16[8,256,256]{2,1,0:T(8,128)(2,1)} %get-tuple-element.106.d_o, ...), custom_call_target="tpu_custom_call" | custom-call | tf_op jit(solution)/shard_map/back_swap/pallas_call | solution.py:1110
  208.7 12.4 %ffn_grads.1 = (bf16[4,2,4,2,64,384]{5,4,3,2,1,0:T(8,128)(2,1)}, bf16[4,2,4,2,64,384]{5,4,3,2,1,0:T(8,128)(2,1)}, bf16[4,2,4,2,64,384]{5,4,3,2,1,0:T(8,128)(2,1)}) custom-call(bf16[2,256,512]{2,1,0:T(8,128)(2,1)} %get-tuple-element.109.n2h, bf16[256,512]{1,0:T(8,128)(2,1)} %get-tuple-element.121.n2_m, bf16[2,256,512]{2,1,0:T(8,128)(2,1)} %get-tuple-element.110.dyh, ...), custom_call_target="tpu_custom_call" | custom-call | tf_op jit(solution)/shard_map/ffn_grads/pallas_call | solution.py:1148
  221.1 50.2 %attend_back.1 = (bf16[8,256,512]{2,1,0:T(8,128)(2,1)}, bf16[2,4,4,32,384]{4,3,2,1,0:T(8,128)(2,1)}, bf16[2,2,4,2,32,384]{5,4,3,2,1,0:T(8,128)(2,1)}, bf16[2,4,2...) custom-call(s32[1,8]{1,0:T(1,128)} %lens.5, ...), custom_call_target="tpu_custom_call" | custom-call | tf_op jit(solution)/shard_map/attend_back/pallas_call | solution.py:938
  271.3 20.9 %project_back.1 = (bf16[8,256,512]{2,1,0:T(8,128)(2,1)}, bf16[16,16,1024]{2,1,0:T(8,128)(2,1)}, f32[1,1024]{1,0:T(1,128)}, f32[1,256]{1,0:T(1,128)}, bf16[2,4,4,...) custom-call(bf16[256,128]{1,0:T(8,128)(2,1)} %get-tuple-element.94.s, ...), custom_call_target="tpu_custom_call", output_to_operand_aliasing={{4}: (18, {}), {5}: (19, {}), {6}: (20, {})} | custom-call | tf_op jit(solution)/shard_map/project_back/pallas_call | solution.py:1268
  292.2 5.1 %core_swap.1 = (bf16[8,256,512]{2,1,0:T(8,128)(2,1)}, bf16[256,512]{1,0:T(8,128)(2,1)}, bf16[4,4,64,384]{3,2,1,0:T(8,128)(2,1)}, bf16[2,4,2,64,384]{4,3,2,1,0:T(8,128)(2,1)}, bf16[4,2,2,64,384]{4,3,2,1,0:T(8,128)(2,1)}) custom-call(bf16[8,256,512]{2,1,0:T(8,128)(2,1)} %get-tuple-element.136.dqkv, bf16[2,256,512]{2,1,0:T(8,128)(2,1)} %get-tuple-element.113.n1h, ...), custom_call_target="tpu_custom_call" | custom-call | tf_op jit(solution)/shard_map/core_swap/pallas_call | solution.py:1349
  297.3 10.1 %attn_grads.1 = (bf16[4,2,4,2,64,256]{5,4,3,2,1,0:T(8,128)(2,1)}, bf16[4,2,4,2,64,256]{5,4,3,2,1,0:T(8,128)(2,1)}, bf16[4,2,4,2,64,256]{5,4,3,2,1,0:T(8,128)(2,1)}) custom-call(bf16[2,256,512]{2,1,0:T(8,128)(2,1)} %get-tuple-element.113.n1h, bf16[256,512]{1,0:T(8,128)(2,1)} %get-tuple-element.140.n1_m, bf16[2,256,512]{2,1,0:T(8,128)(2,1)} %get-tuple-element.111.dhlh, ...), custom_call_target="tpu_custom_call" | custom-call | tf_op jit(solution)/shard_map/attn_grads/pallas_call | solution.py:1181
  307.4 54.7 %last.1 = (f32[64,256]{1,0:T(8,128)}, f32[64,256]{1,0:T(8,128)}, f32[64,256]{1,0:T(8,128)}, f32[64,384]{1,0:T(8,128)}, f32[64,384]{1,0:T(8,128)}, /*index=5*/f32...) custom-call(bf16[4,2,4,2,64,256]{5,4,3,2,1,0:T(8,128)(2,1)} %get-tuple-element.144.p0, ...), custom_call_target="tpu_custom_call" | custom-call | tf_op jit(solution)/shard_map/last/pallas_call | solution.py:1415
  362.0 3.1 arrive.1

commit v4 on v3

--- a/solution.py
+++ b/solution.py
@@ -369,8 +369,9 @@
     return j
 
 
-def run_scatter(at, parts, results, bufs, sems, t0=0):
+def run_scatter(at, parts, results, bufs, sems, resident=False):
     ssem, rsem, lsem = sems
+    t0 = 0
     n = len(parts)
     cur = list(parts)
     waits = []
@@ -384,7 +385,7 @@
             for cp in cps:
                 cp.start()
             loads = []
-            if t == t0:
+            if t == t0 and not resident:
                 for j, (rel, rows, dst) in enumerate(
                     ((1, LO, rel_out.at[0]), (-1, HI, rel_out.at[1]), (0, slice(None), total))
                 ):
@@ -400,7 +401,7 @@
             lead = scatter_leads(s, t)
             for d in range(2):
                 cps[d].wait_recv()
-                if t == t0:
+                if loads:
                     loads[d].wait()
                     mine = (rel_out, side(d))
                 else:
@@ -415,7 +416,7 @@
             lead = scatter_leads(s, t)
             for i in (2, 3, 4, 5):
                 cps[i].wait_recv()
-            if t == t0:
+            if loads:
                 loads[2].wait()
                 mine = (total, same)
             else:
@@ -559,12 +560,12 @@
     return out
 
 
-def slab(w):
-    return pl.BlockSpec((1, 1, 4, 2, 2, 64, w), lambda c: (c % 4, c // 4, 0, 0, 0, 0, 0))
-
-
-def whole(shape):
-    return pl.BlockSpec(shape, lambda *_: (0,) * len(shape))
+def place(c):
+    return (c % 4) * 2 + c // 4
+
+
+def as_slabs(g):
+    return g.reshape(NC, -1, g.shape[-1])
 
 
 def front_kernel(
@@ -836,527 +837,230 @@
     )(lens, qkv, *planes)
 
 
-def later_shapes():
-    leads = [scatter_leads(s, 0) for s in range(3)]
-    return [sds((2,) + n + (32, 384)) for n in leads], [sds((2,) + n + (64, 384)) for n in leads]
-
-
-def attend_back_kernel(lens, qkv, d_o, o_t, lse, p0, p1, p2, dst, *rest):
-    rel_in, piece_in, rest = rest[0:3], rest[3:6], rest[6:]
-    out_s, qs, dos, delta, dq, first, kv_ssem, kv_rsem, kv_lsem = rest[:9]
-    q_ssem, q_rsem, q_lsem, ssem, rsem, _ = rest[9:]
+PAIR = 768
+STEPS = 4
+
+
+def stack_tokens(k, mine, others, scratch):
+    scratch[:, 0:ROWS] = mine[k].astype(F32).T.astype(BF)
+    scratch[:, ROWS:] = others[...].astype(F32).T.astype(BF)
+
+
+def middle_kernel(
+    slt, x, dy, dyh, fgain, oa, wo, wg, wu, wd,
+    dh_o, dhlh, gain_o, g_o, got, oa_m, dhl_m, p0, p1, p2,
+    oa_v, wo_v, w_v, acc, dn2, h_s, n2_s, dhl_s, act, n2h, n2_m, dy_m, do_s, out_s, nt_s, yt_s, g_v,
+    oa_sem, wo_sem, w_sem, g_sem, act_ssem, act_rsem, m_ssem, m_rsem, do_ssem, do_rsem, do_lsem,
+    *row_sems,
+):
     at = where_am_i()
-    row, col = lax.axis_index("row"), lax.axis_index("col")
-    meet(ring_peers(at) + col_peers(at))
-    cps = []
-    for s, p in enumerate((p0, p1, p2)):
-        more = first_sends(s, 0, at, p, rel_in[s], piece_in[s], ssem, rsem)
-        for cp in more:
-            cp.start()
-        cps += more
-    scale = HEAD**-0.5
-
-    @pl.loop(0, NC)
-    def _(i):
-        qs[i] = stacked(qkv[i, :, 0 : 2 * HEAD])
-        g = stacked(d_o[i])
-        dos[i] = g
-        delta[i] = jnp.sum(g.astype(F32).T * o_t[i], axis=0, keepdims=True)
-        dq[i] = jnp.zeros((HEAD, QK), F32)
-        first[i] = first_slots(lambda n: lens[0, n], group_slots(i))
+    row, col, k = lax.axis_index("row"), lax.axis_index("col"), at["k"]
+    to = device(mate(at))
+    lead = []
+    for p in range(NC):
+        c = (p % 2) * 4 + p // 2
+        lanes = pl.ds(256 * p, 256)
+        lead.append(pltpu.make_async_copy(oa.at[c], oa_v.at[:, lanes], oa_sem.at[p]))
+        lead.append(pltpu.make_async_copy(wo.at[p], wo_v.at[:, lanes], wo_sem.at[p]))
+    for cp in lead:
+        cp.start()
+
+    def loads(t):
+        slot = t % 2
+        return [
+            pltpu.make_async_copy(
+                w.at[2 * t + j],
+                w_v.at[slot, :, pl.ds(PAIR * i + 384 * j, 384)],
+                w_sem.at[slot, 2 * i + j],
+            )
+            for i, w in enumerate((wg, wu, wd))
+            for j in range(2)
+        ]
+
+    def act_send(t):
+        rows = pl.ds(0, ROWS), pl.ds(ROWS, ROWS)
+        return remote(act.at[t, rows[0]], act.at[t, rows[1]], act_ssem.at[t], act_rsem.at[t], to)
+
+    def mate_send(i, src, dst):
+        return remote(src, dst, m_ssem.at[i], m_rsem.at[i], to)
+
+    for cp in loads(0):
+        cp.start()
+    meet(col_peers(at) + row_peers(at))
+    to_mate = [mate_send(0, dyh.at[1 - k], dy_m), mate_send(1, oa, oa_m)]
+    for cp in to_mate:
+        cp.start()
+    for cp in lead:
+        cp.wait()
+
+    @pl.loop(0, 4)
+    def _(n):
+        cols = pl.ds(pl.multiple_of(256 * n, 256), 256)
+        acc[:, cols] = x[:, cols].astype(F32) + dot(oa_v[...], wo_v[cols, :], NT)
+
+    h = acc[...]
+    h_s[...] = h
+    n2 = h * mean_square_scale(h) * fgain[...]
+    n2_s[...] = n2.astype(BF)
+    a, b = halves_of(n2)
+    n2h[0] = a.astype(BF)
+    n2h[1] = b.astype(BF)
+    cp = mate_send(2, n2h.at[1 - k], n2_m)
+    cp.start()
+    to_mate.append(cp)
+    dn2[...] = jnp.zeros_like(dn2)
+
+    @pl.loop(0, STEPS)
+    def _(t):
+        slot = t % 2
+
+        @pl.when(t < STEPS - 1)
+        def _():
+            for cp in loads(t + 1):
+                cp.start()
+
+        for cp in loads(t):
+            cp.wait()
+        g = dot(n2_s[...], w_v[slot, :, 0:PAIR])
+        u = dot(n2_s[...], w_v[slot, :, PAIR : 2 * PAIR])
+        dhid = dot(dy[...], w_v[slot, :, 2 * PAIR :])
+        sig = jax.nn.sigmoid(g)
+        silu = g * sig
+        act[t, 0:ROWS, 2 * PAIR :] = (silu * u).astype(BF)
+        act[t, 0:ROWS, 0:PAIR] = (dhid * u * sig * (1.0 + g * (1.0 - sig))).astype(BF)
+        act[t, 0:ROWS, PAIR : 2 * PAIR] = (dhid * silu).astype(BF)
+        act_send(t).start()
+        acc[...] += dot(act[t, 0:ROWS, 2 * PAIR :], w_v[slot, :, 2 * PAIR :], NT)
+        dn2[...] += dot(act[t, 0:ROWS, 0 : 2 * PAIR], w_v[slot, :, 0 : 2 * PAIR], NT)
+
+    h = h_s[...]
+    r2 = mean_square_scale(h)
+    hn = h * r2
+    e = dn2[...]
+    gain_o[...] = jnp.sum(e * hn, axis=0, keepdims=True)
+    e = e * fgain[...]
+    dh = dy[...].astype(F32) + r2 * (e - hn * jnp.mean(e * hn, axis=-1, keepdims=True))
+    dh_o[...] = dh
+    dhl_s[...] = dh.astype(BF)
 
     def block_at(n):
         return (col + 1 + n) % NC
 
-    lanes_q, lanes_kv = pl.ds(0, 2 * HEAD), pl.ds(2 * HEAD, 2 * HEAD)
-    whole_rows = (slice(None),)
-
-    def sends(n, lanes, ssem, rsem):
+    def do_send(n):
         c = block_at(n)
-        return remote(
-            out_s.at[(c,) + whole_rows + (lanes,)],
-            dst.at[(col,) + whole_rows + (lanes,)],
-            ssem.at[n],
-            rsem.at[n],
-            (row, c),
-        )
-
-    def keeps(lanes, sem):
-        return pltpu.make_async_copy(
-            out_s.at[(col,) + whole_rows + (lanes,)], dst.at[(col,) + whole_rows + (lanes,)], sem
-        )
+        return remote(do_s.at[c], g_o.at[col], do_ssem.at[n], do_rsem.at[n], (row, c))
 
     @pl.loop(0, NC)
     def _(n):
-        j = block_at(n)
-        k = qkv[j, :, 2 * HEAD : 3 * HEAD]
-        v = qkv[j, :, 3 * HEAD :]
-        k_t = k.astype(F32).T.astype(BF)
-
-        def step(i, carry):
-            dk, dv = carry
-            s = dot(k, qs[i], NT) * (scale * LOG2E) - lse[i]
-            p = jnp.where(allowed(i, j, first[i]), jnp.exp2(s), 0.0)
-            ds = (p * (dot(v, dos[i], NT) - delta[i]) * scale).astype(BF)
-            dv = dv + dot(p.astype(BF), dos[i])
-            dk = dk + dot(ds, qs[i])
-            dq[i] += dot(k_t, ds)
-            return dk, dv
-
-        zero = jnp.zeros((ROWS, HEAD), F32)
-        dk, dv = lax.fori_loop(j, jnp.minimum(j + SPAN, NC), step, (zero, zero))
-        out_s[j, :, 2 * HEAD : 3 * HEAD] = dk.astype(BF)
-        out_s[j, :, 3 * HEAD :] = dv.astype(BF)
+        c = block_at(n)
+        cols = pl.ds(pl.multiple_of(256 * place(c), 256), 256)
+        do_s[c] = dot(dhl_s[...], wo_v[:, cols]).astype(BF)
 
         @pl.when(n < NC - 1)
         def _():
-            sends(n, lanes_kv, kv_ssem, kv_rsem).start()
-
-    @pl.loop(0, NC)
-    def _(n):
-        i = block_at(n)
-        done = dq[i].T
-        out_s[i, :, 0:HEAD] = done[:ROWS].astype(BF)
-        out_s[i, :, HEAD : 2 * HEAD] = done[ROWS:].astype(BF)
-
-        @pl.when(n < NC - 1)
+            do_send(n).start()
+
+    mine = pltpu.make_async_copy(do_s.at[col], g_o.at[col], do_lsem)
+    mine.start()
+    take = onehot(slt[:, :1].astype(F32).astype(I32) == iota((ROWS, ROWS), 1))
+    out_s[...] = dot(take, acc[...].astype(BF)).astype(BF).reshape(out_s.shape)
+    back = swap_over("row", out_s, got, *row_sems)
+    a, b = halves_of(dhl_s[...].astype(F32))
+    dhlh[0] = a.astype(BF)
+    dhlh[1] = b.astype(BF)
+    cp = mate_send(3, dhlh.at[1 - k], dhl_m)
+    cp.start()
+    to_mate.append(cp)
+    for cp in to_mate:
+        cp.wait()
+    stack_tokens(k, n2h, n2_m, nt_s)
+    stack_tokens(k, dyh, dy_m, yt_s)
+
+    def stores(t):
+        slot = t % 2
+        return [
+            pltpu.make_async_copy(
+                g_v.at[slot, :, pl.ds(PAIR * i + 384 * j, 384)],
+                p.at[2 * t + j],
+                g_sem.at[slot, 2 * i + j],
+            )
+            for i, p in enumerate((p0, p1, p2))
+            for j in range(2)
+        ]
+
+    @pl.loop(0, STEPS)
+    def _(t):
+        slot = t % 2
+
+        @pl.when(t >= 2)
         def _():
-            sends(n, lanes_q, q_ssem, q_rsem).start()
-
-    mine = [keeps(lanes_kv, kv_lsem), keeps(lanes_q, q_lsem)]
-    for cp in mine:
-        cp.start()
-    for cp in mine + cps:
+            for cp in stores(t - 2):
+                cp.wait()
+
+        act_send(t).wait()
+        gu = 2 * PAIR
+        g_v[slot, :, 0:gu] = dot(nt_s[...], act[t, :, 0:gu]).astype(BF)
+        g_v[slot, :, gu:] = dot(yt_s[...], act[t, :, gu:]).astype(BF)
+        for cp in stores(t):
+            cp.start()
+
+    for t in (STEPS - 2, STEPS - 1):
+        for cp in stores(t):
+            cp.wait()
+    for n in range(NC - 1):
+        do_send(n).wait()
+    for cp in [mine] + back:
         cp.wait()
-    for n in range(NC - 1):
-        sends(n, lanes_kv, kv_ssem, kv_rsem).wait()
-        sends(n, lanes_q, q_ssem, q_rsem).wait()
-
-
-def attend_back(lens, qkv, d_o, o_t, lse, parts):
-    rel, piece = later_shapes()
-    return pl.pallas_call(
-        attend_back_kernel,
-        name="attend_back",
-        out_shape=[sds((NC, ROWS, 512))] + rel + piece,
-        in_specs=[pl.BlockSpec(memory_space=pltpu.SMEM)] + [VMEM] * 4 + [HBM] * 3,
-        out_specs=[HBM] * 7,
-        scratch_shapes=[
-            pltpu.VMEM((NC, ROWS, 512), BF),
-            pltpu.VMEM((NC, QK, HEAD), BF),
-            pltpu.VMEM((NC, QK, HEAD), BF),
-            pltpu.VMEM((NC, 1, QK), F32),
-            pltpu.VMEM((NC, HEAD, QK), F32),
-            pltpu.VMEM((NC, 1, QK), I32),
-        ]
-        + swap_sems("col") * 2
-        + scatter_sems(1),
-        compiler_params=params(6),
-    )(lens, qkv, d_o, o_t, lse, *parts)
-
-
-def middle_kernel(
-    slt, x, dy, oa, fgain, wo, wg, wu, wd,
-    out_s, dh_o, dhlh, n2h, act, d_o, gain_o,
-    h_s, n2_s, acc, dn2, dhl_s,
-):
-    i = pl.program_id(0)
-
-    @pl.when(i < NC)
-    def _():
-        part = dot(oa[0], wo[0, 0].reshape(WIDTH, 256), NT)
-
-        @pl.when(i == 0)
-        def _():
-            acc[...] = x[...].astype(F32) + part
-
-        @pl.when(i > 0)
-        def _():
-            acc[...] += part
-
-    @pl.when(i == NC)
-    def _():
-        h = acc[...]
-        h_s[...] = h
-        n2 = h * mean_square_scale(h) * fgain[...]
-        n2_s[...] = n2.astype(BF)
-        a, b = halves_of(n2)
-        n2h[0] = a.astype(BF)
-        n2h[1] = b.astype(BF)
-        dn2[...] = jnp.zeros_like(dn2)
-
-    @pl.when((i >= NC) & (i < 2 * NC))
-    def _():
-        g_w = wg[0, 0].reshape(WIDTH, 384)
-        u_w = wu[0, 0].reshape(WIDTH, 384)
-        d_w = wd[0, 0].reshape(WIDTH, 384)
-        g = dot(n2_s[...], g_w)
-        u = dot(n2_s[...], u_w)
-        dhid = dot(dy[...], d_w)
-        sig = jax.nn.sigmoid(g)
-        silu = g * sig
-        hid = (silu * u).astype(BF)
-        dg = (dhid * u * sig * (1.0 + g * (1.0 - sig))).astype(BF)
-        du = (dhid * silu).astype(BF)
-        act[0, :, 0:384] = dg
-        act[0, :, 384:768] = du
-        act[0, :, 768:] = hid
-        acc[...] += dot(hid, d_w, NT)
-        dn2[...] += dot(dg, g_w, NT) + dot(du, u_w, NT)
-
-    @pl.when(i == 2 * NC - 1)
-    def _():
-        take = onehot(slt[:, :1].astype(F32).astype(I32) == iota((ROWS, ROWS), 1))
-        out_s[...] = dot(take, acc[...].astype(BF)).astype(BF).reshape(out_s.shape)
-        h = h_s[...]
-        r2 = mean_square_scale(h)
-        hn = h * r2
-        e = dn2[...]
-        gain_o[...] = jnp.sum(e * hn, axis=0, keepdims=True)
-        e = e * fgain[...]
-        dh = dy[...].astype(F32) + r2 * (e - hn * jnp.mean(e * hn, axis=-1, keepdims=True))
-        dh_o[...] = dh
-        dhl_s[...] = dh.astype(BF)
-        a, b = halves_of(dh)
-        dhlh[0] = a.astype(BF)
-        dhlh[1] = b.astype(BF)
-
-    @pl.when(i >= 2 * NC)
-    def _():
-        d_o[0] = dot(dhl_s[...], wo[0, 0].reshape(WIDTH, 256)).astype(BF)
-
-
-def middle(slt, x, dy, oa, fgain, wo, wg, wu, wd):
-    def ffn(w):
-        def at(i):
-            c = jnp.clip(i - NC, 0, NC - 1)
-            return (c % 4, c // 4, 0, 0, 0, 0, 0)
-
-        return pl.BlockSpec((1, 1, 4, 2, 2, 64, w), at)
-
-    def out_at(i):
-        c = jnp.where(i < NC, i, jnp.where(i < 2 * NC, NC - 1, i - 2 * NC))
-        return (c % 4, c // 4, 0, 0, 0, 0, 0)
-
+
+
+def middle(slt, x, dy, dyh, fgain, oa, wo, wg, wu, wd):
+    vm = pltpu.VMEM
     return pl.pallas_call(
         middle_kernel,
         name="middle",
-        grid=(3 * NC,),
         out_shape=[
-            sds((NR, 16, WIDTH)),
             sds((ROWS, WIDTH), F32),
             sds((2, ROWS, 512)),
-            sds((2, ROWS, 512)),
-            sds((NC, ROWS, 1152)),
+            sds((1, WIDTH), F32),
             sds((NC, ROWS, 256)),
-            sds((1, WIDTH), F32),
-        ],
-        in_specs=[
-            whole((ROWS, HEAD)),
-            whole((ROWS, WIDTH)),
-            whole((ROWS, WIDTH)),
-            pl.BlockSpec((1, ROWS, 256), lambda i: (jnp.minimum(i, NC - 1), 0, 0)),
-            whole((1, WIDTH)),
-            pl.BlockSpec((1, 1, 4, 2, 2, 64, 256), out_at),
-            ffn(384),
-            ffn(384),
-            ffn(384),
-        ],
-        out_specs=[
-            whole((NR, 16, WIDTH)),
-            whole((ROWS, WIDTH)),
-            whole((2, ROWS, 512)),
-            whole((2, ROWS, 512)),
-            pl.BlockSpec((1, ROWS, 1152), lambda i: (jnp.clip(i - NC, 0, NC - 1), 0, 0)),
-            pl.BlockSpec((1, ROWS, 256), lambda i: (jnp.maximum(i - 2 * NC, 0), 0, 0)),
-            whole((1, WIDTH)),
-        ],
+            sds((NR, 16, WIDTH)),
+            sds((NC, ROWS, 256)),
+            sds((ROWS, 512)),
+        ]
+        + [sds((NC, 512, 384))] * 3,
+        in_specs=[VMEM] * 5 + [HBM] * 5,
+        out_specs=[VMEM] * 3 + [HBM] * 7,
         scratch_shapes=[
-            pltpu.VMEM((ROWS, WIDTH), F32),
-            pltpu.VMEM((ROWS, WIDTH), BF),
-            pltpu.VMEM((ROWS, WIDTH), F32),
-            pltpu.VMEM((ROWS, WIDTH), F32),
-            pltpu.VMEM((ROWS, WIDTH), BF),
-        ],
-        compiler_params=params(),
-    )(slt, x, dy, oa, fgain, wo, wg, wu, wd)
-
-
-def back_swap_kernel(d_o, out_s, act, oa, n2h, dyh, dhlh, *rest):
-    outs, sems = rest[:7], rest[7:]
-    g_o, got, act_m, oa_m, n2_m, dy_m, dhl_m = outs
-    at = where_am_i()
-    meet(col_peers(at) + row_peers(at))
-    cps = swap_over("col", d_o, g_o, *sems[0:3])
-    to = device(mate(at))
-    other = 1 - at["k"]
-    pairs = (
-        (act, act_m),
-        (oa, oa_m),
-        (n2h.at[other], n2_m),
-        (dyh.at[other], dy_m),
-        (dhlh.at[other], dhl_m),
-    )
-    for i, (src, dst) in enumerate(pairs):
-        cp = remote(src, dst, sems[6].at[i], sems[7].at[i], to)
-        cp.start()
-        cps.append(cp)
-    cps += swap_over("row", out_s, got, *sems[3:6])
-    for cp in cps:
-        cp.wait()
-
-
-def back_swap(d_o, out_s, act, oa, n2h, dyh, dhlh):
-    return pl.pallas_call(
-        back_swap_kernel,
-        name="back_swap",
-        out_shape=[sds(d_o.shape), sds(out_s.shape), sds(act.shape), sds(oa.shape)]
-        + [sds((ROWS, 512))] * 3,
-        in_specs=[HBM] * 7,
-        out_specs=[HBM] * 7,
-        scratch_shapes=swap_sems("col") + swap_sems("row") + [DMA((5,)), DMA((5,))],
+            vm((ROWS, 2048), BF),
+            vm((WIDTH, 2048), BF),
+            vm((2, WIDTH, 3 * PAIR), BF),
+            vm((ROWS, WIDTH), F32),
+            vm((ROWS, WIDTH), F32),
+            vm((ROWS, WIDTH), F32),
+            vm((ROWS, WIDTH), BF),
+            vm((ROWS, WIDTH), BF),
+            vm((STEPS, 2 * ROWS, 3 * PAIR), BF),
+            vm((2, ROWS, 512), BF),
+            vm((ROWS, 512), BF),
+            vm((ROWS, 512), BF),
+            vm((NC, ROWS, 256), BF),
+            vm((NR, 16, WIDTH), BF),
+            vm((512, 2 * ROWS), BF),
+            vm((512, 2 * ROWS), BF),
+            vm((2, 512, 3 * PAIR), BF),
+            DMA((NC,)),
+            DMA((NC,)),
+            DMA((2, 6)),
+            DMA((2, 6)),
+            DMA((STEPS,)),
+            DMA((STEPS,)),
+            DMA((4,)),
+            DMA((4,)),
+        ]
+        + swap_sems("col")
+        + swap_sems("row"),
         compiler_params=params(5),
-    )(d_o, out_s, act, oa, n2h, dyh, dhlh)
-
-
-def stack_tokens(k, mine, others, scratch):
-    scratch[:, 0:ROWS] = mine[k].astype(F32).T.astype(BF)
-    scratch[:, ROWS:] = others[...].astype(F32).T.astype(BF)
-
-
-def ffn_grads_kernel(n2h, n2_m, dyh, dy_m, act, act_m, g0, g1, g2, n_s, y_s):
-    c = pl.program_id(0)
-
-    @pl.when(c == 0)
-    def _():
-        k = lax.axis_index("row") % 2
-        stack_tokens(k, n2h, n2_m, n_s)
-        stack_tokens(k, dyh, dy_m, y_s)
-
-    for i, (lhs, out) in enumerate(((n_s, g0), (n_s, g1), (y_s, g2))):
-        cols = slice(384 * i, 384 * i + 384)
-        rhs = jnp.concatenate([act[0, :, cols], act_m[0, :, cols]], axis=0)
-        out[0, 0] = dot(lhs[...], rhs).astype(BF).reshape(4, 2, 64, 384)
-
-
-def grad_slab(w):
-    return pl.BlockSpec((1, 1, 4, 2, 64, w), lambda c: (c % 4, c // 4, 0, 0, 0, 0))
-
-
-def ffn_grads(n2h, n2_m, dyh, dy_m, act, act_m):
-    one = pl.BlockSpec((1, ROWS, 1152), lambda c: (c, 0, 0))
-    return pl.pallas_call(
-        ffn_grads_kernel,
-        name="ffn_grads",
-        grid=(NC,),
-        out_shape=[sds((4, 2, 4, 2, 64, 384))] * 3,
-        in_specs=[whole((2, ROWS, 512)), whole((ROWS, 512))] * 2 + [one, one],
-        out_specs=[grad_slab(384)] * 3,
-        scratch_shapes=[pltpu.VMEM((512, 2 * ROWS), BF)] * 2,
-        compiler_params=params(),
-    )(n2h, n2_m, dyh, dy_m, act, act_m)
-
-
-def attn_grads_kernel(n1h, n1_m, dhlh, dhl_m, dqkv, dqkv_m, oa, oa_m, g0, g1, g2, n_s, h_s):
-    c = pl.program_id(0)
-
-    @pl.when(c == 0)
-    def _():
-        k = lax.axis_index("row") % 2
-        stack_tokens(k, n1h, n1_m, n_s)
-        stack_tokens(k, dhlh, dhl_m, h_s)
-
-    for i, (lhs, mine, others, out) in enumerate(
-        ((n_s, dqkv, dqkv_m, g0), (n_s, dqkv, dqkv_m, g1), (h_s, oa, oa_m, g2))
-    ):
-        cols = slice(256 * i, 256 * i + 256) if i < 2 else slice(0, 256)
-        rhs = jnp.concatenate([mine[0, :, cols], others[0, :, cols]], axis=0)
-        out[0, 0] = dot(lhs[...], rhs).astype(BF).reshape(4, 2, 64, 256)
-
-
-def attn_grads(n1h, n1_m, dhlh, dhl_m, dqkv, dqkv_m, oa, oa_m):
-    def one(w):
-        return pl.BlockSpec((1, ROWS, w), lambda c: (c, 0, 0))
-
-    return pl.pallas_call(
-        attn_grads_kernel,
-        name="attn_grads",
-        grid=(NC,),
-        out_shape=[sds((4, 2, 4, 2, 64, 256))] * 3,
-        in_specs=[whole((2, ROWS, 512)), whole((ROWS, 512))] * 2
-        + [one(512), one(512), one(256), one(256)],
-        out_specs=[grad_slab(256)] * 3,
-        scratch_shapes=[pltpu.VMEM((512, 2 * ROWS), BF)] * 2,
-        compiler_params=params(),
-    )(n1h, n1_m, dhlh, dhl_m, dqkv, dqkv_m, oa, oa_m)
-
-
-def project_back_kernel(
-    slt, x, dh, again, qgain, kgain, cos, sin, raw, dqkv, wq, wkv, p0, p1, p2, r0, r1, r2, i0, i1, i2,
-    d_o, dx_s, gain_o, qk_o, q0, q1, q2, acc, gq, gk, *rest,
-):
-    c = pl.program_id(0)
-    at = where_am_i()
-    rel_v, own_v, (ssem, rsem, lsem) = rest[0:3], rest[3:6], rest[6:]
-    parts, rel_in, piece_in = (p0, p1, p2), (r0, r1, r2), (q0, q1, q2)
-
-    def loads(s):
-        out = [pltpu.make_async_copy(rel_in[s], rel_v[s], lsem.at[s, 0])]
-        for d, (rel, rows) in enumerate(((1, LO), (-1, HI))):
-            src = parts[s].at[part_of(s, 0, at, rel, rows)]
-            out.append(pltpu.make_async_copy(src, own_v[s].at[d], lsem.at[s, 1 + d]))
-        return out
-
-    def sends(s):
-        return [second_send(s, 0, at, d, own_v[s], piece_in[s], ssem, rsem) for d in range(2)]
-
-    @pl.when(c == 0)
-    def _():
-        for s in range(3):
-            for cp in loads(s):
-                cp.start()
-        meet(ring_peers(at))
-
-    @pl.when(c == 1)
-    def _():
-        for s in range(3):
-            for cp in loads(s):
-                cp.wait()
-            lead = (2,) + scatter_leads(s, 0)
-            add_blocks(lead, (own_v[s], same), [(own_v[s], same), (rel_v[s], same)])
-            for cp in sends(s):
-                cp.start()
-
-    @pl.when(c == 0)
-    def _():
-        acc[...] = jnp.zeros_like(acc)
-        gq[...] = jnp.zeros_like(gq)
-        gk[...] = jnp.zeros_like(gk)
-
-    for i, (gain, g_acc) in enumerate(((qgain, gq), (qgain, gq), (kgain, gk))):
-        cols = slice(i * HEAD, (i + 1) * HEAD)
-        v = raw[0, :, cols]
-        r = mean_square_scale(v)
-        xn = v * r
-        dn = unrope(dqkv[0, :, cols].astype(F32), cos[...], sin[...])
-        g_acc[...] += jnp.sum(dn * xn, axis=0, keepdims=True)
-        e = dn * gain[...]
-        d_o[0, :, cols] = (r * (e - xn * jnp.mean(e * xn, axis=-1, keepdims=True))).astype(BF)
-    d_o[0, :, 3 * HEAD :] = dqkv[0, :, 3 * HEAD :]
-    acc[...] += dot(d_o[0, :, 0:256], wq[0, 0].reshape(WIDTH, 256), NT) + dot(
-        d_o[0, :, 256:512], wkv[0, 0].reshape(WIDTH, 256), NT
-    )
-
-    @pl.when(c == NC - 1)
-    def _():
-        xv = x[...].astype(F32)
-        r1 = mean_square_scale(xv)
-        xn = xv * r1
-        e = acc[...]
-        gain_o[...] = jnp.sum(e * xn, axis=0, keepdims=True)
-        e = e * again[...]
-        dx = dh[...] + r1 * (e - xn * jnp.mean(e * xn, axis=-1, keepdims=True))
-        take = onehot(slt[:, :1].astype(F32).astype(I32) == iota((ROWS, ROWS), 1))
-        dx_s[...] = dot(take, dx.astype(BF)).astype(BF).reshape(dx_s.shape)
-        qk_o[...] = jnp.concatenate([gq[...], gk[...]], axis=1)
-        for s in range(3):
-            for cp in sends(s):
-                cp.wait()
-
-
-def project_back(slt, x, dh, again, qgain, kgain, cos, sin, raw, dqkv, wq, wkv, parts, rel, piece):
-    return pl.pallas_call(
-        project_back_kernel,
-        name="project_back",
-        grid=(NC,),
-        out_shape=[
-            sds((NC, ROWS, 512)),
-            sds((NR, 16, WIDTH)),
-            sds((1, WIDTH), F32),
-            sds((1, 2 * HEAD), F32),
-        ]
-        + later_shapes()[1],
-        in_specs=[
-            whole((ROWS, HEAD)),
-            whole((ROWS, WIDTH)),
-            whole((ROWS, WIDTH)),
-            whole((1, WIDTH)),
-            whole((1, HEAD)),
-            whole((1, HEAD)),
-            whole((ROWS, HEAD)),
-            whole((ROWS, HEAD)),
-            pl.BlockSpec((1, ROWS, 384), lambda c: (c, 0, 0)),
-            pl.BlockSpec((1, ROWS, 512), lambda c: (c, 0, 0)),
-            slab(256),
-            slab(256),
-        ]
-        + [HBM] * 9,
-        out_specs=[
-            pl.BlockSpec((1, ROWS, 512), lambda c: (c, 0, 0)),
-            whole((NR, 16, WIDTH)),
-            whole((1, WIDTH)),
-            whole((1, 2 * HEAD)),
-        ]
-        + [HBM] * 3,
-        input_output_aliases={18: 4, 19: 5, 20: 6},
-        scratch_shapes=[
-            pltpu.VMEM((ROWS, WIDTH), F32),
-            pltpu.VMEM((1, HEAD), F32),
-            pltpu.VMEM((1, HEAD), F32),
-        ]
-        + [pltpu.VMEM(r.shape, BF) for r in later_shapes()[0]] * 2
-        + scatter_sems(1),
-        compiler_params=params(7),
-    )(slt, x, dh, again, qgain, kgain, cos, sin, raw, dqkv, wq, wkv, *parts, *rel, *piece)
-
-
-def core_swap_kernel(dqkv, n1h, p0, p1, p2, q0, q1, q2, dqkv_m, n1_m, s0, s1, s2, *rest):
-    own_v, piece_v, (ssem, rsem, lsem, osem) = rest[0:3], rest[3:6], rest[6:]
-    at = where_am_i()
-    loads = []
-    for s, (p, q) in enumerate(((p0, q0), (p1, q1), (p2, q2))):
-        src = p.at[part_of(s, 0, at, 0, slice(None))]
-        pair = [
-            pltpu.make_async_copy(src, own_v[s], lsem.at[s, 0]),
-            pltpu.make_async_copy(q, piece_v[s], lsem.at[s, 1]),
-        ]
-        for cp in pair:
-            cp.start()
-        loads.append(pair)
-    to = device(mate(at))
-    meet([to])
-    cps = [
-        remote(dqkv, dqkv_m, ssem.at[0], rsem.at[0], to),
-        remote(n1h.at[1 - at["k"]], n1_m, ssem.at[1], rsem.at[1], to),
-    ]
-    for cp in cps:
-        cp.start()
-    for s, out in enumerate((s0, s1, s2)):
-        for cp in loads[s]:
-            cp.wait()
-        lead = scatter_leads(s, 0)
-        terms = [(own_v[s], same), (piece_v[s], side(0)), (piece_v[s], side(1))]
-        add_blocks(lead, (own_v[s], same), terms)
-        cp = pltpu.make_async_copy(own_v[s], out, osem.at[s])
-        cp.start()
-        cps.append(cp)
-    for cp in cps:
-        cp.wait()
-
-
-def core_swap(dqkv, n1h, parts, piece):
-    sums = [sds(scatter_leads(s, 0) + (64, 384)) for s in range(3)]
-    return pl.pallas_call(
-        core_swap_kernel,
-        name="core_swap",
-        out_shape=[sds(dqkv.shape), sds((ROWS, 512))] + sums,
-        in_specs=[HBM] * 8,
-        out_specs=[HBM] * 5,
-        scratch_shapes=[pltpu.VMEM(r.shape, BF) for r in sums]
-        + [pltpu.VMEM(r.shape, BF) for r in later_shapes()[1]]
-        + [DMA((2,)), DMA((2,)), DMA((3, 2)), DMA((3,))],
-        compiler_params=params(8),
-    )(dqkv, n1h, *parts, *piece)
+    )(slt, x, dy, dyh, fgain, oa, *map(as_slabs, (wo, wg, wu, wd)))
 
 
 def gain_steps(at, pieces, room, total, ssem, rsem):
@@ -1386,48 +1090,268 @@
         total[...] = acc
 
 
-def last_kernel(
-    p0, p1, p2, s0, s1, s2, dx_s, ga, gf, gqk, r0, r1, r2, t0, t1, t2, got, gsum, *scratch
+def back_kernel(
+    lens, qkv, d_o, o_t, lse, slt, x, dh, again, qgain, kgain, cos, sin, gain_f, n1h, dhlh, dhl_m,
+    raw, wq, wkv, oa, oa_m, p0, p1, p2,
+    r0, r1, r2, t0, t1, t2, got, gsum,
+    out_s, qs, dos, delta, dq, first, came, draw, w_v, raw_v, acc, dx_s, gain_a, gain_qk,
+    n1_m, nt_s, ht_s, oa_v, a0, a1, a2, room,
+    kv_ssem, kv_rsem, kv_lsem, q_ssem, q_rsem, q_lsem, w_sem, m_ssem, m_rsem, n_ssem, n_rsem, oa_sem,
+    g_ssem, g_rsem, *rest,
 ):
-    na, nf = len(scatter_buffers(256)), len(scatter_buffers(384, 1))
-    bufs, more, rest = scratch[:na], scratch[na : na + nf], scratch[na + nf :]
     at = where_am_i()
-    far = [device(moved(at, a, 2)) for a in "xyz"]
-    meet(ring_peers(at) + far + row_peers(at))
-    cps = []
-
-    def rows():
-        yield
-        cps.extend(swap_over("row", dx_s, got, *rest[3:6]))
+    row, col, k = lax.axis_index("row"), lax.axis_index("col"), at["k"]
+    to = device(mate(at))
+    row_sems, rest = rest[:3], rest[3:]
+    a_sems, f_sems, rest = rest[:3], rest[3:6], rest[6:]
+    na = len(scatter_buffers(256))
+    a_bufs, f_bufs = rest[:na], rest[na:]
+    near = [device(moved(at, "z", 1)), device(moved(at, "z", -1))]
+    meet(near + row_peers(at) + col_peers(at))
+    ffn = run_scatter(at, (p0, p1, p2), (t0, t1, t2), f_bufs, f_sems)
+    next(ffn)
+    swap_n1 = remote(n1h.at[1 - k], n1_m, n_ssem, n_rsem, to)
+    swap_n1.start()
+
+    scale = HEAD**-0.5
+
+    @pl.loop(0, NC)
+    def _(i):
+        qs[i] = stacked(qkv[i, :, 0 : 2 * HEAD])
+        g = stacked(d_o[i])
+        dos[i] = g
+        delta[i] = jnp.sum(g.astype(F32).T * o_t[i], axis=0, keepdims=True)
+        dq[i] = jnp.zeros((HEAD, QK), F32)
+        first[i] = first_slots(lambda n: lens[0, n], group_slots(i))
+
+    def block_at(n):
+        return (col + 1 + n) % NC
+
+    lanes_q, lanes_kv = pl.ds(0, 2 * HEAD), pl.ds(2 * HEAD, 2 * HEAD)
+    every = (slice(None),)
+
+    def sends(n, lanes, ssem, rsem):
+        c = block_at(n)
+        src, dst = out_s.at[(c,) + every + (lanes,)], came.at[(col,) + every + (lanes,)]
+        return remote(src, dst, ssem.at[n], rsem.at[n], (row, c))
+
+    def sends_kv(n):
+        return sends(n, lanes_kv, kv_ssem, kv_rsem)
+
+    def sends_q(n):
+        return sends(n, lanes_q, q_ssem, q_rsem)
+
+    def keys(n):
+        j = block_at(n)
+        key = qkv[j, :, 2 * HEAD : 3 * HEAD]
+        value = qkv[j, :, 3 * HEAD :]
+        key_t = key.astype(F32).T.astype(BF)
+
+        def step(i, carry):
+            dk, dv = carry
+            s = dot(key, qs[i], NT) * (scale * LOG2E) - lse[i]
+            p = jnp.where(allowed(i, j, first[i]), jnp.exp2(s), 0.0)
+            ds = (p * (dot(value, dos[i], NT) - delta[i]) * scale).astype(BF)
+            dv = dv + dot(p.astype(BF), dos[i])
+            dk = dk + dot(ds, qs[i])
+            dq[i] += dot(key_t, ds)
+            return dk, dv
+
+        zero = jnp.zeros((ROWS, HEAD), F32)
+        dk, dv = lax.fori_loop(j, jnp.minimum(j + SPAN, NC), step, (zero, zero))
+        out_s[j, :, 2 * HEAD : 3 * HEAD] = dk.astype(BF)
+        out_s[j, :, 3 * HEAD :] = dv.astype(BF)
+
+        @pl.when(n < NC - 1)
+        def _():
+            sends_kv(n).start()
+
+    pl.loop(0, 6)(keys)
+    next(ffn)
+    pl.loop(6, NC)(keys)
+
+    @pl.loop(0, NC)
+    def _(n):
+        i = block_at(n)
+        done = dq[i].T
+        out_s[i, :, 0:HEAD] = done[:ROWS].astype(BF)
+        out_s[i, :, HEAD : 2 * HEAD] = done[ROWS:].astype(BF)
+
+        @pl.when(n < NC - 1)
+        def _():
+            sends_q(n).start()
+
+    mine = []
+    for lanes, sem in ((lanes_kv, kv_lsem), (lanes_q, q_lsem)):
+        here = (col,) + every + (lanes,)
+        mine.append(pltpu.make_async_copy(out_s.at[here], came.at[here], sem))
+    for cp in mine:
+        cp.start()
+
+    def comes_from(n):
+        return (col - 1 - n + NC) % NC
+
+    def loads(n):
+        c, slot = comes_from(n), n % 2
+        return [
+            pltpu.make_async_copy(wq.at[place(c)], w_v.at[slot, :, pl.ds(0, 256)], w_sem.at[0, slot]),
+            pltpu.make_async_copy(
+                wkv.at[place(c)], w_v.at[slot, :, pl.ds(256, 256)], w_sem.at[1, slot]
+            ),
+            pltpu.make_async_copy(raw.at[c], raw_v.at[slot], w_sem.at[2, slot]),
+        ]
+
+    def to_mate(n):
+        c = comes_from(n)
+        src, dst = draw.at[c, pl.ds(0, ROWS)], draw.at[c, pl.ds(ROWS, ROWS)]
+        return remote(src, dst, m_ssem.at[n], m_rsem.at[n], to)
+
+    for cp in loads(0):
+        cp.start()
+    next(ffn)
+    acc[...] = jnp.zeros_like(acc)
+    gain_qk[...] = jnp.zeros_like(gain_qk)
+
+    def columns(n):
+        c, slot = comes_from(n), n % 2
+
+        @pl.when(n < NC - 1)
+        def _():
+            for cp in loads(n + 1):
+                cp.start()
+            sends_kv(n).wait_recv()
+            sends_q(n).wait_recv()
+
+        @pl.when(n == NC - 1)
+        def _():
+            for cp in mine:
+                cp.wait()
+
+        for cp in loads(n):
+            cp.wait()
+        for i, gain in enumerate((qgain, qgain, kgain)):
+            cols = slice(i * HEAD, (i + 1) * HEAD)
+            v = raw_v[slot, :, cols]
+            r = mean_square_scale(v)
+            xn = v * r
+            dn = unrope(came[c, :, cols].astype(F32), cos[...], sin[...])
+            lanes = slice(0, HEAD) if i < 2 else slice(HEAD, 2 * HEAD)
+            gain_qk[:, lanes] += jnp.sum(dn * xn, axis=0, keepdims=True)
+            e = dn * gain[...]
+            e = r * (e - xn * jnp.mean(e * xn, axis=-1, keepdims=True))
+            draw[c, 0:ROWS, cols] = e.astype(BF)
+        draw[c, 0:ROWS, 3 * HEAD :] = came[c, :, 3 * HEAD :]
+        to_mate(n).start()
+        acc[...] += dot(draw[c, 0:ROWS, :], w_v[slot], NT)
+
+    pl.loop(0, 4)(columns)
+    next(ffn)
+    pl.loop(4, NC)(columns)
+
+    xv = x[...].astype(F32)
+    inverse = mean_square_scale(xv)
+    xn = xv * inverse
+    e = acc[...]
+    gain_a[...] = jnp.sum(e * xn, axis=0, keepdims=True)
+    gains = gain_steps(at, (gain_a, gain_f, gain_qk), room, gsum, g_ssem, g_rsem)
+    next(gains)
+    e = e * again[...]
+    dx = dh[...] + inverse * (e - xn * jnp.mean(e * xn, axis=-1, keepdims=True))
+    take = onehot(slt[:, :1].astype(F32).astype(I32) == iota((ROWS, ROWS), 1))
+    dx_s[...] = dot(take, dx.astype(BF)).astype(BF).reshape(dx_s.shape)
+    back = swap_over("row", dx_s, got, *row_sems)
+
+    def oa_loads(n):
+        c, slot = comes_from(n), n % 2
+        return [
+            pltpu.make_async_copy(src.at[c], oa_v.at[slot, pl.ds(ROWS * i, ROWS)], oa_sem.at[i, slot])
+            for i, src in enumerate((oa, oa_m))
+        ]
+
+    for cp in oa_loads(0):
+        cp.start()
+    stack_tokens(k, dhlh, dhl_m, ht_s)
+    swap_n1.wait()
+    stack_tokens(k, n1h, n1_m, nt_s)
+    next(gains)
+
+    @pl.loop(0, NC)
+    def _(n):
+        c, slot = comes_from(n), n % 2
+
+        @pl.when(n < NC - 1)
+        def _():
+            for cp in oa_loads(n + 1):
+                cp.start()
+
+        to_mate(n).wait()
+        g = dot(nt_s[...], draw[c]).astype(BF)
+        a0[c % 4, c // 4] = g[:, 0:256].reshape(4, 2, 64, 256)
+        a1[c % 4, c // 4] = g[:, 256:].reshape(4, 2, 64, 256)
+        for cp in oa_loads(n):
+            cp.wait()
+        a2[c % 4, c // 4] = dot(ht_s[...], oa_v[slot]).astype(BF).reshape(4, 2, 64, 256)
 
     in_turn(
-        run_scatter(at, (p0, p1, p2), (r0, r1, r2), bufs, rest[6:9]),
-        rows(),
-        gain_steps(at, (ga, gf, gqk), rest[0], gsum, rest[1], rest[2]),
-        run_scatter(at, (s0, s1, s2), (t0, t1, t2), more, rest[9:12], 1),
+        run_scatter(at, (a0, a1, a2), (r0, r1, r2), a_bufs, a_sems, True),
+        gains,
+        ffn,
     )
-    for cp in cps:
+    for n in range(NC - 1):
+        sends_kv(n).wait_send()
+        sends_q(n).wait_send()
+    for cp in back:
         cp.wait()
 
 
-def last(parts, sums, dx_s, gains):
+def back(
+    lens, qkv, d_o, o_t, lse, slt, x, dh, again, qgain, kgain, cos, sin, gain_f, n1h, dhlh, dhl_m,
+    raw, wq, wkv, oa, oa_m, f_parts,
+):
+    vm = pltpu.VMEM
     total = 2 * WIDTH + 2 * HEAD
     return pl.pallas_call(
-        last_kernel,
-        name="last",
+        back_kernel,
+        name="back",
         out_shape=[sds((64, 256), F32)] * 3
         + [sds((64, 384), F32)] * 3
-        + [sds(dx_s.shape), sds((1, total), F32)],
-        in_specs=[HBM] * 7 + [VMEM] * 3,
+        + [sds((NR, 16, WIDTH)), sds((1, total), F32)],
+        in_specs=[pl.BlockSpec(memory_space=pltpu.SMEM)] + [VMEM] * 16 + [HBM] * 8,
         out_specs=[VMEM] * 6 + [HBM, VMEM],
-        scratch_shapes=scatter_buffers(256)
-        + scatter_buffers(384, 1)
-        + [pltpu.VMEM((4, 4, 1, total), F32), DMA((4, 3)), DMA((4, 3))]
+        scratch_shapes=[
+            vm((NC, ROWS, 512), BF),
+            vm((NC, QK, HEAD), BF),
+            vm((NC, QK, HEAD), BF),
+            vm((NC, 1, QK), F32),
+            vm((NC, HEAD, QK), F32),
+            vm((NC, 1, QK), I32),
+            vm((NC, ROWS, 512), BF),
+            vm((NC, 2 * ROWS, 512), BF),
+            vm((2, WIDTH, 512), BF),
+            vm((2, ROWS, 384), F32),
+            vm((ROWS, WIDTH), F32),
+            vm((NR, 16, WIDTH), BF),
+            vm((1, WIDTH), F32),
+            vm((1, 2 * HEAD), F32),
+            vm((ROWS, 512), BF),
+            vm((512, 2 * ROWS), BF),
+            vm((512, 2 * ROWS), BF),
+            vm((2, 2 * ROWS, 256), BF),
+        ]
+        + [vm((4, 2, 4, 2, 64, 256), BF)] * 3
+        + [vm((4, 4, 1, total), F32)]
+        + swap_sems("col") * 2
+        + [DMA((3, 2)), DMA((NC,)), DMA((NC,)), DMA, DMA, DMA((2, 2)), DMA((4, 3)), DMA((4, 3))]
         + swap_sems("row")
         + scatter_sems()
-        + scatter_sems(2),
-        compiler_params=params(9),
-    )(*parts, *sums, dx_s, *gains)
+        + scatter_sems()
+        + scatter_buffers(256)
+        + scatter_buffers(384),
+        compiler_params=params(6, 63),
+    )(
+        lens, qkv, d_o, o_t, lse, slt, x, dh, again, qgain, kgain, cos, sin, gain_f, n1h, dhlh,
+        dhl_m, raw, as_slabs(wq), as_slabs(wkv), oa, oa_m, *f_parts,
+    )
 
 
 def arrive_kernel(
@@ -1479,20 +1403,13 @@
         w_query, key_matrix, value_matrix, w_out.T, w_gate, w_up, w_down.T,
     )
     oa, o_t, lse, wg, wu, wd = attend(lengths, qkv, planes)
-    out_s, dh, dhlh, n2h, act, d_o, gain_f = middle(slt, x, dy, oa, fgain, wo, wg, wu, wd)
-    g_o, got_out, act_m, oa_m, n2_m, dy_m, dhl_m = back_swap(
-        d_o, out_s, act, oa, n2h, dyh, dhlh
+    dh, dhlh, gain_f, g_o, got_out, oa_m, dhl_m, *f_parts = middle(
+        slt, x, dy, dyh, fgain, oa, wo, wg, wu, wd
     )
-    f_parts = ffn_grads(n2h, n2_m, dyh, dy_m, act, act_m)
-    dqkv, *later = attend_back(lengths, qkv, g_o, o_t, lse, f_parts)
-    draw, dx_s, gain_a, gain_qk, *piece = project_back(
-        slt, x, dh, again, qgain, kgain, cos, sin, raw, dqkv, wq, wkv,
-        f_parts, later[:3], later[3:],
-    )
-    draw_m, n1_m, *sums = core_swap(draw, n1h, f_parts, piece)
-    a_parts = attn_grads(n1h, n1_m, dhlh, dhl_m, draw, draw_m, oa, oa_m)
-    r_q, r_kv, r_o, r_g, r_u, r_d, got_dx, gains = last(
-        a_parts, sums, dx_s, (gain_a, gain_f, gain_qk)
+    f_parts = [p.reshape(4, 2, 4, 2, 64, 384) for p in f_parts]
+    r_q, r_kv, r_o, r_g, r_u, r_d, got_dx, gains = back(
+        lengths, qkv, g_o, o_t, lse, slt, x, dh, again, qgain, kgain, cos, sin, gain_f, n1h, dhlh,
+        dhl_m, raw, wq, wkv, oa, oa_m, f_parts,
     )
     output, input_grad, ga, gf, gq, gk, g_q, g_k, g_v, g_o, g_g, g_u, g_d = arrive(
         target, got_out, got_dx, r_q, r_kv, r_o, r_g, r_u, r_d, gains

time: 366 us -> 320 us (0.87)
  Pallas kernels: 364 us -> 319 us
    pallas_call x8 -> x2, Pallas kernels: 210 us -> 165 us  [the longest x1 121 us: back(): pl.pallas_call(back_kernel, name='back', out_shape=[sds((64, 256), F32)]...]
where the time goes in v4:
time: 320 us
  Pallas kernels  319 us (100%)
    pallas_call x1, Pallas kernels, back(): pl.pallas_call(back_kernel, name='back', out_shape=[sds((64, 256), F32)]...  121 us
    pallas_call x1, Pallas kernels, front(): pl.pallas_call(front_kernel, name='front', out_shape=[sds((NC, ROWS, 512)...  103 us
    pallas_call x1, Pallas kernels, attend(): pl.pallas_call(attend_kernel, name='attend', out_shape=[sds((NC, ROWS, 25...  48.2 us
    pallas_call x1, Pallas kernels, middle(): pl.pallas_call(middle_kernel, name='middle', out_shape=[sds((ROWS, WIDTH)...  44.1 us

profile of v4, /device:TPU:0, one launch (start us, length us, event | category | flops | bytes accessed | tf_op | source)
XLA Modules:
  0.0 319.7 jit_solution(8684756719167053586)
XLA Ops:
  0.6 102.8 %front.1 = (bf16[8,256,512]{2,1,0:T(8,128)(2,1)}, f32[8,256,384]{2,1,0:T(8,128)}, bf16[256,1024]{1,0:T(8,128)(2,1)}, bf16[256,1024]{1,0:T(8,128)(2,1)}, bf16[2,2...) custom-call(s32[1,256]{1,0:T(1,128)} %bitcast.35, ...), custom_call_target="tpu_custom_call" | custom-call | tf_op jit(solution)/shard_map/front/pallas_call | solution.py:700
  103.5 48.2 %attend.1 = (bf16[8,256,256]{2,1,0:T(8,128)(2,1)}, f32[8,128,512]{2,1,0:T(8,128)}, f32[8,1,512]{2,1,0:T(1,128)}, bf16[4,2,4,2,2,64,384]{6,5,4,3,2,1,0:T(8,128)(2...) custom-call(s32[1,8]{1,0:T(1,128)} %lens.5, ...), custom_call_target="tpu_custom_call", output_to_operand_aliasing={{3}: (2, {}), {4}: (3, {}), {5}: (4, {})} | custom-call | tf_op jit(solution)/shard_map/attend/pallas_call | solution.py:821
  151.7 44.1 %middle.1 = (f32[256,1024]{1,0:T(8,128)}, bf16[2,256,512]{2,1,0:T(8,128)(2,1)}, f32[1,1024]{1,0:T(1,128)}, bf16[8,256,256]{2,1,0:T(8,128)(2,1)}, bf16[16,16,1024...) custom-call(bf16[256,128]{1,0:T(8,128)(2,1)} %get-tuple-element.65.s, ...), custom_call_target="tpu_custom_call" | custom-call | tf_op jit(solution)/shard_map/middle/pallas_call | solution.py:1018
  195.8 120.7 %back.1 = (f32[64,256]{1,0:T(8,128)}, f32[64,256]{1,0:T(8,128)}, f32[64,256]{1,0:T(8,128)}, f32[64,384]{1,0:T(8,128)}, f32[64,384]{1,0:T(8,128)}, /*index=5*/f32...) custom-call(s32[1,8]{1,0:T(1,128)} %lens.5, bf16[8,256,512]{2,1,0:T(8,128)(2,1)} %get-tuple-element.69.qkv, ...), custom_call_target="tpu_custom_call" | custom-call | tf_op jit(solution)/shard_map/back/pallas_call | solution.py:1313
  316.5 3.0 arrive.1

commit v5 on v4

--- a/solution.py
+++ b/solution.py
@@ -22,6 +22,8 @@
 WIDTH = 1024
 GROUP = 2048
 ORDERS = (("x", "y", "z"), ("y", "z", "x"), ("z", "x", "y"))
+ATTN = (256, 256, 256)
+FFN = (256, 256, 640)
 HBM = pl.BlockSpec(memory_space=pltpu.HBM)
 VMEM = pl.BlockSpec(memory_space=pltpu.VMEM)
 DMA = pltpu.SemaphoreType.DMA
@@ -59,11 +61,14 @@
     return out
 
 
-def meet(peers):
+def greet(peers):
     barrier = pltpu.get_barrier_semaphore()
     for p in peers:
         pl.semaphore_signal(barrier, inc=1, device_id=p, device_id_type=MESH)
-    pl.semaphore_wait(barrier, len(peers))
+
+
+def met(peers):
+    pl.semaphore_wait(pltpu.get_barrier_semaphore(), len(peers))
 
 
 def ring_peers(at):
@@ -103,8 +108,7 @@
 SHIFT = (0, -1, 1, 2)
 
 
-def piece_index(at, s, t, g, rel):
-    order = ORDERS[s]
+def piece_index(at, order, t, g, rel):
     sel = {a: at[a] for a in order[t + 1 :]}
     if t > 0 and g is not None:
         sel[order[t - 1]] = (at[order[t - 1]] + SHIFT[g]) % 4
@@ -113,17 +117,17 @@
 
 
 class Gather:
-    def __init__(self, at, outs, sems, phases=(0, 1, 2), own=None):
-        self.at, self.outs, self.own = at, outs, own
-        self.base = {t: sum(4 if p == 0 else 16 for p in phases if p < t) for t in phases}
+    def __init__(self, at, outs, sems, phases=(0, 1, 2), own=None, orders=ORDERS, split=False):
+        self.at, self.outs, self.own, self.orders = at, outs, own, orders
+        self.base = {t: sum(4 if p == 0 or not split else 16 for p in phases if p < t) for t in phases}
         self.ssem, self.rsem, self.msem, self.nsem = sems
         self.n = len(outs)
         self.half = outs[0].shape[5] // 2
         self.late, self.sent = [], []
 
     def copies(self, s, t, g):
-        ref = self.outs[s].at[piece_index(self.at, s, t, g, 0)]
-        a, i = ORDERS[s][t], self.base[t] + 4 * (g or 0)
+        ref = self.outs[s].at[piece_index(self.at, self.orders[s], t, g, 0)]
+        a, i = self.orders[s][t], self.base[t] + 4 * (g or 0)
         src = self.own[s] if self.own and (t == 0 or (t == 1 and g == 0)) else ref
         return [
             remote(src, ref, self.ssem.at[s, i + d], self.rsem.at[s, i + d], device(moved(self.at, a, step)))
@@ -131,10 +135,10 @@
         ]
 
     def forwards(self, s, t, g):
-        a, i = ORDERS[s][t], self.base[t] + 4 * (g or 0) + 2
+        a, i = self.orders[s][t], self.base[t] + 4 * (g or 0) + 2
         out = []
         for d, step in enumerate((1, -1)):
-            came = piece_index(self.at, s, t, g, -step) + (pl.ds(d * self.half, self.half),)
+            came = piece_index(self.at, self.orders[s], t, g, -step) + (pl.ds(d * self.half, self.half),)
             ref = self.outs[s].at[came]
             out.append(
                 remote(
@@ -149,7 +153,7 @@
 
     def to_mate(self, s, g, rel):
         slot = 4 * (g or 0) + SHIFT.index(rel)
-        ref = self.outs[s].at[piece_index(self.at, s, 2, g, rel)]
+        ref = self.outs[s].at[piece_index(self.at, self.orders[s], 2, g, rel)]
         return remote(ref, ref, self.msem.at[s, slot], self.nsem.at[s, slot], device(mate(self.at)))
 
     def share(self, s, g, rel):
@@ -165,11 +169,12 @@
             if t == 2:
                 self.share(s, g, 0)
 
-    def pass_on(self, t, g):
+    def pass_on(self, t, g, wait=True):
         for s in range(self.n):
-            first = self.copies(s, t, g)
+            first = self.copies(s, t, g) if wait else None
             for d, cp in enumerate(self.forwards(s, t, g)):
-                first[d].wait_recv()
+                if wait:
+                    first[d].wait_recv()
                 cp.start()
                 self.sent.append(cp)
                 if t == 2:
@@ -189,23 +194,12 @@
             cp.wait_send()
 
     def lines(self):
-        self.send(0, None)
-        self.send(1, 0)
-        yield
-        self.pass_on(0, None)
-        self.send(1, 1)
-        self.send(1, 2)
-        yield
-        self.pass_on(1, 0)
-        self.arrived(0, None)
-        self.send(1, 3)
-        yield
-        self.pass_on(1, 1)
-        self.pass_on(1, 2)
-        self.pass_on(1, 3)
-        yield
-        for g in range(4):
-            self.arrived(1, g)
+        for t in (0, 1):
+            self.send(t, None)
+            yield
+            self.pass_on(t, None)
+            yield
+            self.arrived(t, None)
 
     def all(self):
         self.send(0, None)
@@ -273,43 +267,26 @@
     return out
 
 
-def unravel(i, shape):
-    out = ()
-    for n in reversed(shape):
-        out = (i % n,) + out
-        i = i // n
-    return out
-
-
-def add_blocks(lead, dst, terms):
-    n = math.prod(lead)
-
-    def one(i):
-        j = unravel(i, lead)
-        total = None
-        for ref, pre in terms:
-            v = ref[pre(j)].astype(F32)
+def add_up(dst, terms):
+    total = None
+    if len(terms) == 2:
+        total = terms[0][0][terms[0][1]] + terms[1][0][terms[1][1]]
+    else:
+        for ref, at in terms:
+            v = ref[at].astype(F32)
             total = v if total is None else total + v
-        dst[0][dst[1](j)] = total.astype(dst[0].dtype)
-
-    if n == 1:
-        one(0)
-    else:
-
-        @pl.loop(0, n)
-        def _(i):
-            one(i)
+    dst[0][dst[1]] = total.astype(dst[0].dtype)
 
 
 def scatter_leads(s, t):
     return lead_shape(ORDERS[s][: 2 - t])
 
 
-def scatter_buffers(w, t0=0, n=3):
+def scatter_buffers(widths, t0=0, n=3):
     out = []
     for s in range(n):
         for t in range(t0, 3):
-            lead = scatter_leads(s, t)
+            lead, w = scatter_leads(s, t), widths[s]
             out.append(pltpu.VMEM((2,) + lead + (32, w), BF))
             out.append(pltpu.VMEM((2,) + lead + (64, w), BF))
             out.append(pltpu.VMEM((2,) + lead + (32, w), BF))
@@ -359,14 +336,6 @@
         rsem.at[s, t - t0, 4 + d],
         device(moved(at, a, (1, -1)[d])),
     )
-
-
-def side(d):
-    return lambda j: (d,) + j
-
-
-def same(j):
-    return j
 
 
 def run_scatter(at, parts, results, bufs, sems, resident=False):
@@ -398,54 +367,33 @@
         yield
         for s in range(n):
             rel_in, piece_in, rel_out, total, cps, loads = st[s]
-            lead = scatter_leads(s, t)
             for d in range(2):
                 cps[d].wait_recv()
                 if loads:
                     loads[d].wait()
-                    mine = (rel_out, side(d))
+                    mine = (rel_out, d)
                 else:
-                    mine = (cur[s], picker(s, t, at, (1, -1)[d], (LO, HI)[d]))
-                add_blocks(lead, (rel_out, side(d)), [mine, (rel_in, side(d))])
+                    mine = (cur[s], part_of(s, t, at, (1, -1)[d], (LO, HI)[d]))
+                add_up((rel_out, d), [mine, (rel_in, d)])
                 cp = second_send(s, t, at, d, rel_out, piece_in, ssem, rsem, t0)
                 cp.start()
                 cps.append(cp)
         yield
         for s in range(n):
             rel_in, piece_in, rel_out, total, cps, loads = st[s]
-            lead = scatter_leads(s, t)
             for i in (2, 3, 4, 5):
                 cps[i].wait_recv()
             if loads:
                 loads[2].wait()
-                mine = (total, same)
+                mine = (total, ...)
             else:
-                mine = (cur[s], picker(s, t, at, 0, slice(None)))
-            dst = (total, same) if t < 2 else (results[s], lambda j: (slice(None),) * 2)
-            add_blocks(lead, dst, [mine, (piece_in, side(0)), (piece_in, side(1))])
+                mine = (cur[s], part_of(s, t, at, 0, slice(None)))
+            dst = (total if t < 2 else results[s], ...)
+            add_up(dst, [mine, (piece_in, 0), (piece_in, 1)])
             cur[s] = total
             waits += cps
     for cp in waits:
         cp.wait_send()
-
-
-def picker(s, t, at, rel, rows):
-    a, axes = ORDERS[s][2 - t], ORDERS[s][: 3 - t]
-    pos = (at[a] + rel) % 4
-
-    def pick(j):
-        it = iter(j)
-        out = ()
-        for q in ("x", "zl", "y", "zh"):
-            if q[0] not in axes:
-                continue
-            if q[0] == a:
-                out += (pos % 2 if q == "zl" else pos // 2 if q == "zh" else pos,)
-            else:
-                out += (next(it),)
-        return out + (rows,)
-
-    return pick
 
 
 def in_turn(*steps):
@@ -483,25 +431,6 @@
     return [DMA((n - 1,)), DMA((n - 1,)), DMA]
 
 
-def col_swap_kernel(src, dst, ssem, rsem, lsem):
-    at = where_am_i()
-    meet(col_peers(at))
-    for cp in swap_over("col", src, dst, ssem, rsem, lsem):
-        cp.wait()
-
-
-def col_swap(src, cid, name):
-    return pl.pallas_call(
-        col_swap_kernel,
-        name=name,
-        out_shape=sds(src.shape),
-        in_specs=[HBM],
-        out_specs=HBM,
-        scratch_shapes=swap_sems("col"),
-        compiler_params=params(cid),
-    )(src)
-
-
 def dot(a, b, dims=((1,), (0,))):
     return lax.dot_general(a, b, (dims, ((), ())), preferred_element_type=F32)
 
@@ -568,76 +497,100 @@
     return g.reshape(NC, -1, g.shape[-1])
 
 
+LOG2E = math.log2(math.e)
+QK = 512
+
+
+def stacked(v):
+    return jnp.concatenate([v[:, :HEAD], v[:, HEAD : 2 * HEAD]], axis=0)
+
+
+SPAN = 5
+
+
+def group_slots(i):
+    return i * ROWS + iota((1, QK), 1) % ROWS
+
+
+def allowed(i, j, first):
+    key = j * ROWS + iota((ROWS, QK), 0)
+    return (key <= group_slots(i)) & (key >= first)
+
+
 def front_kernel(
     t_row, lens, tokens, grads, again, qgain, kgain, freq, w_q, w_k, w_v, w_o, w_g, w_u, w_d,
-    qkv, raw, x_o, dy_o, n1h, dyh, cos, sin, slt, a0, a1, a2, f0, f1, f2,
-    sent, came, kv_s, n1_s, src_s, raw_s, wq_v, wkv_v,
-    own_sem, w_sem, raw_sem, out_ssem, out_rsem, out_lsem, *sems,
+    oa, raw, x_o, dy_o, n1h, dyh, cos, sin, slt, qkv_o, o_t, lse, a0, a1, a2, f0, f1, f2,
+    sent, came, kv_s, u0_s, u1_s, u2_s, n1_s, src_s, raw_s, wq_v, wkv_v, qkv, o_s, s_v,
+    own_sem, w_sem, keep_sem, out_ssem, out_rsem, out_lsem, o_ssem, o_rsem, o_lsem, *sems,
 ):
     at = where_am_i()
     row, col = lax.axis_index("row"), lax.axis_index("col")
     here = block_index({a: at[a] for a in "xyz"}, at["k"])
+    near = [device(moved(at, "z", 1)), device(moved(at, "z", -1))]
+    peers = near + row_peers(at) + col_peers(at)
+    greet(peers)
     kv_s[:, :HEAD] = w_k[...]
     kv_s[:, HEAD:] = w_v[...]
-    pairs = zip((w_q, kv_s, w_o, w_g, w_u, w_d), (a0, a1, a2, f0, f1, f2))
+    u0_s[...] = w_g[:, 0:256]
+    u1_s[...] = w_u[:, 0:256]
+    u2_s[:, 0:128] = w_g[:, 256:]
+    u2_s[:, 128:256] = w_u[:, 256:]
+    u2_s[:, 256:] = w_d[...]
+    pairs = zip((w_q, kv_s, w_o, u0_s, u1_s, u2_s), (a0, a1, a2, f0, f1, f2))
     own = [
         pltpu.make_async_copy(src, dst.at[here], own_sem.at[i])
         for i, (src, dst) in enumerate(pairs)
     ]
     for cp in own:
         cp.start()
-    near = [device(moved(at, "z", 1)), device(moved(at, "z", -1))]
-    meet(near + row_peers(at) + col_peers(at))
-    first = Gather(at, (a0, a1, a2), sems[3:7], own=(w_q, kv_s, w_o))
-    second = Gather(at, (f0, f1, f2), sems[7:11], (0, 1), own=(w_g, w_u, w_d))
-    steps = first.all()
-    more = second.lines()
-    next(steps)
     place, _ = slots_sent(t_row[...])
     sel = place == iota((ROWS, ROWS), 0)
     pick = onehot(sel)
     slot = jnp.sum(jnp.where(sel, t_row[...] % ROWS, 0).astype(F32), axis=1, keepdims=True)
     message = (NR, 16, WIDTH)
-    sent[:, :, 0:WIDTH] = dot(pick, tokens[...]).astype(BF).reshape(message)
-    sent[:, :, WIDTH : 2 * WIDTH] = dot(pick, grads[...]).astype(BF).reshape(message)
-    sent[:, :, 2 * WIDTH :] = (
+    sent[0, :, :, 0:WIDTH] = dot(pick, tokens[...]).astype(BF).reshape(message)
+    sent[0, :, :, WIDTH:] = (
         jnp.broadcast_to(slot, (ROWS, HEAD)).astype(BF).reshape((NR, 16, HEAD))
     )
-    cps = swap_over("row", sent, came, *sems[0:3])
+    met(peers)
+    attn = Gather(at, (a0, a1, a2), sems[6:10], own=(w_q, kv_s, w_o), split=True)
+    lines = Gather(at, (f0, f1, f2), sems[10:14], (0, 1), own=(u0_s, u1_s, u2_s))
+    planes = [
+        Gather(at, (f0, f1), sems[14:18], (2,), orders=ORDERS[:2]),
+        Gather(at, (f2,), sems[18:22], (2,), orders=ORDERS[2:]),
+    ]
+    steps = attn.all()
+    more = lines.lines()
     next(steps)
+    next(more)
+    cps = swap_over("row", sent.at[0], came.at[0], *sems[0:3])
+    next(steps)
+    next(more)
     for cp in own:
         cp.wait()
     for _ in range(5):
         next(steps)
         next(more, None)
-
     slots = col * ROWS + iota((ROWS, HEAD), 0)
     pos = (slots - first_slots(lambda j: lens[0, j], slots)).astype(F32)
     angle = pos * freq[...]
     cos[...] = jnp.cos(angle)
     sine = jnp.sin(angle)
     sin[...] = jnp.where(iota((ROWS, HEAD), 1) < HEAD // 2, -sine, sine)
+    sent[1, :, :, 0:WIDTH] = dot(pick, grads[...]).astype(BF).reshape(message)
     for cp in cps:
         cp.wait()
-    local = came[:, :, 2 * WIDTH :].reshape(ROWS, HEAD)
+    local = came[0, :, :, WIDTH:].reshape(ROWS, HEAD)
     slt[...] = local
     put = onehot(local[:, :1].astype(F32).astype(I32) == iota((ROWS, ROWS), 1))
-    x = dot(put, came[:, :, 0:WIDTH].reshape(ROWS, WIDTH), TN)
+    x = dot(put, came[0, :, :, 0:WIDTH].reshape(ROWS, WIDTH), TN)
     x_o[...] = x.astype(BF)
     n1 = x * mean_square_scale(x) * again[...]
     n1_s[...] = n1.astype(BF)
     a, b = halves_of(n1)
     n1h[0] = a.astype(BF)
     n1h[1] = b.astype(BF)
-    dy = dot(put, came[:, :, WIDTH : 2 * WIDTH].reshape(ROWS, WIDTH), TN)
-    dy_o[...] = dy.astype(BF)
-    a, b = halves_of(dy)
-    dyh[0] = a.astype(BF)
-    dyh[1] = b.astype(BF)
-
     in_turn(steps, more)
-    first.drain()
-    second.drain()
 
     def block_at(i):
         return (col + 1 + i) % NC
@@ -653,11 +606,12 @@
         c = block_at(i)
         return remote(src_s.at[c], qkv.at[col], out_ssem.at[i], out_rsem.at[i], (row, c))
 
+    attn.drain()
+    planes[1].send(2, None)
     for cp in loads(0):
         cp.start()
 
-    @pl.loop(0, NC)
-    def _(i):
+    def columns(i):
         c = block_at(i)
 
         @pl.when(i < NC - 1)
@@ -683,96 +637,26 @@
         def _():
             sends(i).start()
 
+    pl.loop(0, NC)(columns)
     mine = pltpu.make_async_copy(src_s.at[col], qkv.at[col], out_lsem)
     mine.start()
-    keep = pltpu.make_async_copy(raw_s, raw, raw_sem)
-    keep.start()
+    keep = [pltpu.make_async_copy(raw_s, raw, keep_sem.at[0])]
+    keep[0].start()
+    cps = swap_over("row", sent.at[1, :, :, pl.ds(0, WIDTH)], came.at[1, :, :, pl.ds(0, WIDTH)], *sems[3:6])
     for i in range(NC - 1):
         sends(i).wait()
+    planes[0].send(2, None)
     mine.wait()
-    keep.wait()
-
-
-def front(target, lens, tokens, grads, again, qgain, kgain, *weights):
-    freq = ROPE_BASE ** (-(np.arange(HEAD) % (HEAD // 2)).astype(np.float32) * 2.0 / HEAD)
-    freq = jnp.asarray(freq.astype(np.float32).reshape(1, HEAD))
-    rows = pltpu.VMEM((NR, 16, 2 * WIDTH + HEAD), BF)
-    return pl.pallas_call(
-        front_kernel,
-        name="front",
-        out_shape=[
-            sds((NC, ROWS, 512)),
-            sds((NC, ROWS, 384), F32),
-            sds((ROWS, WIDTH)),
-            sds((ROWS, WIDTH)),
-            sds((2, ROWS, 512)),
-            sds((2, ROWS, 512)),
-            sds((ROWS, HEAD), F32),
-            sds((ROWS, HEAD), F32),
-            sds((ROWS, HEAD)),
-        ]
-        + [gather_shape(256)] * 3
-        + [gather_shape(384)] * 3,
-        in_specs=[VMEM, pl.BlockSpec(memory_space=pltpu.SMEM)]
-        + [VMEM] * 6
-        + [HBM, VMEM, VMEM]
-        + [HBM] * 4,
-        out_specs=[HBM] * 2 + [VMEM] * 7 + [HBM] * 6,
-        scratch_shapes=[rows, rows, pltpu.VMEM((64, 256), BF)]
-        + [
-            pltpu.VMEM((ROWS, WIDTH), BF),
-            pltpu.VMEM((NC, ROWS, 512), BF),
-            pltpu.VMEM((NC, ROWS, 384), F32),
-            pltpu.VMEM((2, 4, 2, 2, 64, 256), BF),
-            pltpu.VMEM((2, 4, 2, 2, 64, 256), BF),
-        ]
-        + [DMA((6,)), DMA((2, 2)), DMA, DMA((NC - 1,)), DMA((NC - 1,)), DMA]
-        + swap_sems("row")
-        + gather_sems(36, 16)
-        + gather_sems(20, 0),
-        compiler_params=params(1),
-    )(target.reshape(1, ROWS), lens, tokens, grads, again, qgain, kgain, freq, *weights)
-
-
-LOG2E = math.log2(math.e)
-QK = 512
-
-
-def stacked(v):
-    return jnp.concatenate([v[:, :HEAD], v[:, HEAD : 2 * HEAD]], axis=0)
-
-
-SPAN = 5
-
-
-def group_slots(i):
-    return i * ROWS + iota((1, QK), 1) % ROWS
-
-
-def allowed(i, j, first):
-    key = j * ROWS + iota((ROWS, QK), 0)
-    return (key <= group_slots(i)) & (key >= first)
-
-
-def attend_kernel(
-    lens, qkv, i0, i1, i2, oa, o_t, lse, f0, f1, f2, o_s, s_v, ssem, rsem, lsem, *sems
-):
-    at = where_am_i()
-    row, col = lax.axis_index("row"), lax.axis_index("col")
-    meet(ring_peers(at) + [device(mate(at))] + col_peers(at))
-    more = Gather(at, (f0, f1, f2), sems, (2,))
-    more.send(2, None)
+    keep.append(pltpu.make_async_copy(qkv, qkv_o, keep_sem.at[1]))
+    keep[1].start()
+
     scale = HEAD**-0.5 * LOG2E
 
-    def block_at(n):
-        return (col + 1 + n) % NC
-
-    def sends(n):
+    def o_sends(n):
         c = block_at(n)
-        return remote(o_s.at[c], oa.at[col], ssem.at[n], rsem.at[n], (row, c))
-
-    @pl.loop(0, NC)
-    def _(n):
+        return remote(o_s.at[c], oa.at[col], o_ssem.at[n], o_rsem.at[n], (row, c))
+
+    def queries(n):
         i = block_at(n)
         q = stacked(qkv[i, :, 0 : 2 * HEAD])
         start = first_slots(lambda j: lens[0, j], group_slots(i))
@@ -798,43 +682,79 @@
 
         @pl.when(n < NC - 1)
         def _():
-            sends(n).start()
-
-        @pl.when(n == NC - 2)
-        def _():
-            more.pass_on(2, None)
-
-    mine = pltpu.make_async_copy(o_s.at[col], oa.at[col], lsem)
+            o_sends(n).start()
+
+    pl.loop(0, 6)(queries)
+    planes[1].pass_on(2, None)
+    planes[0].pass_on(2, None)
+    pl.loop(6, NC)(queries)
+    mine = pltpu.make_async_copy(o_s.at[col], oa.at[col], o_lsem)
     mine.start()
-    more.arrived(2, None)
+    for cp in cps:
+        cp.wait()
+    dy = dot(put, came[1, :, :, 0:WIDTH].reshape(ROWS, WIDTH), TN)
+    dy_o[...] = dy.astype(BF)
+    a, b = halves_of(dy)
+    dyh[0] = a.astype(BF)
+    dyh[1] = b.astype(BF)
+    planes[0].arrived(2, None)
+    planes[1].arrived(2, None)
     for n in range(NC - 1):
-        sends(n).wait()
-    mine.wait()
-    for s in range(3):
-        for cp in more.copies(s, 2, None) + more.forwards(s, 2, None):
-            cp.wait_send()
-        for rel in SHIFT:
-            more.to_mate(s, None, rel).wait()
-
-
-def attend(lens, qkv, planes):
+        o_sends(n).wait()
+    for cp in [mine] + keep:
+        cp.wait()
+    for g in [lines] + planes:
+        g.drain()
+
+
+def front(target, lens, tokens, grads, again, qgain, kgain, *weights):
+    freq = ROPE_BASE ** (-(np.arange(HEAD) % (HEAD // 2)).astype(np.float32) * 2.0 / HEAD)
+    freq = jnp.asarray(freq.astype(np.float32).reshape(1, HEAD))
+    vm = pltpu.VMEM
     return pl.pallas_call(
-        attend_kernel,
-        name="attend",
+        front_kernel,
+        name="front",
         out_shape=[
             sds((NC, ROWS, 256)),
+            sds((NC, ROWS, 384), F32),
+            sds((ROWS, WIDTH)),
+            sds((ROWS, WIDTH)),
+            sds((2, ROWS, 512)),
+            sds((2, ROWS, 512)),
+            sds((ROWS, HEAD), F32),
+            sds((ROWS, HEAD), F32),
+            sds((ROWS, HEAD)),
+            sds((NC, ROWS, 512)),
             sds((NC, HEAD, QK), F32),
             sds((NC, 1, QK), F32),
         ]
-        + [gather_shape(384)] * 3,
-        in_specs=[pl.BlockSpec(memory_space=pltpu.SMEM), VMEM] + [HBM] * 3,
-        out_specs=[HBM, VMEM, VMEM] + [HBM] * 3,
-        input_output_aliases={2: 3, 3: 4, 4: 5},
-        scratch_shapes=[pltpu.VMEM((NC, ROWS, 256), BF), pltpu.VMEM((SPAN, ROWS, QK), F32)]
-        + swap_sems("col")
-        + gather_sems(4, 4),
-        compiler_params=params(2),
-    )(lens, qkv, *planes)
+        + [gather_shape(w) for w in ATTN + FFN],
+        in_specs=[VMEM, pl.BlockSpec(memory_space=pltpu.SMEM)]
+        + [VMEM] * 6
+        + [HBM, VMEM, VMEM, HBM]
+        + [VMEM] * 3,
+        out_specs=[HBM] * 2 + [VMEM] * 7 + [HBM] + [VMEM] * 2 + [HBM] * 6,
+        scratch_shapes=[vm((2, NR, 16, WIDTH + HEAD), BF)] * 2
+        + [vm((64, w), BF) for w in (256,) + FFN]
+        + [
+            vm((ROWS, WIDTH), BF),
+            vm((NC, ROWS, 512), BF),
+            vm((NC, ROWS, 384), F32),
+            vm((2, 4, 2, 2, 64, 256), BF),
+            vm((2, 4, 2, 2, 64, 256), BF),
+            vm((NC, ROWS, 512), BF),
+            vm((NC, ROWS, 256), BF),
+            vm((SPAN, ROWS, QK), F32),
+        ]
+        + [DMA((6,)), DMA((2, 2)), DMA((2,))]
+        + swap_sems("col") * 2
+        + swap_sems("row") * 2
+        + gather_sems(36, 16)
+        + gather_sems(8, 0)
+        + gather_sems(4, 4, 2)
+        + gather_sems(4, 4, 1),
+        compiler_params=params(1),
+    )(target.reshape(1, ROWS), lens, tokens, grads, again, qgain, kgain, freq, *weights)
 
 
 PAIR = 768
@@ -846,8 +766,19 @@
     scratch[:, ROWS:] = others[...].astype(F32).T.astype(BF)
 
 
+def lanes_of(j):
+    at = 384 * j
+    return (
+        (0, pl.ds(0, 256), pl.ds(at, 256)),
+        (2, pl.ds(0, 128), pl.ds(at + 256, 128)),
+        (1, pl.ds(0, 256), pl.ds(PAIR + at, 256)),
+        (2, pl.ds(128, 128), pl.ds(PAIR + at + 256, 128)),
+        (2, pl.ds(256, 384), pl.ds(2 * PAIR + at, 384)),
+    )
+
+
 def middle_kernel(
-    slt, x, dy, dyh, fgain, oa, wo, wg, wu, wd,
+    slt, x, dy, dyh, fgain, oa, wo, f0, f1, f2,
     dh_o, dhlh, gain_o, g_o, got, oa_m, dhl_m, p0, p1, p2,
     oa_v, wo_v, w_v, acc, dn2, h_s, n2_s, dhl_s, act, n2h, n2_m, dy_m, do_s, out_s, nt_s, yt_s, g_v,
     oa_sem, wo_sem, w_sem, g_sem, act_ssem, act_rsem, m_ssem, m_rsem, do_ssem, do_rsem, do_lsem,
@@ -856,6 +787,8 @@
     at = where_am_i()
     row, col, k = lax.axis_index("row"), lax.axis_index("col"), at["k"]
     to = device(mate(at))
+    peers = col_peers(at) + row_peers(at)
+    greet(peers)
     lead = []
     for p in range(NC):
         c = (p % 2) * 4 + p // 2
@@ -869,12 +802,12 @@
         slot = t % 2
         return [
             pltpu.make_async_copy(
-                w.at[2 * t + j],
-                w_v.at[slot, :, pl.ds(PAIR * i + 384 * j, 384)],
-                w_sem.at[slot, 2 * i + j],
+                (f0, f1, f2)[i].at[2 * t + j, :, src],
+                w_v.at[slot, :, dst],
+                w_sem.at[slot, 5 * j + n],
             )
-            for i, w in enumerate((wg, wu, wd))
             for j in range(2)
+            for n, (i, src, dst) in enumerate(lanes_of(j))
         ]
 
     def act_send(t):
@@ -885,10 +818,6 @@
         return remote(src, dst, m_ssem.at[i], m_rsem.at[i], to)
 
     for cp in loads(0):
-        cp.start()
-    meet(col_peers(at) + row_peers(at))
-    to_mate = [mate_send(0, dyh.at[1 - k], dy_m), mate_send(1, oa, oa_m)]
-    for cp in to_mate:
         cp.start()
     for cp in lead:
         cp.wait()
@@ -905,9 +834,11 @@
     a, b = halves_of(n2)
     n2h[0] = a.astype(BF)
     n2h[1] = b.astype(BF)
-    cp = mate_send(2, n2h.at[1 - k], n2_m)
-    cp.start()
-    to_mate.append(cp)
+    met(peers)
+    pairs = ((dyh.at[1 - k], dy_m), (oa, oa_m), (n2h.at[1 - k], n2_m))
+    to_mate = [mate_send(i, src, dst) for i, (src, dst) in enumerate(pairs)]
+    for cp in to_mate:
+        cp.start()
     dn2[...] = jnp.zeros_like(dn2)
 
     @pl.loop(0, STEPS)
@@ -980,12 +911,12 @@
         slot = t % 2
         return [
             pltpu.make_async_copy(
-                g_v.at[slot, :, pl.ds(PAIR * i + 384 * j, 384)],
-                p.at[2 * t + j],
-                g_sem.at[slot, 2 * i + j],
+                g_v.at[slot, :, src],
+                (p0, p1, p2)[i].at[2 * t + j, :, dst],
+                g_sem.at[slot, 5 * j + n],
             )
-            for i, p in enumerate((p0, p1, p2))
             for j in range(2)
+            for n, (i, dst, src) in enumerate(lanes_of(j))
         ]
 
     @pl.loop(0, STEPS)
@@ -1013,7 +944,7 @@
         cp.wait()
 
 
-def middle(slt, x, dy, dyh, fgain, oa, wo, wg, wu, wd):
+def middle(slt, x, dy, dyh, fgain, oa, wo, *planes):
     vm = pltpu.VMEM
     return pl.pallas_call(
         middle_kernel,
@@ -1027,7 +958,7 @@
             sds((NC, ROWS, 256)),
             sds((ROWS, 512)),
         ]
-        + [sds((NC, 512, 384))] * 3,
+        + [sds((NC, 512, w)) for w in FFN],
         in_specs=[VMEM] * 5 + [HBM] * 5,
         out_specs=[VMEM] * 3 + [HBM] * 7,
         scratch_shapes=[
@@ -1050,8 +981,8 @@
             vm((2, 512, 3 * PAIR), BF),
             DMA((NC,)),
             DMA((NC,)),
-            DMA((2, 6)),
-            DMA((2, 6)),
+            DMA((2, 10)),
+            DMA((2, 10)),
             DMA((STEPS,)),
             DMA((STEPS,)),
             DMA((4,)),
@@ -1060,7 +991,7 @@
         + swap_sems("col")
         + swap_sems("row"),
         compiler_params=params(5),
-    )(slt, x, dy, dyh, fgain, oa, *map(as_slabs, (wo, wg, wu, wd)))
+    )(slt, x, dy, dyh, fgain, oa, *map(as_slabs, (wo,) + planes))
 
 
 def gain_steps(at, pieces, room, total, ssem, rsem):
@@ -1091,12 +1022,12 @@
 
 
 def back_kernel(
-    lens, qkv, d_o, o_t, lse, slt, x, dh, again, qgain, kgain, cos, sin, gain_f, n1h, dhlh, dhl_m,
-    raw, wq, wkv, oa, oa_m, p0, p1, p2,
+    lens, qkv, d_o, lse, slt, x, dh, again, qgain, kgain, cos, sin, gain_f, n1h, dhlh, dhl_m,
+    o_t, raw, wq, wkv, oa, oa_m, p0, p1, p2,
     r0, r1, r2, t0, t1, t2, got, gsum,
     out_s, qs, dos, delta, dq, first, came, draw, w_v, raw_v, acc, dx_s, gain_a, gain_qk,
-    n1_m, nt_s, ht_s, oa_v, a0, a1, a2, room,
-    kv_ssem, kv_rsem, kv_lsem, q_ssem, q_rsem, q_lsem, w_sem, m_ssem, m_rsem, n_ssem, n_rsem, oa_sem,
+    n1_m, nt_s, ht_s, oa_v, o_v, a0, a1, a2, room,
+    kv_ssem, kv_rsem, kv_lsem, q_ssem, q_rsem, q_lsem, w_sem, m_ssem, m_rsem, n_ssem, n_rsem, oa_sem, o_sem,
     g_ssem, g_rsem, *rest,
 ):
     at = where_am_i()
@@ -1104,25 +1035,38 @@
     to = device(mate(at))
     row_sems, rest = rest[:3], rest[3:]
     a_sems, f_sems, rest = rest[:3], rest[3:6], rest[6:]
-    na = len(scatter_buffers(256))
+    na = len(scatter_buffers(ATTN))
     a_bufs, f_bufs = rest[:na], rest[na:]
     near = [device(moved(at, "z", 1)), device(moved(at, "z", -1))]
-    meet(near + row_peers(at) + col_peers(at))
+    peers = near + row_peers(at) + col_peers(at)
+    greet(peers)
+
+    scale = HEAD**-0.5
+
+    def o_load(i):
+        return pltpu.make_async_copy(o_t.at[i], o_v.at[i % 2], o_sem.at[i % 2])
+
+    o_load(0).start()
+
+    @pl.loop(0, NC)
+    def _(i):
+        @pl.when(i < NC - 1)
+        def _():
+            o_load(i + 1).start()
+
+        qs[i] = stacked(qkv[i, :, 0 : 2 * HEAD])
+        g = stacked(d_o[i])
+        dos[i] = g
+        o_load(i).wait()
+        delta[i] = jnp.sum(g.astype(F32).T * o_v[i % 2], axis=0, keepdims=True)
+        dq[i] = jnp.zeros((HEAD, QK), F32)
+        first[i] = first_slots(lambda n: lens[0, n], group_slots(i))
+
+    met(peers)
     ffn = run_scatter(at, (p0, p1, p2), (t0, t1, t2), f_bufs, f_sems)
     next(ffn)
     swap_n1 = remote(n1h.at[1 - k], n1_m, n_ssem, n_rsem, to)
     swap_n1.start()
-
-    scale = HEAD**-0.5
-
-    @pl.loop(0, NC)
-    def _(i):
-        qs[i] = stacked(qkv[i, :, 0 : 2 * HEAD])
-        g = stacked(d_o[i])
-        dos[i] = g
-        delta[i] = jnp.sum(g.astype(F32).T * o_t[i], axis=0, keepdims=True)
-        dq[i] = jnp.zeros((HEAD, QK), F32)
-        first[i] = first_slots(lambda n: lens[0, n], group_slots(i))
 
     def block_at(n):
         return (col + 1 + n) % NC
@@ -1166,9 +1110,7 @@
         def _():
             sends_kv(n).start()
 
-    pl.loop(0, 6)(keys)
-    next(ffn)
-    pl.loop(6, NC)(keys)
+    pl.loop(0, NC)(keys)
 
     @pl.loop(0, NC)
     def _(n):
@@ -1244,9 +1186,7 @@
         to_mate(n).start()
         acc[...] += dot(draw[c, 0:ROWS, :], w_v[slot], NT)
 
-    pl.loop(0, 4)(columns)
-    next(ffn)
-    pl.loop(4, NC)(columns)
+    pl.loop(0, NC)(columns)
 
     xv = x[...].astype(F32)
     inverse = mean_square_scale(xv)
@@ -1260,6 +1200,7 @@
     take = onehot(slt[:, :1].astype(F32).astype(I32) == iota((ROWS, ROWS), 1))
     dx_s[...] = dot(take, dx.astype(BF)).astype(BF).reshape(dx_s.shape)
     back = swap_over("row", dx_s, got, *row_sems)
+    next(ffn)
 
     def oa_loads(n):
         c, slot = comes_from(n), n % 2
@@ -1314,9 +1255,9 @@
         back_kernel,
         name="back",
         out_shape=[sds((64, 256), F32)] * 3
-        + [sds((64, 384), F32)] * 3
+        + [sds((64, w), F32) for w in FFN]
         + [sds((NR, 16, WIDTH)), sds((1, total), F32)],
-        in_specs=[pl.BlockSpec(memory_space=pltpu.SMEM)] + [VMEM] * 16 + [HBM] * 8,
+        in_specs=[pl.BlockSpec(memory_space=pltpu.SMEM)] + [VMEM] * 15 + [HBM] * 9,
         out_specs=[VMEM] * 6 + [HBM, VMEM],
         scratch_shapes=[
             vm((NC, ROWS, 512), BF),
@@ -1337,20 +1278,22 @@
             vm((512, 2 * ROWS), BF),
             vm((512, 2 * ROWS), BF),
             vm((2, 2 * ROWS, 256), BF),
+            vm((2, HEAD, QK), F32),
         ]
         + [vm((4, 2, 4, 2, 64, 256), BF)] * 3
         + [vm((4, 4, 1, total), F32)]
         + swap_sems("col") * 2
-        + [DMA((3, 2)), DMA((NC,)), DMA((NC,)), DMA, DMA, DMA((2, 2)), DMA((4, 3)), DMA((4, 3))]
+        + [DMA((3, 2)), DMA((NC,)), DMA((NC,)), DMA, DMA, DMA((2, 2)), DMA((2,))]
+        + [DMA((4, 3)), DMA((4, 3))]
         + swap_sems("row")
         + scatter_sems()
         + scatter_sems()
-        + scatter_buffers(256)
-        + scatter_buffers(384),
+        + scatter_buffers(ATTN)
+        + scatter_buffers(FFN),
         compiler_params=params(6, 63),
     )(
-        lens, qkv, d_o, o_t, lse, slt, x, dh, again, qgain, kgain, cos, sin, gain_f, n1h, dhlh,
-        dhl_m, raw, as_slabs(wq), as_slabs(wkv), oa, oa_m, *f_parts,
+        lens, qkv, d_o, lse, slt, x, dh, again, qgain, kgain, cos, sin, gain_f, n1h, dhlh,
+        dhl_m, o_t, raw, as_slabs(wq), as_slabs(wkv), oa, oa_m, *f_parts,
     )
 
 
@@ -1370,9 +1313,11 @@
     k_o[...] = kv[:, :HEAD]
     v_o[...] = kv[:, HEAD:]
     o_o[...] = o[...]
-    g_o[...] = g[...]
-    u_o[...] = u[...]
-    d_o[...] = d[...]
+    g_o[:, 0:256] = g[...]
+    g_o[:, 256:] = d[:, 0:128]
+    u_o[:, 0:256] = u[...]
+    u_o[:, 256:] = d[:, 128:256]
+    d_o[...] = d[:, 256:]
 
 
 def arrive(target, *args):
@@ -1398,15 +1343,14 @@
     again, fgain = attn_gain.reshape(1, WIDTH), ffn_gain.reshape(1, WIDTH)
     qgain, kgain = q_gain.reshape(1, HEAD), k_gain.reshape(1, HEAD)
 
-    qkv, raw, x, dy, n1h, dyh, cos, sin, slt, wq, wkv, wo, *planes = front(
+    oa, raw, x, dy, n1h, dyh, cos, sin, slt, qkv, o_t, lse, wq, wkv, wo, *planes = front(
         target, lengths, tokens, grad_out, again, qgain, kgain,
         w_query, key_matrix, value_matrix, w_out.T, w_gate, w_up, w_down.T,
     )
-    oa, o_t, lse, wg, wu, wd = attend(lengths, qkv, planes)
     dh, dhlh, gain_f, g_o, got_out, oa_m, dhl_m, *f_parts = middle(
-        slt, x, dy, dyh, fgain, oa, wo, wg, wu, wd
+        slt, x, dy, dyh, fgain, oa, wo, *planes
     )
-    f_parts = [p.reshape(4, 2, 4, 2, 64, 384) for p in f_parts]
+    f_parts = [p.reshape(4, 2, 4, 2, 64, -1) for p in f_parts]
     r_q, r_kv, r_o, r_g, r_u, r_d, got_dx, gains = back(
         lengths, qkv, g_o, o_t, lse, slt, x, dh, again, qgain, kgain, cos, sin, gain_f, n1h, dhlh,
         dhl_m, raw, wq, wkv, oa, oa_m, f_parts,

time: 320 us -> 290 us (0.906)
  Pallas kernels: 319 us -> 289 us
    pallas_call x2 -> x1, Pallas kernels: 151 us -> 133 us  [front(): pl.pallas_call(front_kernel, name='front', out_shape=[sds((NC, ROWS, 256)...]
    pallas_call x1, Pallas kernels: 121 us -> 109 us  [back(): pl.pallas_call(back_kernel, name='back', out_shape=[sds((64, 256), F32)]...]
where the time goes in v5:
time: 290 us; the launch traced here: 289 us
  Pallas kernels  289 us (100%)
    pallas_call x1, Pallas kernels, front(): pl.pallas_call(front_kernel, name='front', out_shape=[sds((NC, ROWS, 256)...  133 us
    pallas_call x1, Pallas kernels, back(): pl.pallas_call(back_kernel, name='back', out_shape=[sds((64, 256), F32)]...  109 us
    pallas_call x1, Pallas kernels, middle(): pl.pallas_call(middle_kernel, name='middle', out_shape=[sds((ROWS, WIDTH)...  43.9 us

profile of v5, /device:TPU:0, one launch (start us, length us, event | category | flops | bytes accessed | tf_op | source)
XLA Modules:
  0.0 289.5 jit_solution(6276736437309435092)
XLA Ops:
  0.6 133.1 %front.1 = (bf16[8,256,256]{2,1,0:T(8,128)(2,1)}, f32[8,256,384]{2,1,0:T(8,128)}, bf16[256,1024]{1,0:T(8,128)(2,1)}, bf16[256,1024]{1,0:T(8,128)(2,1)}, bf16[2,2...) custom-call(s32[1,256]{1,0:T(1,128)} %bitcast.35, ...), custom_call_target="tpu_custom_call" | custom-call | tf_op jit(solution)/shard_map/front/pallas_call | solution.py:714
  133.7 43.9 %middle.1 = (f32[256,1024]{1,0:T(8,128)}, bf16[2,256,512]{2,1,0:T(8,128)(2,1)}, f32[1,1024]{1,0:T(1,128)}, bf16[8,256,256]{2,1,0:T(8,128)(2,1)}, bf16[16,16,1024...) custom-call(bf16[256,128]{1,0:T(8,128)(2,1)} %get-tuple-element.62.s, ...), custom_call_target="tpu_custom_call" | custom-call | tf_op jit(solution)/shard_map/middle/pallas_call | solution.py:949
  177.6 108.6 %back.1 = (f32[64,256]{1,0:T(8,128)}, f32[64,256]{1,0:T(8,128)}, f32[64,256]{1,0:T(8,128)}, f32[64,256]{1,0:T(8,128)}, f32[64,256]{1,0:T(8,128)}, /*index=5*/f32...) custom-call(s32[1,8]{1,0:T(1,128)} %lens.3, bf16[8,256,512]{2,1,0:T(8,128)(2,1)} %get-tuple-element.72.qkv, ...), custom_call_target="tpu_custom_call" | custom-call | tf_op jit(solution)/shard_map/back/pallas_call | solution.py:1254
  286.2 3.1 %arrive.1 = (bf16[256,1024]{1,0:T(8,128)(2,1)}, bf16[256,1024]{1,0:T(8,128)(2,1)}, f32[1,1024]{1,0:T(1,128)}, f32[1,1024]{1,0:T(1,128)}, f32[1,128]{1,0:T(1,128)...) custom-call(s32[1,256]{1,0:T(1,128)} %bitcast.36, ...), custom_call_target="tpu_custom_call" | custom-call | tf_op jit(solution)/shard_map/arrive/pallas_call | solution.py:1324

commit v6 on v5

--- a/solution.py
+++ b/solution.py
@@ -517,13 +517,210 @@
     return (key <= group_slots(i)) & (key >= first)
 
 
+PAIR = 768
+STEPS = 4
+
+
+def stack_tokens(k, mine, others, scratch):
+    scratch[:, 0:ROWS] = mine[k].astype(F32).T.astype(BF)
+    scratch[:, ROWS:] = others[...].astype(F32).T.astype(BF)
+
+
+def lanes_of(j):
+    at = 384 * j
+    return (
+        (0, pl.ds(0, 256), pl.ds(at, 256)),
+        (2, pl.ds(0, 128), pl.ds(at + 256, 128)),
+        (1, pl.ds(0, 256), pl.ds(PAIR + at, 256)),
+        (2, pl.ds(128, 128), pl.ds(PAIR + at + 256, 128)),
+        (2, pl.ds(256, 384), pl.ds(2 * PAIR + at, 384)),
+    )
+
+
+def middle_steps(
+    at, slt, x, dy, dyh, fgain, oa, wo, f0, f1, f2,
+    dh_o, dhlh, gain_o, g_o, got, oa_m, dhl_m, p0, p1, p2,
+    oa_v, wo_v, w_v, acc, dn2, h_s, n2_s, dhl_s, act, n2h, n2_m, dy_m, do_s, out_s, nt_s, yt_s,
+    oa_sem, wo_sem, w_sem, g_sem, act_ssem, act_rsem, m_ssem, m_rsem, do_ssem, do_rsem, do_lsem,
+    *row_sems,
+):
+    row, col, k = lax.axis_index("row"), lax.axis_index("col"), at["k"]
+    to = device(mate(at))
+    lead, more = [], []
+    flat = [f.reshape(NC, WIDTH, w) for f, w in zip((f0, f1, f2), FFN)]
+    parts = [p.reshape(NC, 512, w) for p, w in zip((p0, p1, p2), FFN)]
+    for p in range(NC):
+        c = (p % 2) * 4 + p // 2
+        lanes = pl.ds(256 * p, 256)
+        lead.append(pltpu.make_async_copy(wo.reshape(NC, WIDTH, 256).at[p], wo_v.at[:, lanes], wo_sem.at[p]))
+        more.append(pltpu.make_async_copy(oa.at[c], oa_v.at[:, lanes], oa_sem.at[p]))
+    for cp in lead:
+        cp.start()
+    yield
+    for cp in more:
+        cp.start()
+    lead += more
+
+    def loads(t):
+        slot = t % 2
+        return [
+            pltpu.make_async_copy(
+                flat[i].at[2 * t + j, :, src],
+                w_v.at[slot, :, dst],
+                w_sem.at[slot, 5 * j + n],
+            )
+            for j in range(2)
+            for n, (i, src, dst) in enumerate(lanes_of(j))
+        ]
+
+    def weights(slot, start, stop):
+        return w_v[slot, :, start:stop]
+
+    def act_send(t):
+        rows = pl.ds(0, ROWS), pl.ds(ROWS, ROWS)
+        return remote(act.at[t, rows[0]], act.at[t, rows[1]], act_ssem.at[t], act_rsem.at[t], to)
+
+    def mate_send(i, src, dst):
+        return remote(src, dst, m_ssem.at[i], m_rsem.at[i], to)
+
+    for cp in lead:
+        cp.wait()
+
+    @pl.loop(0, 4)
+    def _(n):
+        cols = pl.ds(pl.multiple_of(256 * n, 256), 256)
+        acc[:, cols] = x[:, cols].astype(F32) + dot(oa_v[...], wo_v[cols, :], NT)
+
+    h = acc[...]
+    h_s[...] = h
+    n2 = h * mean_square_scale(h) * fgain[...]
+    n2_s[...] = n2.astype(BF)
+    a, b = halves_of(n2)
+    n2h[0] = a.astype(BF)
+    n2h[1] = b.astype(BF)
+    pairs = ((dyh.at[1 - k], dy_m), (oa, oa_m), (n2h.at[1 - k], n2_m))
+    to_mate = [mate_send(i, src, dst) for i, (src, dst) in enumerate(pairs)]
+    for cp in to_mate:
+        cp.start()
+    dn2[...] = jnp.zeros_like(dn2)
+    yield
+    for cp in loads(0):
+        cp.start()
+
+    @pl.loop(0, STEPS)
+    def _(t):
+        slot = t % 2
+
+        @pl.when(t < STEPS - 1)
+        def _():
+            for cp in loads(t + 1):
+                cp.start()
+
+        for cp in loads(t):
+            cp.wait()
+        g = dot(n2_s[...], weights(slot, 0, PAIR))
+        u = dot(n2_s[...], weights(slot, PAIR, 2 * PAIR))
+        dhid = dot(dy[...], weights(slot, 2 * PAIR, 3 * PAIR))
+        sig = jax.nn.sigmoid(g)
+        silu = g * sig
+        act[t, 0:ROWS, 2 * PAIR :] = (silu * u).astype(BF)
+        act[t, 0:ROWS, 0:PAIR] = (dhid * u * sig * (1.0 + g * (1.0 - sig))).astype(BF)
+        act[t, 0:ROWS, PAIR : 2 * PAIR] = (dhid * silu).astype(BF)
+        act_send(t).start()
+        acc[...] += dot(act[t, 0:ROWS, 2 * PAIR :], weights(slot, 2 * PAIR, 3 * PAIR), NT)
+        dn2[...] += dot(act[t, 0:ROWS, 0 : 2 * PAIR], weights(slot, 0, 2 * PAIR), NT)
+
+    h = h_s[...]
+    r2 = mean_square_scale(h)
+    hn = h * r2
+    e = dn2[...]
+    gain_o[...] = jnp.sum(e * hn, axis=0, keepdims=True)
+    e = e * fgain[...]
+    dh = dy[...].astype(F32) + r2 * (e - hn * jnp.mean(e * hn, axis=-1, keepdims=True))
+    dh_o[...] = dh
+    dhl_s[...] = dh.astype(BF)
+
+    def block_at(n):
+        return (col + 1 + n) % NC
+
+    def do_send(n):
+        c = block_at(n)
+        return remote(do_s.at[c], g_o.at[col], do_ssem.at[n], do_rsem.at[n], (row, c))
+
+    @pl.loop(0, NC)
+    def _(n):
+        c = block_at(n)
+        cols = pl.ds(pl.multiple_of(256 * place(c), 256), 256)
+        do_s[c] = dot(dhl_s[...], wo_v[:, cols]).astype(BF)
+
+        @pl.when(n < NC - 1)
+        def _():
+            do_send(n).start()
+
+    mine = pltpu.make_async_copy(do_s.at[col], g_o.at[col], do_lsem)
+    mine.start()
+    take = onehot(slt[:, :1].astype(F32).astype(I32) == iota((ROWS, ROWS), 1))
+    out_s[...] = dot(take, acc[...].astype(BF)).astype(BF).reshape(out_s.shape)
+    back = swap_over("row", out_s, got, *row_sems)
+    a, b = halves_of(dhl_s[...].astype(F32))
+    dhlh[0] = a.astype(BF)
+    dhlh[1] = b.astype(BF)
+    cp = mate_send(3, dhlh.at[1 - k], dhl_m)
+    cp.start()
+    to_mate.append(cp)
+    for cp in to_mate:
+        cp.wait()
+    stack_tokens(k, n2h, n2_m, nt_s)
+    stack_tokens(k, dyh, dy_m, yt_s)
+
+    def stores(t):
+        slot = t % 2
+        return [
+            pltpu.make_async_copy(
+                w_v.at[slot, pl.ds(0, 512), src],
+                parts[i].at[2 * t + j, :, dst],
+                g_sem.at[slot, 5 * j + n],
+            )
+            for j in range(2)
+            for n, (i, dst, src) in enumerate(lanes_of(j))
+        ]
+
+    @pl.loop(0, STEPS)
+    def _(t):
+        slot = t % 2
+
+        @pl.when(t >= 2)
+        def _():
+            for cp in stores(t - 2):
+                cp.wait()
+
+        act_send(t).wait()
+        gu = 2 * PAIR
+        g = dot(nt_s[...], act[t, :, 0:gu]).astype(BF)
+        w_v[slot, 0:512, 0:gu] = g
+        g = dot(yt_s[...], act[t, :, gu:]).astype(BF)
+        w_v[slot, 0:512, gu:] = g
+        for cp in stores(t):
+            cp.start()
+
+    for t in (STEPS - 2, STEPS - 1):
+        for cp in stores(t):
+            cp.wait()
+    for n in range(NC - 1):
+        do_send(n).wait()
+    for cp in [mine] + back:
+        cp.wait()
+
+
 def front_kernel(
-    t_row, lens, tokens, grads, again, qgain, kgain, freq, w_q, w_k, w_v, w_o, w_g, w_u, w_d,
-    oa, raw, x_o, dy_o, n1h, dyh, cos, sin, slt, qkv_o, o_t, lse, a0, a1, a2, f0, f1, f2,
-    sent, came, kv_s, u0_s, u1_s, u2_s, n1_s, src_s, raw_s, wq_v, wkv_v, qkv, o_s, s_v,
-    own_sem, w_sem, keep_sem, out_ssem, out_rsem, out_lsem, o_ssem, o_rsem, o_lsem, *sems,
+    t_row, lens, tokens, grads, again, fgain, qgain, kgain, freq, w_q, w_k, w_v, w_o, w_g, w_u, w_d,
+    oa, raw, x_o, n1h, cos, sin, slt, qkv_o, o_t, lse, a0, a1, a2,
+    dh_o, dhlh, gain_o, g_o, got, oa_m, dhl_m, p0, p1, p2, f0, f1, f2,
+    sent, came, dy_s, dyh, kv_s, u0_s, u1_s, u2_s, n1_s, src_s, raw_s, wq_v, wkv_v, qkv, o_s, s_v,
+    own_sem, w_sem, keep_sem, out_ssem, out_rsem, out_lsem, o_ssem, o_rsem, o_lsem, *rest,
 ):
     at = where_am_i()
+    sems, rest = rest[:22], rest[22:]
     row, col = lax.axis_index("row"), lax.axis_index("col")
     here = block_index({a: at[a] for a in "xyz"}, at["k"])
     near = [device(moved(at, "z", 1)), device(moved(at, "z", -1))]
@@ -543,8 +740,8 @@
     ]
     for cp in own:
         cp.start()
-    place, _ = slots_sent(t_row[...])
-    sel = place == iota((ROWS, ROWS), 0)
+    spot, _ = slots_sent(t_row[...])
+    sel = spot == iota((ROWS, ROWS), 0)
     pick = onehot(sel)
     slot = jnp.sum(jnp.where(sel, t_row[...] % ROWS, 0).astype(F32), axis=1, keepdims=True)
     message = (NR, 16, WIDTH)
@@ -595,11 +792,13 @@
     def block_at(i):
         return (col + 1 + i) % NC
 
+    slabs = [a.reshape(NC, WIDTH, 256) for a in (a0, a1)]
+
     def loads(i):
         c, slot = block_at(i), i % 2
         return [
-            pltpu.make_async_copy(a0.at[c % 4, c // 4], wq_v.at[slot], w_sem.at[0, slot]),
-            pltpu.make_async_copy(a1.at[c % 4, c // 4], wkv_v.at[slot], w_sem.at[1, slot]),
+            pltpu.make_async_copy(slabs[0].at[place(c)], wq_v.at[slot], w_sem.at[0, slot]),
+            pltpu.make_async_copy(slabs[1].at[place(c)], wkv_v.at[slot], w_sem.at[1, slot]),
         ]
 
     def sends(i):
@@ -622,8 +821,8 @@
         for cp in loads(i):
             cp.wait()
         n = n1_s[...]
-        q = dot(n, wq_v[i % 2].reshape(WIDTH, 256))
-        kv = dot(n, wkv_v[i % 2].reshape(WIDTH, 256))
+        q = dot(n, wq_v[i % 2])
+        kv = dot(n, wkv_v[i % 2])
         raw_s[c, :, 0:256] = q
         raw_s[c, :, 256:384] = kv[:, :HEAD]
         pieces = ((q[:, :HEAD], qgain), (q[:, HEAD:], qgain), (kv[:, :HEAD], kgain))
@@ -643,9 +842,9 @@
     keep = [pltpu.make_async_copy(raw_s, raw, keep_sem.at[0])]
     keep[0].start()
     cps = swap_over("row", sent.at[1, :, :, pl.ds(0, WIDTH)], came.at[1, :, :, pl.ds(0, WIDTH)], *sems[3:6])
+    planes[0].send(2, None)
     for i in range(NC - 1):
         sends(i).wait()
-    planes[0].send(2, None)
     mine.wait()
     keep.append(pltpu.make_async_copy(qkv, qkv_o, keep_sem.at[1]))
     keep[1].start()
@@ -684,64 +883,81 @@
         def _():
             o_sends(n).start()
 
-    pl.loop(0, 6)(queries)
+    ffn = middle_steps(
+        at, slt, x_o, dy_s, dyh, fgain, oa, a2, f0, f1, f2,
+        dh_o, dhlh, gain_o, g_o, got, oa_m, dhl_m, p0, p1, p2, *rest,
+    )
+    next(ffn)
+    pl.loop(0, NC)(queries)
     planes[1].pass_on(2, None)
     planes[0].pass_on(2, None)
-    pl.loop(6, NC)(queries)
     mine = pltpu.make_async_copy(o_s.at[col], oa.at[col], o_lsem)
     mine.start()
     for cp in cps:
         cp.wait()
     dy = dot(put, came[1, :, :, 0:WIDTH].reshape(ROWS, WIDTH), TN)
-    dy_o[...] = dy.astype(BF)
+    dy_s[...] = dy.astype(BF)
     a, b = halves_of(dy)
     dyh[0] = a.astype(BF)
     dyh[1] = b.astype(BF)
-    planes[0].arrived(2, None)
-    planes[1].arrived(2, None)
     for n in range(NC - 1):
         o_sends(n).wait()
     for cp in [mine] + keep:
         cp.wait()
+    next(ffn)
+    planes[0].arrived(2, None)
+    planes[1].arrived(2, None)
     for g in [lines] + planes:
         g.drain()
-
-
-def front(target, lens, tokens, grads, again, qgain, kgain, *weights):
+    next(ffn, None)
+
+
+def front(target, lens, tokens, grads, again, fgain, qgain, kgain, *weights):
     freq = ROPE_BASE ** (-(np.arange(HEAD) % (HEAD // 2)).astype(np.float32) * 2.0 / HEAD)
     freq = jnp.asarray(freq.astype(np.float32).reshape(1, HEAD))
     vm = pltpu.VMEM
+    outs = [
+        (HBM, sds((NC, ROWS, 256))),
+        (HBM, sds((NC, ROWS, 384), F32)),
+        (VMEM, sds((ROWS, WIDTH))),
+        (VMEM, sds((2, ROWS, 512))),
+        (VMEM, sds((ROWS, HEAD), F32)),
+        (VMEM, sds((ROWS, HEAD), F32)),
+        (VMEM, sds((ROWS, HEAD))),
+        (HBM, sds((NC, ROWS, 512))),
+        (VMEM, sds((NC, HEAD, QK), F32)),
+        (VMEM, sds((NC, 1, QK), F32)),
+    ]
+    outs += [(HBM, gather_shape(w)) for w in ATTN]
+    outs += [
+        (VMEM, sds((ROWS, WIDTH), F32)),
+        (VMEM, sds((2, ROWS, 512))),
+        (VMEM, sds((1, WIDTH), F32)),
+        (HBM, sds((NC, ROWS, 256))),
+        (HBM, sds((NR, 16, WIDTH))),
+        (HBM, sds((NC, ROWS, 256))),
+        (HBM, sds((ROWS, 512))),
+    ]
+    outs += [(HBM, sds((4, 2, 4, 2, 64, w))) for w in FFN]
+    outs += [(HBM, gather_shape(w)) for w in FFN]
     return pl.pallas_call(
         front_kernel,
         name="front",
-        out_shape=[
-            sds((NC, ROWS, 256)),
-            sds((NC, ROWS, 384), F32),
-            sds((ROWS, WIDTH)),
-            sds((ROWS, WIDTH)),
-            sds((2, ROWS, 512)),
-            sds((2, ROWS, 512)),
-            sds((ROWS, HEAD), F32),
-            sds((ROWS, HEAD), F32),
-            sds((ROWS, HEAD)),
-            sds((NC, ROWS, 512)),
-            sds((NC, HEAD, QK), F32),
-            sds((NC, 1, QK), F32),
-        ]
-        + [gather_shape(w) for w in ATTN + FFN],
+        out_shape=[shape for _, shape in outs],
         in_specs=[VMEM, pl.BlockSpec(memory_space=pltpu.SMEM)]
-        + [VMEM] * 6
+        + [VMEM] * 7
         + [HBM, VMEM, VMEM, HBM]
         + [VMEM] * 3,
-        out_specs=[HBM] * 2 + [VMEM] * 7 + [HBM] + [VMEM] * 2 + [HBM] * 6,
+        out_specs=[space for space, _ in outs],
         scratch_shapes=[vm((2, NR, 16, WIDTH + HEAD), BF)] * 2
+        + [vm((ROWS, WIDTH), BF), vm((2, ROWS, 512), BF)]
         + [vm((64, w), BF) for w in (256,) + FFN]
         + [
             vm((ROWS, WIDTH), BF),
             vm((NC, ROWS, 512), BF),
             vm((NC, ROWS, 384), F32),
-            vm((2, 4, 2, 2, 64, 256), BF),
-            vm((2, 4, 2, 2, 64, 256), BF),
+            vm((2, WIDTH, 256), BF),
+            vm((2, WIDTH, 256), BF),
             vm((NC, ROWS, 512), BF),
             vm((NC, ROWS, 256), BF),
             vm((SPAN, ROWS, QK), F32),
@@ -752,216 +968,8 @@
         + gather_sems(36, 16)
         + gather_sems(8, 0)
         + gather_sems(4, 4, 2)
-        + gather_sems(4, 4, 1),
-        compiler_params=params(1),
-    )(target.reshape(1, ROWS), lens, tokens, grads, again, qgain, kgain, freq, *weights)
-
-
-PAIR = 768
-STEPS = 4
-
-
-def stack_tokens(k, mine, others, scratch):
-    scratch[:, 0:ROWS] = mine[k].astype(F32).T.astype(BF)
-    scratch[:, ROWS:] = others[...].astype(F32).T.astype(BF)
-
-
-def lanes_of(j):
-    at = 384 * j
-    return (
-        (0, pl.ds(0, 256), pl.ds(at, 256)),
-        (2, pl.ds(0, 128), pl.ds(at + 256, 128)),
-        (1, pl.ds(0, 256), pl.ds(PAIR + at, 256)),
-        (2, pl.ds(128, 128), pl.ds(PAIR + at + 256, 128)),
-        (2, pl.ds(256, 384), pl.ds(2 * PAIR + at, 384)),
-    )
-
-
-def middle_kernel(
-    slt, x, dy, dyh, fgain, oa, wo, f0, f1, f2,
-    dh_o, dhlh, gain_o, g_o, got, oa_m, dhl_m, p0, p1, p2,
-    oa_v, wo_v, w_v, acc, dn2, h_s, n2_s, dhl_s, act, n2h, n2_m, dy_m, do_s, out_s, nt_s, yt_s, g_v,
-    oa_sem, wo_sem, w_sem, g_sem, act_ssem, act_rsem, m_ssem, m_rsem, do_ssem, do_rsem, do_lsem,
-    *row_sems,
-):
-    at = where_am_i()
-    row, col, k = lax.axis_index("row"), lax.axis_index("col"), at["k"]
-    to = device(mate(at))
-    peers = col_peers(at) + row_peers(at)
-    greet(peers)
-    lead = []
-    for p in range(NC):
-        c = (p % 2) * 4 + p // 2
-        lanes = pl.ds(256 * p, 256)
-        lead.append(pltpu.make_async_copy(oa.at[c], oa_v.at[:, lanes], oa_sem.at[p]))
-        lead.append(pltpu.make_async_copy(wo.at[p], wo_v.at[:, lanes], wo_sem.at[p]))
-    for cp in lead:
-        cp.start()
-
-    def loads(t):
-        slot = t % 2
-        return [
-            pltpu.make_async_copy(
-                (f0, f1, f2)[i].at[2 * t + j, :, src],
-                w_v.at[slot, :, dst],
-                w_sem.at[slot, 5 * j + n],
-            )
-            for j in range(2)
-            for n, (i, src, dst) in enumerate(lanes_of(j))
-        ]
-
-    def act_send(t):
-        rows = pl.ds(0, ROWS), pl.ds(ROWS, ROWS)
-        return remote(act.at[t, rows[0]], act.at[t, rows[1]], act_ssem.at[t], act_rsem.at[t], to)
-
-    def mate_send(i, src, dst):
-        return remote(src, dst, m_ssem.at[i], m_rsem.at[i], to)
-
-    for cp in loads(0):
-        cp.start()
-    for cp in lead:
-        cp.wait()
-
-    @pl.loop(0, 4)
-    def _(n):
-        cols = pl.ds(pl.multiple_of(256 * n, 256), 256)
-        acc[:, cols] = x[:, cols].astype(F32) + dot(oa_v[...], wo_v[cols, :], NT)
-
-    h = acc[...]
-    h_s[...] = h
-    n2 = h * mean_square_scale(h) * fgain[...]
-    n2_s[...] = n2.astype(BF)
-    a, b = halves_of(n2)
-    n2h[0] = a.astype(BF)
-    n2h[1] = b.astype(BF)
-    met(peers)
-    pairs = ((dyh.at[1 - k], dy_m), (oa, oa_m), (n2h.at[1 - k], n2_m))
-    to_mate = [mate_send(i, src, dst) for i, (src, dst) in enumerate(pairs)]
-    for cp in to_mate:
-        cp.start()
-    dn2[...] = jnp.zeros_like(dn2)
-
-    @pl.loop(0, STEPS)
-    def _(t):
-        slot = t % 2
-
-        @pl.when(t < STEPS - 1)
-        def _():
-            for cp in loads(t + 1):
-                cp.start()
-
-        for cp in loads(t):
-            cp.wait()
-        g = dot(n2_s[...], w_v[slot, :, 0:PAIR])
-        u = dot(n2_s[...], w_v[slot, :, PAIR : 2 * PAIR])
-        dhid = dot(dy[...], w_v[slot, :, 2 * PAIR :])
-        sig = jax.nn.sigmoid(g)
-        silu = g * sig
-        act[t, 0:ROWS, 2 * PAIR :] = (silu * u).astype(BF)
-        act[t, 0:ROWS, 0:PAIR] = (dhid * u * sig * (1.0 + g * (1.0 - sig))).astype(BF)
-        act[t, 0:ROWS, PAIR : 2 * PAIR] = (dhid * silu).astype(BF)
-        act_send(t).start()
-        acc[...] += dot(act[t, 0:ROWS, 2 * PAIR :], w_v[slot, :, 2 * PAIR :], NT)
-        dn2[...] += dot(act[t, 0:ROWS, 0 : 2 * PAIR], w_v[slot, :, 0 : 2 * PAIR], NT)
-
-    h = h_s[...]
-    r2 = mean_square_scale(h)
-    hn = h * r2
-    e = dn2[...]
-    gain_o[...] = jnp.sum(e * hn, axis=0, keepdims=True)
-    e = e * fgain[...]
-    dh = dy[...].astype(F32) + r2 * (e - hn * jnp.mean(e * hn, axis=-1, keepdims=True))
-    dh_o[...] = dh
-    dhl_s[...] = dh.astype(BF)
-
-    def block_at(n):
-        return (col + 1 + n) % NC
-
-    def do_send(n):
-        c = block_at(n)
-        return remote(do_s.at[c], g_o.at[col], do_ssem.at[n], do_rsem.at[n], (row, c))
-
-    @pl.loop(0, NC)
-    def _(n):
-        c = block_at(n)
-        cols = pl.ds(pl.multiple_of(256 * place(c), 256), 256)
-        do_s[c] = dot(dhl_s[...], wo_v[:, cols]).astype(BF)
-
-        @pl.when(n < NC - 1)
-        def _():
-            do_send(n).start()
-
-    mine = pltpu.make_async_copy(do_s.at[col], g_o.at[col], do_lsem)
-    mine.start()
-    take = onehot(slt[:, :1].astype(F32).astype(I32) == iota((ROWS, ROWS), 1))
-    out_s[...] = dot(take, acc[...].astype(BF)).astype(BF).reshape(out_s.shape)
-    back = swap_over("row", out_s, got, *row_sems)
-    a, b = halves_of(dhl_s[...].astype(F32))
-    dhlh[0] = a.astype(BF)
-    dhlh[1] = b.astype(BF)
-    cp = mate_send(3, dhlh.at[1 - k], dhl_m)
-    cp.start()
-    to_mate.append(cp)
-    for cp in to_mate:
-        cp.wait()
-    stack_tokens(k, n2h, n2_m, nt_s)
-    stack_tokens(k, dyh, dy_m, yt_s)
-
-    def stores(t):
-        slot = t % 2
-        return [
-            pltpu.make_async_copy(
-                g_v.at[slot, :, src],
-                (p0, p1, p2)[i].at[2 * t + j, :, dst],
-                g_sem.at[slot, 5 * j + n],
-            )
-            for j in range(2)
-            for n, (i, dst, src) in enumerate(lanes_of(j))
-        ]
-
-    @pl.loop(0, STEPS)
-    def _(t):
-        slot = t % 2
-
-        @pl.when(t >= 2)
-        def _():
-            for cp in stores(t - 2):
-                cp.wait()
-
-        act_send(t).wait()
-        gu = 2 * PAIR
-        g_v[slot, :, 0:gu] = dot(nt_s[...], act[t, :, 0:gu]).astype(BF)
-        g_v[slot, :, gu:] = dot(yt_s[...], act[t, :, gu:]).astype(BF)
-        for cp in stores(t):
-            cp.start()
-
-    for t in (STEPS - 2, STEPS - 1):
-        for cp in stores(t):
-            cp.wait()
-    for n in range(NC - 1):
-        do_send(n).wait()
-    for cp in [mine] + back:
-        cp.wait()
-
-
-def middle(slt, x, dy, dyh, fgain, oa, wo, *planes):
-    vm = pltpu.VMEM
-    return pl.pallas_call(
-        middle_kernel,
-        name="middle",
-        out_shape=[
-            sds((ROWS, WIDTH), F32),
-            sds((2, ROWS, 512)),
-            sds((1, WIDTH), F32),
-            sds((NC, ROWS, 256)),
-            sds((NR, 16, WIDTH)),
-            sds((NC, ROWS, 256)),
-            sds((ROWS, 512)),
-        ]
-        + [sds((NC, 512, w)) for w in FFN],
-        in_specs=[VMEM] * 5 + [HBM] * 5,
-        out_specs=[VMEM] * 3 + [HBM] * 7,
-        scratch_shapes=[
+        + gather_sems(4, 4, 1)
+        + [
             vm((ROWS, 2048), BF),
             vm((WIDTH, 2048), BF),
             vm((2, WIDTH, 3 * PAIR), BF),
@@ -978,7 +986,6 @@
             vm((NR, 16, WIDTH), BF),
             vm((512, 2 * ROWS), BF),
             vm((512, 2 * ROWS), BF),
-            vm((2, 512, 3 * PAIR), BF),
             DMA((NC,)),
             DMA((NC,)),
             DMA((2, 10)),
@@ -990,8 +997,8 @@
         ]
         + swap_sems("col")
         + swap_sems("row"),
-        compiler_params=params(5),
-    )(slt, x, dy, dyh, fgain, oa, *map(as_slabs, (wo,) + planes))
+        compiler_params=params(1, 63),
+    )(target.reshape(1, ROWS), lens, tokens, grads, again, fgain, qgain, kgain, freq, *weights)
 
 
 def gain_steps(at, pieces, room, total, ssem, rsem):
@@ -1110,10 +1117,15 @@
         def _():
             sends_kv(n).start()
 
-    pl.loop(0, NC)(keys)
-
-    @pl.loop(0, NC)
-    def _(n):
+        pl.when(complete(n))(lambda: queries(n))
+
+    start = block_at(0)
+
+    def complete(n):
+        j = block_at(n)
+        return (j < start) | (jnp.maximum(j - (SPAN - 1), 0) >= start)
+
+    def queries(n):
         i = block_at(n)
         done = dq[i].T
         out_s[i, :, 0:HEAD] = done[:ROWS].astype(BF)
@@ -1122,6 +1134,12 @@
         @pl.when(n < NC - 1)
         def _():
             sends_q(n).start()
+
+    pl.loop(0, NC)(keys)
+
+    @pl.loop(0, NC)
+    def _(n):
+        pl.when(jnp.logical_not(complete(n)))(lambda: queries(n))
 
     mine = []
     for lanes, sem in ((lanes_kv, kv_lsem), (lanes_q, q_lsem)):
@@ -1132,6 +1150,13 @@
 
     def comes_from(n):
         return (col - 1 - n + NC) % NC
+
+    def oa_loads(n):
+        slot = n % 2
+        return [
+            pltpu.make_async_copy(src.at[n], oa_v.at[slot, pl.ds(ROWS * i, ROWS)], oa_sem.at[i, slot])
+            for i, src in enumerate((oa, oa_m))
+        ]
 
     def loads(n):
         c, slot = comes_from(n), n % 2
@@ -1143,18 +1168,41 @@
             pltpu.make_async_copy(raw.at[c], raw_v.at[slot], w_sem.at[2, slot]),
         ]
 
+    for cp in oa_loads(0) + loads(0):
+        cp.start()
+    stack_tokens(k, dhlh, dhl_m, ht_s)
+
+    @pl.loop(0, NC)
+    def _(n):
+        @pl.when(n < NC - 1)
+        def _():
+            for cp in oa_loads(n + 1):
+                cp.start()
+
+        for cp in oa_loads(n):
+            cp.wait()
+        a2[n % 4, n // 4] = dot(ht_s[...], oa_v[n % 2]).astype(BF).reshape(4, 2, 64, 256)
+
+    swap_n1.wait()
+    stack_tokens(k, n1h, n1_m, nt_s)
+    acc[...] = jnp.zeros_like(acc)
+    gain_qk[...] = jnp.zeros_like(gain_qk)
+    next(ffn)
+
     def to_mate(n):
         c = comes_from(n)
         src, dst = draw.at[c, pl.ds(0, ROWS)], draw.at[c, pl.ds(ROWS, ROWS)]
         return remote(src, dst, m_ssem.at[n], m_rsem.at[n], to)
 
-    for cp in loads(0):
-        cp.start()
-    next(ffn)
-    acc[...] = jnp.zeros_like(acc)
-    gain_qk[...] = jnp.zeros_like(gain_qk)
-
-    def columns(n):
+    def weights_of(n):
+        c = comes_from(n)
+        to_mate(n).wait()
+        g = dot(nt_s[...], draw[c]).astype(BF)
+        a0[c % 4, c // 4] = g[:, 0:256].reshape(4, 2, 64, 256)
+        a1[c % 4, c // 4] = g[:, 256:].reshape(4, 2, 64, 256)
+
+    @pl.loop(0, NC)
+    def _(n):
         c, slot = comes_from(n), n % 2
 
         @pl.when(n < NC - 1)
@@ -1186,7 +1234,13 @@
         to_mate(n).start()
         acc[...] += dot(draw[c, 0:ROWS, :], w_v[slot], NT)
 
-    pl.loop(0, NC)(columns)
+        @pl.when(n > 0)
+        def _():
+            weights_of(n - 1)
+
+    weights_of(NC - 1)
+    attn = run_scatter(at, (a0, a1, a2), (r0, r1, r2), a_bufs, a_sems, True)
+    next(attn)
 
     xv = x[...].astype(F32)
     inverse = mean_square_scale(xv)
@@ -1200,44 +1254,7 @@
     take = onehot(slt[:, :1].astype(F32).astype(I32) == iota((ROWS, ROWS), 1))
     dx_s[...] = dot(take, dx.astype(BF)).astype(BF).reshape(dx_s.shape)
     back = swap_over("row", dx_s, got, *row_sems)
-    next(ffn)
-
-    def oa_loads(n):
-        c, slot = comes_from(n), n % 2
-        return [
-            pltpu.make_async_copy(src.at[c], oa_v.at[slot, pl.ds(ROWS * i, ROWS)], oa_sem.at[i, slot])
-            for i, src in enumerate((oa, oa_m))
-        ]
-
-    for cp in oa_loads(0):
-        cp.start()
-    stack_tokens(k, dhlh, dhl_m, ht_s)
-    swap_n1.wait()
-    stack_tokens(k, n1h, n1_m, nt_s)
-    next(gains)
-
-    @pl.loop(0, NC)
-    def _(n):
-        c, slot = comes_from(n), n % 2
-
-        @pl.when(n < NC - 1)
-        def _():
-            for cp in oa_loads(n + 1):
-                cp.start()
-
-        to_mate(n).wait()
-        g = dot(nt_s[...], draw[c]).astype(BF)
-        a0[c % 4, c // 4] = g[:, 0:256].reshape(4, 2, 64, 256)
-        a1[c % 4, c // 4] = g[:, 256:].reshape(4, 2, 64, 256)
-        for cp in oa_loads(n):
-            cp.wait()
-        a2[c % 4, c // 4] = dot(ht_s[...], oa_v[slot]).astype(BF).reshape(4, 2, 64, 256)
-
-    in_turn(
-        run_scatter(at, (a0, a1, a2), (r0, r1, r2), a_bufs, a_sems, True),
-        gains,
-        ffn,
-    )
+    in_turn(attn, gains, ffn)
     for n in range(NC - 1):
         sends_kv(n).wait_send()
         sends_q(n).wait_send()
@@ -1301,8 +1318,8 @@
     t_row, out, dx, q, kv, o, g, u, d, gains,
     out_o, dx_o, ga, gf, gq, gk, q_o, k_o, v_o, o_o, g_o, u_o, d_o,
 ):
-    _, place = slots_sent(t_row[...])
-    pick = onehot(place == iota((ROWS, ROWS), 1))
+    _, spot = slots_sent(t_row[...])
+    pick = onehot(spot == iota((ROWS, ROWS), 1))
     out_o[...] = dot(pick, out[...].reshape(ROWS, WIDTH)).astype(BF)
     dx_o[...] = dot(pick, dx[...].reshape(ROWS, WIDTH)).astype(BF)
     ga[...] = gains[:, 0:WIDTH]
@@ -1343,14 +1360,11 @@
     again, fgain = attn_gain.reshape(1, WIDTH), ffn_gain.reshape(1, WIDTH)
     qgain, kgain = q_gain.reshape(1, HEAD), k_gain.reshape(1, HEAD)
 
-    oa, raw, x, dy, n1h, dyh, cos, sin, slt, qkv, o_t, lse, wq, wkv, wo, *planes = front(
-        target, lengths, tokens, grad_out, again, qgain, kgain,
+    oa, raw, x, n1h, cos, sin, slt, qkv, o_t, lse, wq, wkv, _, dh, dhlh, gain_f, g_o, got_out, oa_m, dhl_m, *rest = front(
+        target, lengths, tokens, grad_out, again, fgain, qgain, kgain,
         w_query, key_matrix, value_matrix, w_out.T, w_gate, w_up, w_down.T,
     )
-    dh, dhlh, gain_f, g_o, got_out, oa_m, dhl_m, *f_parts = middle(
-        slt, x, dy, dyh, fgain, oa, wo, *planes
-    )
-    f_parts = [p.reshape(4, 2, 4, 2, 64, -1) for p in f_parts]
+    f_parts = rest[:3]
     r_q, r_kv, r_o, r_g, r_u, r_d, got_dx, gains = back(
         lengths, qkv, g_o, o_t, lse, slt, x, dh, again, qgain, kgain, cos, sin, gain_f, n1h, dhlh,
         dhl_m, raw, wq, wkv, oa, oa_m, f_parts,

time: 290 us -> 284 us (0.979)
  Pallas kernels: 289 us -> 283 us
    pallas_call x2 -> x1, Pallas kernels: 177 us -> 169 us  [front(): pl.pallas_call(front_kernel, name='front', out_shape=[shape for _, shape...]
where the time goes in v6:
time: 284 us
  Pallas kernels  283 us (100%)
    pallas_call x1, Pallas kernels, front(): pl.pallas_call(front_kernel, name='front', out_shape=[shape for _, shape...  169 us
    pallas_call x1, Pallas kernels, back(): pl.pallas_call(back_kernel, name='back', out_shape=[sds((64, 256), F32)]...  110 us

profile of v6, /device:TPU:0, one launch (start us, length us, event | category | flops | bytes accessed | tf_op | source)
XLA Modules:
  0.0 283.5 jit_solution(14618220914504478648)
XLA Ops:
  0.6 169.3 %front.1 = (bf16[8,256,256]{2,1,0:T(8,128)(2,1)}, f32[8,256,384]{2,1,0:T(8,128)}, bf16[256,1024]{1,0:T(8,128)(2,1)}, bf16[2,256,512]{2,1,0:T(8,128)(2,1)}, f32[2...) custom-call(s32[1,256]{1,0:T(1,128)} %bitcast.22, ...), custom_call_target="tpu_custom_call" | custom-call | tf_op jit(solution)/shard_map/front/pallas_call | solution.py:943
  170.0 110.3 %back.1 = (f32[64,256]{1,0:T(8,128)}, f32[64,256]{1,0:T(8,128)}, f32[64,256]{1,0:T(8,128)}, f32[64,256]{1,0:T(8,128)}, f32[64,256]{1,0:T(8,128)}, /*index=5*/f32...) custom-call(s32[1,8]{1,0:T(1,128)} %lens.3, bf16[8,256,512]{2,1,0:T(8,128)(2,1)} %get-tuple-element.57.qkv, ...), custom_call_target="tpu_custom_call" | custom-call | tf_op jit(solution)/shard_map/back/pallas_call | solution.py:1271
  280.3 3.0 %arrive.1 = (bf16[256,1024]{1,0:T(8,128)(2,1)}, bf16[256,1024]{1,0:T(8,128)(2,1)}, f32[1,1024]{1,0:T(1,128)}, f32[1,1024]{1,0:T(1,128)}, f32[1,128]{1,0:T(1,128)...) custom-call(s32[1,256]{1,0:T(1,128)} %bitcast.23, ...), custom_call_target="tpu_custom_call" | custom-call | tf_op jit(solution)/shard_map/arrive/pallas_call | solution.py:1341

commit v7 on v6

--- a/solution.py
+++ b/solution.py
@@ -24,6 +24,7 @@
 ORDERS = (("x", "y", "z"), ("y", "z", "x"), ("z", "x", "y"))
 ATTN = (256, 256, 256)
 FFN = (256, 256, 640)
+FFN_GRADS = (256, 256, 640)
 HBM = pl.BlockSpec(memory_space=pltpu.HBM)
 VMEM = pl.BlockSpec(memory_space=pltpu.VMEM)
 DMA = pltpu.SemaphoreType.DMA
@@ -194,12 +195,22 @@
             cp.wait_send()
 
     def lines(self):
-        for t in (0, 1):
-            self.send(t, None)
-            yield
-            self.pass_on(t, None)
-            yield
-            self.arrived(t, None)
+        self.send(0, None)
+        self.send(1, 0)
+        yield
+        self.pass_on(0, None)
+        self.send(1, 1)
+        self.send(1, 2)
+        yield
+        self.pass_on(1, 0)
+        self.arrived(0, None)
+        self.send(1, 3)
+        yield
+        for g in (1, 2, 3):
+            self.pass_on(1, g)
+        yield
+        for g in range(4):
+            self.arrived(1, g)
 
     def all(self):
         self.send(0, None)
@@ -526,15 +537,23 @@
     scratch[:, ROWS:] = others[...].astype(F32).T.astype(BF)
 
 
-def lanes_of(j):
-    at = 384 * j
-    return (
-        (0, pl.ds(0, 256), pl.ds(at, 256)),
-        (2, pl.ds(0, 128), pl.ds(at + 256, 128)),
-        (1, pl.ds(0, 256), pl.ds(PAIR + at, 256)),
-        (2, pl.ds(128, 128), pl.ds(PAIR + at + 256, 128)),
-        (2, pl.ds(256, 384), pl.ds(2 * PAIR + at, 384)),
+def pieces_of(widths):
+    w0, w1, _ = widths
+    out = (
+        (0, 0, 0, 0, w0),
+        (2, 0, 0, w0, 384 - w0),
+        (1, 0, 1, 0, w1),
+        (2, 384 - w0, 1, w1, 384 - w1),
+        (2, 768 - w0 - w1, 2, 0, 384),
     )
+    return [p for p in out if p[4] > 0]
+
+
+def lanes_of(widths, j):
+    return [
+        (s, pl.ds(a, n), pl.ds(PAIR * part + 384 * j + b, n))
+        for s, a, part, b, n in pieces_of(widths)
+    ]
 
 
 def middle_steps(
@@ -548,7 +567,7 @@
     to = device(mate(at))
     lead, more = [], []
     flat = [f.reshape(NC, WIDTH, w) for f, w in zip((f0, f1, f2), FFN)]
-    parts = [p.reshape(NC, 512, w) for p, w in zip((p0, p1, p2), FFN)]
+    parts = [p.reshape(NC, 512, w) for p, w in zip((p0, p1, p2), FFN_GRADS)]
     for p in range(NC):
         c = (p % 2) * 4 + p // 2
         lanes = pl.ds(256 * p, 256)
@@ -570,7 +589,7 @@
                 w_sem.at[slot, 5 * j + n],
             )
             for j in range(2)
-            for n, (i, src, dst) in enumerate(lanes_of(j))
+            for n, (i, src, dst) in enumerate(lanes_of(FFN, j))
         ]
 
     def weights(slot, start, stop):
@@ -598,13 +617,13 @@
     a, b = halves_of(n2)
     n2h[0] = a.astype(BF)
     n2h[1] = b.astype(BF)
+    dn2[...] = jnp.zeros_like(dn2)
+    yield
+    for cp in loads(0):
+        cp.start()
     pairs = ((dyh.at[1 - k], dy_m), (oa, oa_m), (n2h.at[1 - k], n2_m))
     to_mate = [mate_send(i, src, dst) for i, (src, dst) in enumerate(pairs)]
     for cp in to_mate:
-        cp.start()
-    dn2[...] = jnp.zeros_like(dn2)
-    yield
-    for cp in loads(0):
         cp.start()
 
     @pl.loop(0, STEPS)
@@ -682,7 +701,7 @@
                 g_sem.at[slot, 5 * j + n],
             )
             for j in range(2)
-            for n, (i, dst, src) in enumerate(lanes_of(j))
+            for n, (i, dst, src) in enumerate(lanes_of(FFN_GRADS, j))
         ]
 
     @pl.loop(0, STEPS)
@@ -728,11 +747,9 @@
     greet(peers)
     kv_s[:, :HEAD] = w_k[...]
     kv_s[:, HEAD:] = w_v[...]
-    u0_s[...] = w_g[:, 0:256]
-    u1_s[...] = w_u[:, 0:256]
-    u2_s[:, 0:128] = w_g[:, 256:]
-    u2_s[:, 128:256] = w_u[:, 256:]
-    u2_s[:, 256:] = w_d[...]
+    for i, at_lane, part, lane, n in pieces_of(FFN):
+        src = (w_g, w_u, w_d)[part]
+        (u0_s, u1_s, u2_s)[i][:, at_lane : at_lane + n] = src[:, lane : lane + n]
     pairs = zip((w_q, kv_s, w_o, u0_s, u1_s, u2_s), (a0, a1, a2, f0, f1, f2))
     own = [
         pltpu.make_async_copy(src, dst.at[here], own_sem.at[i])
@@ -744,14 +761,9 @@
     sel = spot == iota((ROWS, ROWS), 0)
     pick = onehot(sel)
     slot = jnp.sum(jnp.where(sel, t_row[...] % ROWS, 0).astype(F32), axis=1, keepdims=True)
-    message = (NR, 16, WIDTH)
-    sent[0, :, :, 0:WIDTH] = dot(pick, tokens[...]).astype(BF).reshape(message)
-    sent[0, :, :, WIDTH:] = (
-        jnp.broadcast_to(slot, (ROWS, HEAD)).astype(BF).reshape((NR, 16, HEAD))
-    )
     met(peers)
     attn = Gather(at, (a0, a1, a2), sems[6:10], own=(w_q, kv_s, w_o), split=True)
-    lines = Gather(at, (f0, f1, f2), sems[10:14], (0, 1), own=(u0_s, u1_s, u2_s))
+    lines = Gather(at, (f0, f1, f2), sems[10:14], (0, 1), own=(u0_s, u1_s, u2_s), split=True)
     planes = [
         Gather(at, (f0, f1), sems[14:18], (2,), orders=ORDERS[:2]),
         Gather(at, (f2,), sems[18:22], (2,), orders=ORDERS[2:]),
@@ -760,6 +772,11 @@
     more = lines.lines()
     next(steps)
     next(more)
+    message = (NR, 16, WIDTH)
+    sent[0, :, :, 0:WIDTH] = dot(pick, tokens[...]).astype(BF).reshape(message)
+    sent[0, :, :, WIDTH:] = (
+        jnp.broadcast_to(slot, (ROWS, HEAD)).astype(BF).reshape((NR, 16, HEAD))
+    )
     cps = swap_over("row", sent.at[0], came.at[0], *sems[0:3])
     next(steps)
     next(more)
@@ -805,7 +822,8 @@
         c = block_at(i)
         return remote(src_s.at[c], qkv.at[col], out_ssem.at[i], out_rsem.at[i], (row, c))
 
-    attn.drain()
+    for cp in attn.late:
+        cp.wait()
     planes[1].send(2, None)
     for cp in loads(0):
         cp.start()
@@ -909,6 +927,8 @@
     planes[1].arrived(2, None)
     for g in [lines] + planes:
         g.drain()
+    for cp in attn.sent:
+        cp.wait_send()
     next(ffn, None)
 
 
@@ -938,7 +958,7 @@
         (HBM, sds((NC, ROWS, 256))),
         (HBM, sds((ROWS, 512))),
     ]
-    outs += [(HBM, sds((4, 2, 4, 2, 64, w))) for w in FFN]
+    outs += [(HBM, sds((4, 2, 4, 2, 64, w))) for w in FFN_GRADS]
     outs += [(HBM, gather_shape(w)) for w in FFN]
     return pl.pallas_call(
         front_kernel,
@@ -966,7 +986,7 @@
         + swap_sems("col") * 2
         + swap_sems("row") * 2
         + gather_sems(36, 16)
-        + gather_sems(8, 0)
+        + gather_sems(20, 0)
         + gather_sems(4, 4, 2)
         + gather_sems(4, 4, 1)
         + [
@@ -1272,7 +1292,7 @@
         back_kernel,
         name="back",
         out_shape=[sds((64, 256), F32)] * 3
-        + [sds((64, w), F32) for w in FFN]
+        + [sds((64, w), F32) for w in FFN_GRADS]
         + [sds((NR, 16, WIDTH)), sds((1, total), F32)],
         in_specs=[pl.BlockSpec(memory_space=pltpu.SMEM)] + [VMEM] * 15 + [HBM] * 9,
         out_specs=[VMEM] * 6 + [HBM, VMEM],
@@ -1306,7 +1326,7 @@
         + scatter_sems()
         + scatter_sems()
         + scatter_buffers(ATTN)
-        + scatter_buffers(FFN),
+        + scatter_buffers(FFN_GRADS),
         compiler_params=params(6, 63),
     )(
         lens, qkv, d_o, lse, slt, x, dh, again, qgain, kgain, cos, sin, gain_f, n1h, dhlh,
@@ -1330,11 +1350,8 @@
     k_o[...] = kv[:, :HEAD]
     v_o[...] = kv[:, HEAD:]
     o_o[...] = o[...]
-    g_o[:, 0:256] = g[...]
-    g_o[:, 256:] = d[:, 0:128]
-    u_o[:, 0:256] = u[...]
-    u_o[:, 256:] = d[:, 128:256]
-    d_o[...] = d[:, 256:]
+    for i, at_lane, part, lane, n in pieces_of(FFN_GRADS):
+        (g_o, u_o, d_o)[part][:, lane : lane + n] = (g, u, d)[i][:, at_lane : at_lane + n]
 
 
 def arrive(target, *args):

time: 284 us -> 280 us (0.986)
  Pallas kernels: 283 us -> 279 us
    pallas_call x1, Pallas kernels: 169 us -> 166 us  [front(): pl.pallas_call(front_kernel, name='front', out_shape=[shape for _, shape...]
where the time goes in v7:
time: 280 us; the launch traced here: 279 us
  Pallas kernels  279 us (100%)
    pallas_call x1, Pallas kernels, front(): pl.pallas_call(front_kernel, name='front', out_shape=[shape for _, shape...  166 us
    pallas_call x1, Pallas kernels, back(): pl.pallas_call(back_kernel, name='back', out_shape=[sds((64, 256), F32)]...  109 us

profile of v7, /device:TPU:0, one launch (start us, length us, event | category | flops | bytes accessed | tf_op | source)
XLA Modules:
  0.0 279.4 jit_solution(18409158658537073103)
XLA Ops:
  0.6 166.1 %front.1 = (bf16[8,256,256]{2,1,0:T(8,128)(2,1)}, f32[8,256,384]{2,1,0:T(8,128)}, bf16[256,1024]{1,0:T(8,128)(2,1)}, bf16[2,256,512]{2,1,0:T(8,128)(2,1)}, f32[2...) custom-call(s32[1,256]{1,0:T(1,128)} %bitcast.22, ...), custom_call_target="tpu_custom_call" | custom-call | tf_op jit(solution)/shard_map/front/pallas_call | solution.py:963
  166.7 109.5 %back.1 = (f32[64,256]{1,0:T(8,128)}, f32[64,256]{1,0:T(8,128)}, f32[64,256]{1,0:T(8,128)}, f32[64,256]{1,0:T(8,128)}, f32[64,256]{1,0:T(8,128)}, /*index=5*/f32...) custom-call(s32[1,8]{1,0:T(1,128)} %lens.3, bf16[8,256,512]{2,1,0:T(8,128)(2,1)} %get-tuple-element.57.qkv, ...), custom_call_target="tpu_custom_call" | custom-call | tf_op jit(solution)/shard_map/back/pallas_call | solution.py:1291
  276.2 3.0 %arrive.1 = (bf16[256,1024]{1,0:T(8,128)(2,1)}, bf16[256,1024]{1,0:T(8,128)(2,1)}, f32[1,1024]{1,0:T(1,128)}, f32[1,1024]{1,0:T(1,128)}, f32[1,128]{1,0:T(1,128)...) custom-call(s32[1,256]{1,0:T(1,128)} %bitcast.23, ...), custom_call_target="tpu_custom_call" | custom-call | tf_op jit(solution)/shard_map/arrive/pallas_call | solution.py:1358

commit v8 on v7

--- a/solution.py
+++ b/solution.py
@@ -620,7 +620,7 @@
     dn2[...] = jnp.zeros_like(dn2)
     yield
     for cp in loads(0):
-        cp.start()
+        cp.start(priority=1)
     pairs = ((dyh.at[1 - k], dy_m), (oa, oa_m), (n2h.at[1 - k], n2_m))
     to_mate = [mate_send(i, src, dst) for i, (src, dst) in enumerate(pairs)]
     for cp in to_mate:
@@ -633,7 +633,7 @@
         @pl.when(t < STEPS - 1)
         def _():
             for cp in loads(t + 1):
-                cp.start()
+                cp.start(priority=1)
 
         for cp in loads(t):
             cp.wait()
@@ -826,7 +826,7 @@
         cp.wait()
     planes[1].send(2, None)
     for cp in loads(0):
-        cp.start()
+        cp.start(priority=1)
 
     def columns(i):
         c = block_at(i)
@@ -834,7 +834,7 @@
         @pl.when(i < NC - 1)
         def _():
             for cp in loads(i + 1):
-                cp.start()
+                cp.start(priority=1)
 
         for cp in loads(i):
             cp.wait()
@@ -1189,7 +1189,7 @@
         ]
 
     for cp in oa_loads(0) + loads(0):
-        cp.start()
+        cp.start(priority=1)
     stack_tokens(k, dhlh, dhl_m, ht_s)
 
     @pl.loop(0, NC)
@@ -1197,7 +1197,7 @@
         @pl.when(n < NC - 1)
         def _():
             for cp in oa_loads(n + 1):
-                cp.start()
+                cp.start(priority=1)
 
         for cp in oa_loads(n):
             cp.wait()
@@ -1228,7 +1228,7 @@
         @pl.when(n < NC - 1)
         def _():
             for cp in loads(n + 1):
-                cp.start()
+                cp.start(priority=1)
             sends_kv(n).wait_recv()
             sends_q(n).wait_recv()
 

time: 280 us -> 280 us (level)
  no operation moved by 1% of the time
where the time goes in v8:
time: 280 us; the launch traced here: 279 us
  Pallas kernels  279 us (100%)
    pallas_call x1, Pallas kernels, front(): pl.pallas_call(front_kernel, name='front', out_shape=[shape for _, shape...  166 us
    pallas_call x1, Pallas kernels, back(): pl.pallas_call(back_kernel, name='back', out_shape=[sds((64, 256), F32)]...  109 us

profile of v8, /device:TPU:0, one launch (start us, length us, event | category | flops | bytes accessed | tf_op | source)
XLA Modules:
  0.0 279.4 jit_solution(16922299420537422121)
XLA Ops:
  0.6 166.1 %front.1 = (bf16[8,256,256]{2,1,0:T(8,128)(2,1)}, f32[8,256,384]{2,1,0:T(8,128)}, bf16[256,1024]{1,0:T(8,128)(2,1)}, bf16[2,256,512]{2,1,0:T(8,128)(2,1)}, f32[2...) custom-call(s32[1,256]{1,0:T(1,128)} %bitcast.22, ...), custom_call_target="tpu_custom_call" | custom-call | tf_op jit(solution)/shard_map/front/pallas_call | solution.py:963
  166.7 109.5 %back.1 = (f32[64,256]{1,0:T(8,128)}, f32[64,256]{1,0:T(8,128)}, f32[64,256]{1,0:T(8,128)}, f32[64,256]{1,0:T(8,128)}, f32[64,256]{1,0:T(8,128)}, /*index=5*/f32...) custom-call(s32[1,8]{1,0:T(1,128)} %lens.3, bf16[8,256,512]{2,1,0:T(8,128)(2,1)} %get-tuple-element.57.qkv, ...), custom_call_target="tpu_custom_call" | custom-call | tf_op jit(solution)/shard_map/back/pallas_call | solution.py:1291
  276.2 3.0 %arrive.1 = (bf16[256,1024]{1,0:T(8,128)(2,1)}, bf16[256,1024]{1,0:T(8,128)(2,1)}, f32[1,1024]{1,0:T(1,128)}, f32[1,1024]{1,0:T(1,128)}, f32[1,128]{1,0:T(1,128)...) custom-call(s32[1,256]{1,0:T(1,128)} %bitcast.23, ...), custom_call_target="tpu_custom_call" | custom-call | tf_op jit(solution)/shard_map/arrive/pallas_call | solution.py:1358
